TPU v7x, 32 devices: a whole 2x2x4 slice. The times are simulated.
32 devices in a mesh: groups: 2 (over x), space: 16 (over z, y, core).
Axes of the slice: x: 2, y: 2, z: 4, core: 2. Of those that a mesh axis runs over, the one named last changes fastest.
Arguments:
- atom_features: bfloat16 [288, 32, 256], P(('groups', 'space')), parts along dimension 0, may hold values from -6 to 6
- offsets: bfloat16 [288, 3, 32], P(('groups', 'space')), parts along dimension 0, may hold values from 0 to 1
- counts: int32 [288], P(('groups', 'space')), parts along dimension 0, may hold values from 8 to 32, as said below
- radial_weight: bfloat16 [4, 256, 256], replicated, may hold values from -0.375 to 0.375
- charge_weight: bfloat16 [256, 256], replicated, may hold values from -0.375 to 0.375
- wave_filter: float32 [4, 256], replicated, may hold values from -5 to 5
- wavevectors: int32 [3, 1024], replicated, may hold values from -4 to 25, as said below
Outputs:
- updated: bfloat16 [288, 32, 256], P(('groups', 'space')), parts along dimension 0
There are 2 independent parts, one for each index of `groups`. A program takes and returns all parts, laid end to end along the dimension named above; an argument that names none is the same for every part. Nothing has to cross between parts.
Inputs may be any that keep to these rules, and one draw needn't show every extreme that they name: Cell c holds its atoms in its first counts[c] slots; in every draw some cell is full. `wavevectors`: the 1024 columns are distinct index triples from one half of the lattice: no column is zero or the negative of another; the first two indices lie in -4 to 4 and the third in 0 to 25, and where the third is 0 the first is above 0, or the first is 0 and the second above 0.
All inputs are finite; a program needn't handle non-finite values.
Results may differ from a plain program's by a relative error of at most 0.005.
Values may be sent and summed in bfloat16 or wider, within the bound.
No kernel may reach another device: no remote copies, remote signals or barrier semaphores. Data moves between devices by JAX's collectives and lax.ppermute only.
A program may use at most 64 MiB of HBM per device.

v0:
```python
import math

import jax
import jax.numpy as jnp
from jax import lax
from jax.sharding import PartitionSpec as P

GRID = 3


CUTOFF = 1.0
block_rows = 512


def with_halo(value, sides, width):
    for axis, dim in sides:
        size, length = (lax.axis_size(axis), value.shape[dim])
        up = [(i, (i + 1) % size) for i in range(size)]
        down = [(j, i) for i, j in up]
        last = lax.slice_in_dim(value, length - width, length, axis=dim)
        leading = lax.slice_in_dim(value, 0, width, axis=dim)
        before = lax.ppermute(last, axis, up)
        after = lax.ppermute(leading, axis, down)
        value = jnp.concatenate([before, value, after], axis=dim)
    return value


def cell_geometry(near_count, cell_slots):
    columns = jnp.arange(near_count * cell_slots, dtype=jnp.int32)
    return (columns // cell_slots, columns % cell_slots)


def pair_radius(own_coords, near_coords, near_cell, near_slot, cell_index, layer_cells):
    own_x = cell_index // GRID
    own_y = cell_index % GRID
    layer_of = near_cell // layer_cells
    within = near_cell % layer_cells
    shift_x = ((within // GRID - own_x + 1) % GRID - 1).astype(jnp.float32)
    shift_y = ((within % GRID - own_y + 1) % GRID - 1).astype(jnp.float32)
    shift_z = (layer_of - 1).astype(jnp.float32)
    own_pos = own_coords.astype(jnp.float32)
    near_pos = near_coords.astype(jnp.float32)
    delta_x = (shift_x + near_pos[0])[None, :] - own_pos[0][:, None]
    delta_y = (shift_y + near_pos[1])[None, :] - own_pos[1][:, None]
    delta_z = (shift_z + near_pos[2])[None, :] - own_pos[2][:, None]
    radius = jnp.sqrt(delta_x * delta_x + delta_y * delta_y + delta_z * delta_z)
    smooth = jnp.where(radius < CUTOFF, 0.5 * (jnp.cos(math.pi * radius / CUTOFF) + 1.0), 0.0)
    slot_ids = jnp.arange(own_pos.shape[1], dtype=jnp.int32)
    itself = (near_cell == layer_cells + cell_index)[None, :] & (
        near_slot[None, :] == slot_ids[:, None]
    )
    return (radius, smooth, itself)


def wave_numbers(wave_rows, layers_total):
    two_pi = 2.0 * math.pi
    wave_float = wave_rows.astype(jnp.float32)
    along_x = two_pi * wave_float[0] / GRID
    along_y = two_pi * wave_float[1] / GRID
    along_z = two_pi * wave_float[2] / layers_total
    return (along_x, along_y, along_z)


def phase_table(positions, wave_rows, layers_total):
    along_x, along_y, along_z = wave_numbers(wave_rows, layers_total)
    return (
        positions[0][:, None] * along_x[None, :]
        + positions[1][:, None] * along_y[None, :]
        + positions[2][:, None] * along_z[None, :]
    )


def structure_terms(positions, charges, wave_rows, layers_total):
    row_count = wave_rows.shape[1]
    feature_width = charges.shape[1]
    pieces = jnp.transpose(wave_rows.reshape(3, row_count // block_rows, block_rows), (1, 0, 2))

    def structure_one_block(wave_block):
        phases = phase_table(positions, wave_block, layers_total)
        cosine = jnp.cos(phases).astype(jnp.bfloat16)
        sine_part = jnp.sin(phases).astype(jnp.bfloat16)
        real_part = lax.dot_general(
            cosine, charges, (((0,), (0,)), ((), ())), preferred_element_type=jnp.float32
        )
        imag_part = lax.dot_general(
            sine_part, charges, (((0,), (0,)), ((), ())), preferred_element_type=jnp.float32
        )
        return jnp.concatenate([real_part, imag_part], axis=1)

    return lax.map(structure_one_block, pieces).reshape(row_count, 2 * feature_width)


def filter_rows(structure, wave_rows, layers_total, wave_filter):
    along_x, along_y, along_z = wave_numbers(wave_rows, layers_total)
    magnitude = jnp.sqrt(along_x * along_x + along_y * along_y + along_z * along_z)
    centres = 3.0 * jnp.arange(wave_filter.shape[0], dtype=jnp.float32)
    offset_k = (magnitude[:, None] - centres[None, :]) / 3.0
    basis_rows = jnp.exp(-(offset_k * offset_k))
    gain_rows = jnp.dot(
        basis_rows, wave_filter, precision=lax.Precision.HIGHEST, preferred_element_type=jnp.float32
    )
    return (structure * jnp.concatenate([gain_rows, gain_rows], axis=1)).astype(jnp.bfloat16)


def add_inverse(running, filtered, wave_rows, positions, layers_total):
    row_count = filtered.shape[0]
    feature_width = filtered.shape[1] // 2
    block_count = row_count // block_rows
    factor_blocks = filtered.reshape(block_count, block_rows, 2 * feature_width)
    wave_blocks = jnp.transpose(wave_rows.reshape(3, block_count, block_rows), (1, 0, 2))

    def add_one_block(summed, block_item):
        factors, wave_block = block_item
        phases = phase_table(positions, wave_block, layers_total)
        cosine = jnp.cos(phases).astype(jnp.bfloat16)
        sine_part = jnp.sin(phases).astype(jnp.bfloat16)
        summed = summed + jnp.dot(
            cosine, factors[:, :feature_width], preferred_element_type=jnp.float32
        )
        summed = summed + jnp.dot(
            sine_part, factors[:, feature_width:], preferred_element_type=jnp.float32
        )
        return (summed, None)

    outcome = lax.scan(add_one_block, running, (factor_blocks, wave_blocks))
    return outcome[0]


def local(atom_features, offsets, counts, radial_weight, charge_weight, wave_filter, wavevectors):
    layer_cells, cell_slots, feature_width = atom_features.shape
    basis_count = radial_weight.shape[0]
    wave_count = wavevectors.shape[1]
    layers_total = lax.axis_size("space")
    layer_index = lax.axis_index("space")
    slot_ids = jnp.arange(cell_slots, dtype=jnp.int32)
    live_mask = (slot_ids[None, :] < counts[:, None]).astype(jnp.float32)
    masked = (atom_features.astype(jnp.float32) * live_mask[:, :, None]).astype(jnp.bfloat16)
    near_features, near_offsets = (
        with_halo(masked, (("space", 0),), layer_cells),
        with_halo(offsets, (("space", 0),), layer_cells),
    )
    near_count = 3 * layer_cells
    near_flat = near_features.reshape(near_count * cell_slots, feature_width)
    near_coords = jnp.transpose(near_offsets, (1, 0, 2)).reshape(3, near_count * cell_slots)
    near_cell, near_slot = cell_geometry(near_count, cell_slots)
    cell_ids = jnp.arange(layer_cells, dtype=jnp.int32)
    values = jnp.stack(
        [
            jnp.dot(
                near_flat, radial_weight[basis_index], preferred_element_type=jnp.float32
            ).astype(jnp.bfloat16)
            for basis_index in range(basis_count)
        ]
    )

    def cell_short(own_coords, cell_index):
        radius, smooth, itself = pair_radius(
            own_coords, near_coords, near_cell, near_slot, cell_index, layer_cells
        )
        running = jnp.zeros((cell_slots, feature_width), jnp.float32)
        for basis_index in range(basis_count):
            centre = (basis_index + 0.5) * CUTOFF / basis_count
            scaled = (radius - centre) * (basis_count / CUTOFF)
            pair_weights = jnp.where(itself, 0.0, jnp.exp(-(scaled * scaled)) * smooth).astype(
                jnp.bfloat16
            )
            running = running + jnp.dot(
                pair_weights, values[basis_index], preferred_element_type=jnp.float32
            )
        return running

    short_sum = jax.vmap(cell_short)(offsets, cell_ids)
    base_x = (cell_ids // GRID).astype(jnp.float32)
    base_y = (cell_ids % GRID).astype(jnp.float32)
    base_z = layer_index.astype(jnp.float32)
    coords = offsets.astype(jnp.float32)
    positions = jnp.stack(
        [
            (base_x[:, None] + coords[:, 0, :]).reshape(-1),
            (base_y[:, None] + coords[:, 1, :]).reshape(-1),
            (base_z + coords[:, 2, :]).reshape(-1),
        ]
    )
    charges = jnp.dot(
        masked.reshape(layer_cells * cell_slots, feature_width),
        charge_weight,
        preferred_element_type=jnp.float32,
    ).astype(jnp.bfloat16)
    empty_sum = jnp.zeros((layer_cells * cell_slots, feature_width), jnp.float32)
    share_rows = wave_count // layers_total
    wave_rows = wavevectors
    own_share = lax.psum_scatter(
        structure_terms(positions, charges, wave_rows, layers_total),
        "space",
        scatter_dimension=0,
        tiled=True,
    )
    own_waves = lax.dynamic_slice_in_dim(wavevectors, layer_index * share_rows, share_rows, 1)
    filtered = filter_rows(own_share, own_waves, layers_total, wave_filter)
    wave_rows = wavevectors
    reciprocal = add_inverse(
        empty_sum,
        lax.all_gather(filtered, "space", axis=0, tiled=True),
        wave_rows,
        positions,
        layers_total,
    )
    short_scaled = short_sum * (1.0 / math.sqrt(cell_slots))
    recip_scaled = reciprocal * (
        1.0 / math.sqrt(layer_cells * layers_total * cell_slots * wave_count)
    )
    combined = (
        atom_features.astype(jnp.float32)
        + short_scaled
        + recip_scaled.reshape(layer_cells, cell_slots, feature_width)
    )
    return (live_mask[:, :, None] * combined).astype(jnp.bfloat16)


def solution(mesh):
    in_specs = (
        P(("groups", "space"), None, None),
        P(("groups", "space"), None, None),
        P(("groups", "space")),
        P(),
        P(),
        P(),
        P(),
    )
    out_specs = P(("groups", "space"), None, None)
    return jax.shard_map(local, mesh=mesh, in_specs=in_specs, out_specs=out_specs, check_vma=False)
```

profile of v0, /device:TPU:0, one launch (start us, length us, event | category | flops | bytes accessed | tf_op | source)
XLA Modules:
  0.0 150.5 jit_solution(8142153261382945371)
XLA Ops:
  8.3 1.0 fusion.102
  9.6 13.8 %while.29 = (s32[]{:T(128)}, f32[2,512,512]{2,1,0:T(8,128)}, f32[9,32]{1,0:T(8,128)}, s32[2,3,512]{2,1,0:T(4,128)}, f32[9,32]{1,0:T(8,128)}, /*index=5*/f32[9,32...) while((s32[]{:T(128)}, f32[2,512,512]{2,1,0:T(8,128)}, ...), condition=%wide.wide.region_1.2_spmd, body=%wide.wide.region_0.1_spmd.sunk | while | flops 153029632 | bytes 7678845 | solution.py:90
  10.3 2.3 %fusion.204 = f32[512,256]{0,1:T(8,128)S(1)} fusion(bf16[288,256]{1,0:T(8,128)(2,1)S(1)} %get-tuple-element.522, f32[512]{0:T(512)S(1)} %bitcast.123, f32[288]{0:T(512)S(1)} %get-tuple-element.523, f32[512]{0:T(512)S(1)} %bitcast.125, f32[288]{0:T(512)S(1)} %get-tuple-element.524, f32[512]{0:T(512)S(1)} %bitcast.121, f32[288]{0:T(512)S(1)} %get-tuple-element.525), kind=kOutput, calls=%fused_computation.5.clone.clone.1 | convolution fusion | flops 76382208 | bytes 681344 | tf_op jit(solution)/shard_map/while/body/eval_jaxpr/dot_general | solution.py:85
  12.7 2.3 %fusion.205 = f32[512,256]{0,1:T(8,128)S(1)} fusion(bf16[288,256]{1,0:T(8,128)(2,1)S(1)} %get-tuple-element.522, f32[512]{0:T(512)S(1)} %bitcast.124, f32[288]{0:T(512)S(1)} %get-tuple-element.523, f32[512]{0:T(512)S(1)} %bitcast.126, f32[288]{0:T(512)S(1)} %get-tuple-element.524, f32[512]{0:T(512)S(1)} %bitcast.122, f32[288]{0:T(512)S(1)} %get-tuple-element.525), kind=kOutput, calls=%fused_computation.4.clone.clone.1 | convolution fusion | flops 76382208 | bytes 681344 | tf_op jit(solution)/shard_map/while/body/eval_jaxpr/dot_general | solution.py:82
  15.4 1.1 constant_dynamic-update-slice_fusion.3
  17.2 2.4 %fusion.204 = f32[512,256]{0,1:T(8,128)S(1)} fusion(bf16[288,256]{1,0:T(8,128)(2,1)S(1)} %get-tuple-element.522, f32[512]{0:T(512)S(1)} %bitcast.123, f32[288]{0:T(512)S(1)} %get-tuple-element.523, f32[512]{0:T(512)S(1)} %bitcast.125, f32[288]{0:T(512)S(1)} %get-tuple-element.524, f32[512]{0:T(512)S(1)} %bitcast.121, f32[288]{0:T(512)S(1)} %get-tuple-element.525), kind=kOutput, calls=%fused_computation.5.clone.clone.1 | convolution fusion | flops 76382208 | bytes 681344 | tf_op jit(solution)/shard_map/while/body/eval_jaxpr/dot_general | solution.py:85
  19.6 2.3 %fusion.205 = f32[512,256]{0,1:T(8,128)S(1)} fusion(bf16[288,256]{1,0:T(8,128)(2,1)S(1)} %get-tuple-element.522, f32[512]{0:T(512)S(1)} %bitcast.124, f32[288]{0:T(512)S(1)} %get-tuple-element.523, f32[512]{0:T(512)S(1)} %bitcast.126, f32[288]{0:T(512)S(1)} %get-tuple-element.524, f32[512]{0:T(512)S(1)} %bitcast.122, f32[288]{0:T(512)S(1)} %get-tuple-element.525), kind=kOutput, calls=%fused_computation.4.clone.clone.1 | convolution fusion | flops 76382208 | bytes 681344 | tf_op jit(solution)/shard_map/while/body/eval_jaxpr/dot_general | solution.py:82
  22.3 1.1 constant_dynamic-update-slice_fusion.3
  23.5 5.5 %collective-permute-start.3 = (bf16[9,32,256]{2,1,0:T(8,128)(2,1)S(1)}, bf16[9,32,256]{2,1,0:T(8,128)(2,1)S(1)}, u32[]{:S(2)}, u32[]{:S(2)}) collective-permute-start(bf16[9,32,256]{2,1,0:T(8,128)(2,1)S(1)} %fusion.102), channel_id=1, source_target_pairs={{1,0},{2,1},{3,2},{4,3},{5,4},{6,5},{7,6},{8,7},{9,8},{10,9},{11,1... | collective-permute-start | bytes 442376 | tf_op jit(solution)/shard_map/ppermute | solution.py:23
  29.0 4.4 %collective-permute-start.1 = (bf16[9,3,32]{2,1,0:T(4,128)(2,1)S(1)}, bf16[9,3,32]{2,1,0:T(4,128)(2,1)S(1)}, u32[]{:S(2)}, u32[]{:S(2)}) collective-permute-start(bf16[9,3,32]{2,1,0:T(4,128)(2,1)S(1)} %copy-done.9), channel_id=1, source_target_pairs={{1,0},{2,1},{3,2},{4,3},{5,4},{6,5},{7,6},{8,7},{9,8},{10,9},{11,1... | collective-permute-start | bytes 5192 | tf_op jit(solution)/shard_map/ppermute | solution.py:23
  34.1 53.8 %reduce-scatter.2.cloned.1.call-done = f32[64,512]{1,0:T(8,128)} async-done(((f32[1024,512]{1,0:T(8,128)}), f32[64,512]{1,0:T(8,128)}) %reduce-scatter.2.cloned.1.call-update) | async-done | bytes 131088 | tf_op jit(solution)/shard_map/reduce_scatter | solution.py:192
  87.8 1.5 %fusion.103 = bf16[64,512]{1,0:T(8,128)(2,1)} fusion(f32[64,512]{1,0:T(8,128)} %reduce-scatter.2.cloned.1.call-done, f32[64,256]{1,0:T(8,128)S(1)} %fusion.145), kind=kLoop, calls=%fused_computation.136 | loop fusion | flops 98304 | bytes 262144 | tf_op jit(solution)/shard_map/convert_element_type | solution.py:102
  90.3 4.6 %fusion.41 = f32[9,32,256]{2,1,0:T(8,128)S(1)} fusion(bf16[864,256]{1,0:T(8,128)(2,1)S(1)} %bitcast.108, f32[9,32]{1,0:T(8,128)S(1)} %get-tuple-element.293, f32[864]{0:T(1024)S(1)} %fusion.141, f32[9,32]{1,0:T(8,128)S(1)} %get-tuple-element.294, f32[9,864]{1,0:T(8,128)S(1)} %get-tuple-element.301, f32[9,32]{1,0:T(8,128)S(1)} %get-tuple-element.292, ...), kind=kOutput, calls=%fused_computation.74 | convolution fusion | flops 246094848 | bytes 1054720 | tf_op jit(solution)/shard_map/vmap()/dot_general | solution.py:167
  94.9 4.6 %convolution_add_fusion.4 = f32[9,32,256]{2,1,0:T(8,128)S(1)} fusion(f32[9,32,256]{2,1,0:T(8,128)S(1)} %fusion.41, bf16[864,256]{1,0:T(8,128)(2,1)S(1)} %bitcast.109, f32[9,32]{1,0:T(8,128)S(1)} %get-tuple-element.293, f32[864]{0:T(1024)S(1)} %fusion.141, f32[9,32]{1,0:T(8,128)S(1)} %get-tuple-element.294, f32[9,864]{1,0:T(8,128)S(1)} %get-tuple-element.301, ...), kind=kOutput, calls=%fused_computation.61 | convolution fusion | flops 246168576 | bytes 1349632 | tf_op jit(solution)/shard_map/vmap()/dot_general | solution.py:167
  99.5 4.8 %convolution_add_fusion.3 = f32[9,32,256]{2,1,0:T(8,128)S(1)} fusion(f32[9,32,256]{2,1,0:T(8,128)S(1)} %convolution_add_fusion.4, bf16[864,256]{1,0:T(8,128)(2,1)S(1)} %bitcast.110, f32[9,32]{1,0:T(8,128)S(1)} %get-tuple-element.293, f32[864]{0:T(1024)S(1)} %fusion.141, f32[9,32]{1,0:T(8,128)S(1)} %get-tuple-element.294, ...), kind=kOutput, calls=%fused_computation.60 | convolution fusion | flops 246168576 | bytes 1349632 | tf_op jit(solution)/shard_map/vmap()/dot_general | solution.py:167
  104.3 22.9 %all-gather.2.cloned.1.call-done = bf16[1024,512]{1,0:T(8,128)(2,1)} async-done(((bf16[64,512]{1,0:T(8,128)(2,1)}), bf16[1024,512]{1,0:T(8,128)(2,1)}) %all-gather.2.cloned.1.call-update) | async-done | bytes 1048592 | tf_op jit(solution)/shard_map/all_gather | solution.py:203
  127.2 11.1 %while.30 = (s32[]{:T(128)}, f32[288,256]{1,0:T(8,128)S(1)}, f32[9,32]{1,0:T(8,128)}, s32[2,3,512]{2,1,0:T(4,128)S(1)}, f32[9,32]{1,0:T(8,128)}, /*index=5*/f32[...) while((s32[]{:T(128)}, f32[288,256]{1,0:T(8,128)S(1)}, ...), condition=%wide.wide.region_4.5_spmd.clone, body=%wide.wide.region_3.4_spmd.clone.sunk | while | flops 152988672 | bytes 2801807 | solution.py:125
  127.2 1.1 dynamic-slice_bitcast_fusion.3
  128.4 2.2 %convolution_add_fusion.9 = f32[288,256]{1,0:T(8,128)S(1)} fusion(f32[288,256]{1,0:T(8,128)S(1)} %get-tuple-element.540, f32[512]{0:T(512)S(1)} %bitcast.117, f32[288]{0:T(512)S(1)} %get-tuple-element.558, f32[512]{0:T(512)S(1)} %bitcast.119, f32[288]{0:T(512)S(1)} %get-tuple-element.559, f32[512]{0:T(512)S(1)} %bitcast.115, ...), kind=kOutput, calls=%fused_computation.24.clone.clone.1 | convolution fusion | flops 76529664 | bytes 864257 | tf_op jit(solution)/shard_map/while/body/eval_jaxpr/dot_general | solution.py:117
  130.6 2.2 %convolution_add_fusion.10 = f32[288,256]{1,0:T(8,128)S(1)} fusion(f32[288,256]{1,0:T(8,128)S(1)} %convolution_add_fusion.9, f32[512]{0:T(512)S(1)} %bitcast.118, f32[288]{0:T(512)S(1)} %get-tuple-element.558, f32[512]{0:T(512)S(1)} %bitcast.120, f32[288]{0:T(512)S(1)} %get-tuple-element.559, f32[512]{0:T(512)S(1)} %bitcast.116, ...), kind=kOutput, calls=%fused_computation.23.clone.clone.1 | convolution fusion | flops 76455936 | bytes 864256 | tf_op jit(solution)/shard_map/while/body/eval_jaxpr/dot_general | solution.py:120
  132.8 1.1 dynamic-slice_bitcast_fusion.3
  133.9 2.2 %convolution_add_fusion.9 = f32[288,256]{1,0:T(8,128)S(1)} fusion(f32[288,256]{1,0:T(8,128)S(1)} %get-tuple-element.540, f32[512]{0:T(512)S(1)} %bitcast.117, f32[288]{0:T(512)S(1)} %get-tuple-element.558, f32[512]{0:T(512)S(1)} %bitcast.119, f32[288]{0:T(512)S(1)} %get-tuple-element.559, f32[512]{0:T(512)S(1)} %bitcast.115, ...), kind=kOutput, calls=%fused_computation.24.clone.clone.1 | convolution fusion | flops 76529664 | bytes 864257 | tf_op jit(solution)/shard_map/while/body/eval_jaxpr/dot_general | solution.py:117
  136.1 2.2 %convolution_add_fusion.10 = f32[288,256]{1,0:T(8,128)S(1)} fusion(f32[288,256]{1,0:T(8,128)S(1)} %convolution_add_fusion.9, f32[512]{0:T(512)S(1)} %bitcast.118, f32[288]{0:T(512)S(1)} %get-tuple-element.558, f32[512]{0:T(512)S(1)} %bitcast.120, f32[288]{0:T(512)S(1)} %get-tuple-element.559, f32[512]{0:T(512)S(1)} %bitcast.116, ...), kind=kOutput, calls=%fused_computation.23.clone.clone.1 | convolution fusion | flops 76455936 | bytes 864256 | tf_op jit(solution)/shard_map/while/body/eval_jaxpr/dot_general | solution.py:120
  138.4 5.3 %fusion.36 = bf16[9,32,256]{2,1,0:T(8,128)(2,1)} fusion(f32[9,32,256]{2,1,0:T(8,128)S(1)} %bitcast.114, f32[9,32,256]{2,1,0:T(8,128)S(1)} %convolution_add_fusion.3, bf16[864,256]{1,0:T(8,128)(2,1)S(1)} %bitcast.111, f32[9,32]{1,0:T(8,128)S(1)} %get-tuple-element.293, f32[864]{0:T(1024)S(1)} %fusion.141, f32[9,32]{1,0:T(8,128)S(1)} %get-tuple-element.294, ...), kind=kOutput, calls=%fused_computation.66 | convolution fusion | flops 246610944 | bytes 1652736 | tf_op jit(solution)/shard_map/vmap()/dot_general | solution.py:167
  (82 shorter events, 5.8 us)
Async XLA Ops:
  6.5 2.8 %copy-start = (bf16[256,256]{1,0:T(8,128)(2,1)S(1)}, bf16[256,256]{1,0:T(8,128)(2,1)}, u32[]{:S(2)}) copy-start(bf16[256,256]{1,0:T(8,128)(2,1)} %param.15) | copy-start | bytes 393220
  6.5 81.3 %reduce-scatter.2.cloned.1.call-start = ((), (), s32[]{:S(2)}) async-start(), calls=%async_computation.1 | async-start | bytes 2228224 | tf_op jit(solution)/shard_map/reduce_scatter | solution.py:192
  8.1 1.5 copy-start.3
  8.1 1.5 copy-start.5
  8.1 1.5 copy-start.7
  23.4 5.6 %copy-start.9 = (bf16[9,3,32]{2,1,0:T(4,128)(2,1)S(1)}, bf16[9,3,32]{2,1,0:T(4,128)(2,1)}, u32[]{:S(2)}) copy-start(bf16[9,3,32]{2,1,0:T(4,128)(2,1)} %param.12) | copy-start | bytes 5188
  23.4 10.1 %copy-start.1 = (s32[2,3,512]{2,1,0:T(4,128)S(1)}, s32[2,3,512]{2,1,0:T(4,128)}, u32[]{:S(2)}) copy-start(s32[2,3,512]{2,1,0:T(4,128)} %get-tuple-element.570) | copy-start | bytes 36868
  23.4 10.4 %copy-start.10 = (f32[4,256]{1,0:T(4,128)S(1)}, f32[4,256]{1,0:T(4,128)}, u32[]{:S(2)}) copy-start(f32[4,256]{1,0:T(4,128)} %param.16) | copy-start | bytes 12292
  23.4 66.1 %copy-start.4 = (f32[9,32]{1,0:T(8,128)S(1)}, f32[9,32]{1,0:T(8,128)}, u32[]{:S(2)}) copy-start(f32[9,32]{1,0:T(8,128)} %get-tuple-element.576) | copy-start | bytes 3460
  23.4 66.2 %copy-start.6 = (f32[9,32]{1,0:T(8,128)S(1)}, f32[9,32]{1,0:T(8,128)}, u32[]{:S(2)}) copy-start(f32[9,32]{1,0:T(8,128)} %get-tuple-element.577) | copy-start | bytes 3460
  23.4 66.2 %copy-start.8 = (f32[9,32]{1,0:T(8,128)S(1)}, f32[9,32]{1,0:T(8,128)}, u32[]{:S(2)}) copy-start(f32[9,32]{1,0:T(8,128)} %get-tuple-element.578) | copy-start | bytes 3460
  23.4 66.9 %copy-start.11 = (bf16[4,256,256]{2,1,0:T(8,128)(2,1)S(1)}, bf16[4,256,256]{2,1,0:T(8,128)(2,1)}, u32[]{:S(2)}) copy-start(bf16[4,256,256]{2,1,0:T(8,128)(2,1)} %param.14) | copy-start | bytes 1572868
  23.4 103.8 %all-gather.2.cloned.1.call-start = ((), (), s32[]{:S(2)}) async-start(), calls=%async_computation.2 | async-start | bytes 1114112 | tf_op jit(solution)/shard_map/all_gather | solution.py:203
  23.5 66.8 %collective-permute-start.3 = (bf16[9,32,256]{2,1,0:T(8,128)(2,1)S(1)}, bf16[9,32,256]{2,1,0:T(8,128)(2,1)S(1)}, u32[]{:S(2)}, u32[]{:S(2)}) collective-permute-start(bf16[9,32,256]{2,1,0:T(8,128)(2,1)S(1)} %fusion.102), channel_id=1, source_target_pairs={{1,0},{2,1},{3,2},{4,3},{5,4},{6,5},{7,6},{8,7},{9,8},{10,9},{11,1... | collective-permute-start | bytes 442376 | tf_op jit(solution)/shard_map/ppermute | solution.py:23
  29.0 61.3 %collective-permute-start.2 = (bf16[9,32,256]{2,1,0:T(8,128)(2,1)S(1)}, bf16[9,32,256]{2,1,0:T(8,128)(2,1)S(1)}, u32[]{:S(2)}, u32[]{:S(2)}) collective-permute-start(bf16[9,32,256]{2,1,0:T(8,128)(2,1)S(1)} %fusion.102), channel_id=1, source_target_pairs={{0,1},{1,2},{2,3},{3,4},{4,5},{5,6},{6,7},{7,8},{8,9},{9,10},{10,1... | collective-permute-start | bytes 442376 | tf_op jit(solution)/shard_map/ppermute | solution.py:22
  29.0 60.7 %collective-permute-start.1 = (bf16[9,3,32]{2,1,0:T(4,128)(2,1)S(1)}, bf16[9,3,32]{2,1,0:T(4,128)(2,1)S(1)}, u32[]{:S(2)}, u32[]{:S(2)}) collective-permute-start(bf16[9,3,32]{2,1,0:T(4,128)(2,1)S(1)} %copy-done.9), channel_id=1, source_target_pairs={{1,0},{2,1},{3,2},{4,3},{5,4},{6,5},{7,6},{8,7},{9,8},{10,9},{11,1... | collective-permute-start | bytes 5192 | tf_op jit(solution)/shard_map/ppermute | solution.py:23
  33.4 56.3 %collective-permute-start = (bf16[9,3,32]{2,1,0:T(4,128)(2,1)S(1)}, bf16[9,3,32]{2,1,0:T(4,128)(2,1)S(1)}, u32[]{:S(2)}, u32[]{:S(2)}) collective-permute-start(bf16[9,3,32]{2,1,0:T(4,128)(2,1)S(1)} %copy-done.9), channel_id=1, source_target_pairs={{0,1},{1,2},{2,3},{3,4},{4,5},{5,6},{6,7},{7,8},{8,9},{9,10},{10,1... | collective-permute-start | bytes 5192 | tf_op jit(solution)/shard_map/ppermute | solution.py:22
  127.2 11.2 %copy-start.2 = (bf16[9,32,256]{2,1,0:T(8,128)(2,1)S(1)}, bf16[9,32,256]{2,1,0:T(8,128)(2,1)}, u32[]{:S(2)}) copy-start(bf16[9,32,256]{2,1,0:T(8,128)(2,1)} %param.11) | copy-start | bytes 442372
Sparse Core Ops, SparseCore 0:
  23.5 64.2 reduce-scatter.1
  90.2 36.9 all-gather.1
where the time goes:
time: 151 us
  waiting for transfers between devices  76.7 us (51%)
  matrix products  38 us (25%)
  between operations  13.7 us (9%)
  starting transfers between devices  9.98 us (7%)
  other arithmetic  6.27 us (4%)
  local copies, waits for them, and re-layouts  5.82 us (4%)
    reduce_scatter x1, waiting for transfers between devices, local(): lax.psum_scatter(structure_terms(positions, charges, wave_rows, layers_to...  53.8 us
    all_gather x1, waiting for transfers between devices, local(): lax.all_gather(filtered, 'space', axis=0, tiled=True)  22.9 us
    dot_general x4, matrix products, cell_short(): jnp.dot(pair_weights, values[basis_index], preferred_element_type=jnp.flo...  19.3 us
    ppermute x2, starting transfers between devices, with_halo(): after = lax.ppermute(leading, axis, down)  9.93 us
    dot_general x2, matrix products, structure_one_block(): lax.dot_general(sine_part, charges, (((0,), (0,)), ((), ())), preferred_e...  4.7 us
    dot_general x2, matrix products, structure_one_block(): lax.dot_general(cosine, charges, (((0,), (0,)), ((), ())), preferred_elem...  4.65 us
    dot_general x2, matrix products, add_one_block(): jnp.dot(sine_part, factors[:, feature_width:], preferred_element_type=jnp...  4.45 us
    dot_general x2, matrix products, add_one_block(): jnp.dot(cosine, factors[:, :feature_width], preferred_element_type=jnp.fl...  4.38 us
  transfers between devices with their start and end apart: 6, of which 2 were waited for; matrix products, arithmetic and copies ran while one was open for 11% of the time, Pallas kernels for 0%

commit v1 on v0

v1 whole, which is shorter than its diff:
```python
import functools
import math

import jax
import jax.numpy as jnp
from jax import lax
from jax.experimental import pallas as pl
from jax.experimental.pallas import tpu as pltpu
from jax.sharding import PartitionSpec as P

GRID = 3
CUTOFF = 1.0
BF16 = jnp.bfloat16
F32 = jnp.float32
COORD_ROWS = 16
LANES = 128
SINE = (4.44287959, -7.30781805, 3.59778873, -0.791238217)
COSINE = (1.4142135, -6.97885099, 5.73946117, -1.88356299, 0.310698193)
HALF_COSINE = (0.999999953, -1.23369821, 0.253650745, -0.0208106275, 0.000858190619)
PARAMS = pltpu.CompilerParams(vmem_limit_bytes=40 * 1024 * 1024)


def horner(coefficients, value):
    total = coefficients[-1]
    for coefficient in coefficients[-2::-1]:
        total = total * value + coefficient
    return total


def turn_cos_sin(scaled, scale):
    turns = scaled * scale
    rest = turns - jnp.round(turns)
    square = rest * rest
    half_sine = horner(SINE, square) * rest
    half_cosine = horner(COSINE, square)
    return (1.0 - half_sine * half_sine, half_sine * half_cosine)


def pad_up(value, unit):
    return -(-value // unit) * unit


def tails_side_by_side(rows_of, width, tail):
    lane = lax.broadcasted_iota(jnp.int32, (COORD_ROWS, width), 1)
    total = jnp.zeros((COORD_ROWS, width), F32)
    for l, rows in enumerate(rows_of):
        total = jnp.where((lane >= l * tail) & (lane < (l + 1) * tail), rows[:, :width], total)
    return total


def structure_kernel(chunk_count, atoms, scale, first, last, *refs):
    chunks = refs[:chunk_count]
    refs = refs[chunk_count:]
    main_ref, tail_ref = refs[:2]
    refs = refs[2:]
    if not first:
        sum_ref, refs = refs[0], refs[1:]
    if last:
        mine_ref, send_ref, refs = refs[0], refs[1], refs[2:]
    else:
        out_ref, refs = refs[0], refs[1:]
    phase_ref, table_ref, stack_ref = refs
    waves = main_ref.shape[0]
    half = waves // 2
    width = chunks[0].shape[1]
    tail = atoms - width
    depth = stack_ref.shape[0]
    tail_width = depth - chunk_count * width
    step = 32

    def fill(first_lane, lanes):
        def body(index, carry):
            row = pl.multiple_of(index * step, step)
            cosine, sine = turn_cos_sin(phase_ref[pl.ds(row, step), 0:lanes], scale)
            place = row + jnp.where(row >= half, half, 0)
            place = pl.multiple_of(place, step)
            table_ref[pl.ds(place, step), first_lane : first_lane + lanes] = cosine.astype(BF16)
            table_ref[pl.ds(place + half, step), first_lane : first_lane + lanes] = sine.astype(BF16)
            return carry

        lax.fori_loop(0, waves // step, body, 0, unroll=2)

    for l, chunk in enumerate(chunks):
        stack_ref[l * width : (l + 1) * width, :] = chunk[0:width, :]
        at = chunk_count * width + l * tail
        stack_ref[at : at + tail, :] = chunk[width:atoms, :]
    used = chunk_count * width + chunk_count * tail
    if used < depth:
        stack_ref[used:depth, :] = jnp.zeros((depth - used, width), BF16)
    for l, chunk in enumerate(chunks):
        phase_ref[...] = jnp.dot(
            main_ref[...], chunk[atoms : atoms + COORD_ROWS, :], preferred_element_type=F32
        )
        fill(l * width, width)
    rows = tails_side_by_side(
        [chunk[atoms : atoms + COORD_ROWS, :].astype(F32) for chunk in chunks], tail_width, tail
    )
    phase_ref[:, 0:tail_width] = jnp.dot(
        tail_ref[...], rows.astype(BF16), preferred_element_type=F32
    )
    fill(chunk_count * width, tail_width)
    total = jnp.dot(table_ref[...], stack_ref[...], preferred_element_type=F32)
    if not first:
        total = total + sum_ref[...]
    if last:
        mine_ref[...] = total[0:waves]
        send_ref[...] = total[waves:].astype(BF16)
    else:
        out_ref[...] = total


def add_structure(chunks, main_waves, tail_waves, running, atoms, scale, last):
    count = len(chunks)
    width = chunks[0].shape[1]
    waves = main_waves.shape[0]
    tail_width = pad_up(count * (atoms - width), LANES)
    depth = count * width + tail_width
    if last:
        shapes = (
            jax.ShapeDtypeStruct((waves, width), F32),
            jax.ShapeDtypeStruct((waves, width), BF16),
        )
    else:
        shapes = jax.ShapeDtypeStruct((2 * waves, width), F32)
    more = () if running is None else (running,)
    return pl.pallas_call(
        functools.partial(structure_kernel, count, atoms, scale, running is None, last),
        out_shape=shapes,
        scratch_shapes=[
            pltpu.VMEM((waves, width), F32),
            pltpu.VMEM((2 * waves, depth), BF16),
            pltpu.VMEM((depth, width), BF16),
        ],
        compiler_params=PARAMS,
        cost_estimate=pl.CostEstimate(
            flops=60 * 2 * waves * depth * width // 10,
            bytes_accessed=8 * waves * width,
            transcendentals=0,
        ),
        name="structure",
    )(*chunks, main_waves, tail_waves, *more)


def own_table_kernel(scale, own_ref, waves_ref, table_ref, phase_ref):
    waves = waves_ref.shape[1]
    half = waves // 2
    atoms = own_ref.shape[0]
    phase_ref[...] = jnp.dot(own_ref[...], waves_ref[...], preferred_element_type=F32)
    step = 16

    def body(index, carry):
        row = pl.multiple_of(index * step, step)
        for block in range(2):
            cosine, sine = turn_cos_sin(
                phase_ref[pl.ds(row, step), block * half : (block + 1) * half], scale
            )
            at = block * waves
            table_ref[pl.ds(row, step), at : at + half] = cosine.astype(BF16)
            table_ref[pl.ds(row, step), at + half : at + waves] = sine.astype(BF16)
        return carry

    lax.fori_loop(0, atoms // step, body, 0)


def own_table(own_cols, main_waves_t, scale):
    atoms, waves = own_cols.shape[0], main_waves_t.shape[1]
    return pl.pallas_call(
        functools.partial(own_table_kernel, scale),
        out_shape=jax.ShapeDtypeStruct((atoms, 2 * waves), BF16),
        scratch_shapes=[pltpu.VMEM((atoms, waves), F32)],
        compiler_params=PARAMS,
        cost_estimate=pl.CostEstimate(
            flops=1200 * atoms * waves, bytes_accessed=4 * atoms * waves, transcendentals=0
        ),
        name="own_table",
    )(own_cols, main_waves_t)


def short_kernel(
    cells, slots, basis_count, side_ref, own_ref, side_chunk_ref, far_ref, cols_ref, radial_ref,
    out_ref, near_ref, weight_ref, mixed_ref,
):
    atoms = cells * slots
    width = own_ref.shape[1]
    tail = atoms - width
    chunks = (own_ref, side_chunk_ref, far_ref)
    near = near_ref.shape[0]
    tail_width = near - 3 * width
    side = side_ref[0].astype(F32)
    shifts = (0.0, side, -side)
    mains, tails = [], []
    tail_lane = lax.broadcasted_iota(jnp.int32, (1, tail_width), 1)
    shift_row = jnp.zeros((1, tail_width), F32)
    for l, chunk in enumerate(chunks):
        near_ref[l * width : (l + 1) * width, :] = chunk[0:width, :]
        at = 3 * width + l * tail
        near_ref[at : at + tail, :] = chunk[width:atoms, :]
        rows = chunk[atoms : atoms + COORD_ROWS, :].astype(F32)
        mains.append(
            (rows[0:1], rows[1:2], rows[3:4], rows[4:5], rows[5:6] + shifts[l])
        )
        tails.append(rows)
        here = (tail_lane >= l * tail) & (tail_lane < (l + 1) * tail)
        shift_row = jnp.where(here, shifts[l], shift_row)
    used = 3 * (width + tail)
    if used < near:
        near_ref[used:near, :] = jnp.zeros((near - used, width), BF16)
    joined = tails_side_by_side(tails, tail_width, tail)
    mains.append(
        (joined[8:9], joined[9:10], joined[11:12], joined[12:13], joined[13:14] + shift_row)
    )
    cell_x, cell_y, off_x, off_y, off_z = (
        jnp.concatenate([part[k] for part in mains], axis=1) for k in range(5)
    )
    lane = lax.broadcasted_iota(jnp.int32, (1, near), 1)
    own_index = jnp.where(
        lane < width,
        lane,
        jnp.where((lane >= 3 * width) & (lane < 3 * width + tail), lane - 2 * width, near),
    )

    def wrapped(delta):
        return jnp.where(
            delta >= GRID - 1.0, delta - GRID, jnp.where(delta < -1.0, delta + GRID, delta)
        )

    step = 16
    sharp = basis_count / CUTOFF
    for cell in range(cells):
        row_x = wrapped(cell_x - float(cell // GRID)) + off_x
        row_y = wrapped(cell_y - float(cell % GRID)) + off_y
        for row in range(cell * slots, (cell + 1) * slots, step):
            own = cols_ref[row : row + step, :].astype(F32)
            delta_x = row_x - own[:, 3:4]
            delta_y = row_y - own[:, 4:5]
            delta_z = off_z - own[:, 5:6]
            square = delta_x * delta_x + delta_y * delta_y + delta_z * delta_z
            radius = jnp.sqrt(square)
            root = horner(HALF_COSINE, square * (1.0 / (CUTOFF * CUTOFF)))
            own_row = row + lax.broadcasted_iota(jnp.int32, (step, 1), 0)
            counted = (radius < CUTOFF) & (own_index != own_row)
            smooth = jnp.where(counted, root * root, 0.0)
            for basis in range(basis_count):
                scaled = (radius - (basis + 0.5) * CUTOFF / basis_count) * sharp
                weight_ref[basis * atoms + row : basis * atoms + row + step, :] = (
                    jnp.exp(-(scaled * scaled)) * smooth
                ).astype(BF16)
    for basis in range(basis_count):
        mixed_ref[:, basis * width : (basis + 1) * width] = jnp.dot(
            weight_ref[basis * atoms : (basis + 1) * atoms, :],
            near_ref[...],
            preferred_element_type=F32,
        ).astype(BF16)
    out_ref[...] = jnp.dot(mixed_ref[...], radial_ref[...], preferred_element_type=F32)


def short_range(side, own, side_chunk, far, own_cols, radial_flat, cells, slots, basis_count):
    atoms = cells * slots
    width = own.shape[1]
    near = 3 * width + pad_up(3 * (atoms - width), LANES)
    vmem = pl.BlockSpec(memory_space=pltpu.VMEM)
    return pl.pallas_call(
        functools.partial(short_kernel, cells, slots, basis_count),
        out_shape=jax.ShapeDtypeStruct((atoms, width), F32),
        in_specs=[pl.BlockSpec(memory_space=pltpu.SMEM)] + [vmem] * 5,
        out_specs=vmem,
        scratch_shapes=[
            pltpu.VMEM((near, width), BF16),
            pltpu.VMEM((basis_count * atoms, near), BF16),
            pltpu.VMEM((atoms, basis_count * width), BF16),
        ],
        compiler_params=PARAMS,
        cost_estimate=pl.CostEstimate(
            flops=10 * basis_count * atoms * near * width, bytes_accessed=4 * near * width,
            transcendentals=0,
        ),
        name="short_range",
    )(side, own, side_chunk, far, own_cols, radial_flat)


def filter_kernel(mine_ref, other_ref, charge_ref, gain_ref, out_ref):
    half = gain_ref.shape[0]
    total = mine_ref[...] + other_ref[...].astype(F32)
    structure = jnp.dot(total.astype(BF16), charge_ref[...], preferred_element_type=F32)
    gain = gain_ref[...]
    out_ref[0:half] = (structure[0:half] * gain).astype(BF16)
    out_ref[half:] = (structure[half:] * gain).astype(BF16)


def filter_half(mine, other, charge_weight, gain):
    return pl.pallas_call(
        filter_kernel,
        out_shape=jax.ShapeDtypeStruct(mine.shape, BF16),
        compiler_params=PARAMS,
        name="filter",
    )(mine, other, charge_weight, gain)


def inverse_kernel(scale, table_ref, factor_ref, base_ref, out_ref):
    out_ref[...] = base_ref[...] + scale * jnp.dot(
        table_ref[...], factor_ref[...], preferred_element_type=F32
    )


def finish_kernel(scale, slots, counts_ref, table_ref, factor_ref, base_ref, out_ref):
    total = base_ref[...] + scale * jnp.dot(
        table_ref[...], factor_ref[...], preferred_element_type=F32
    )
    slot = lax.broadcasted_iota(jnp.int32, (slots, total.shape[1]), 0)
    for cell in range(total.shape[0] // slots):
        rows = total[cell * slots : (cell + 1) * slots]
        out_ref[cell] = jnp.where(slot < counts_ref[cell], rows, 0.0).astype(BF16)


def local(atom_features, offsets, counts, radial_weight, charge_weight, wave_filter, wavevectors):
    cells, slots, width = atom_features.shape
    atoms = cells * slots
    basis_count = radial_weight.shape[0]
    wave_count = wavevectors.shape[1]
    size = lax.axis_size("space")
    layer = lax.axis_index("space")
    cores = 2 if size % 2 == 0 else 1
    near_y = 2 if (size // cores) % 2 == 0 else 1
    deep = size // (cores * near_y)
    core = layer % cores
    half = wave_count // 2

    slot_ids = jnp.arange(slots, dtype=jnp.int32)
    live = slot_ids[None, :] < counts[:, None]
    masked = jnp.where(live[:, :, None], atom_features, jnp.zeros((), BF16)).reshape(atoms, width)
    cell_ids = jnp.arange(cells, dtype=jnp.int32)
    cell_of = jnp.repeat(cell_ids, slots)
    flat_offsets = jnp.transpose(offsets, (1, 0, 2)).reshape(3, atoms)
    places = jnp.concatenate(
        [
            jnp.stack(
                [cell_of // GRID, cell_of % GRID, jnp.broadcast_to(layer, (atoms,))]
            ).astype(BF16),
            flat_offsets,
            jnp.zeros((2, atoms), BF16),
        ],
        axis=0,
    )
    tail = atoms - width
    coords = jnp.concatenate(
        [places[:, :width], jnp.tile(places[:, width:], (1, width // tail))], axis=0
    )
    payload = jnp.concatenate([masked, coords], axis=0)

    def swap(value, mask):
        return lax.ppermute(value, "space", [(i, i ^ mask) for i in range(size)])

    stride = cores * near_y
    along = {k: swap(payload, k * stride) for k in range(deep - 1, 0, -1)}
    beside = swap(payload, cores)
    pair = swap(payload, 1)
    across = {k: swap(along[k], cores) for k in sorted(along)}

    own_half = lax.dynamic_slice_in_dim(wavevectors, core * half, half, 1)
    other_half = lax.dynamic_slice_in_dim(wavevectors, (1 - core) * half, half, 1)
    waves = jnp.concatenate([own_half, other_half], axis=1)
    steps = jnp.array([[size], [size], [GRID]], jnp.int32)
    one = (waves * steps).astype(BF16)
    blank = jnp.zeros((2, wave_count), BF16)
    rows_main = jnp.concatenate([one, one, blank, jnp.zeros((8, wave_count), BF16)], axis=0)
    rows_tail = jnp.concatenate([jnp.zeros((8, wave_count), BF16), one, one, blank], axis=0)
    main_waves, tail_waves = rows_main.T, rows_tail.T
    scale = 1.0 / (GRID * size)
    own_cols = jnp.concatenate([places, jnp.zeros((8, atoms), BF16)], axis=0).T

    two_pi = 2.0 * math.pi
    wave_float = own_half.astype(F32)
    along_x = two_pi * wave_float[0] / GRID
    along_y = two_pi * wave_float[1] / GRID
    along_z = two_pi * wave_float[2] / size
    magnitude = jnp.sqrt(along_x * along_x + along_y * along_y + along_z * along_z)
    gain = jnp.zeros((half, width), F32)
    for b in range(wave_filter.shape[0]):
        offset_k = (magnitude - 3.0 * b) / 3.0
        gain = gain + jnp.exp(-(offset_k * offset_k))[:, None] * wave_filter[b][None, :]

    table = own_table(own_cols, rows_main, scale)

    z = layer // stride
    y = (layer // cores) % near_y
    step_z = jnp.where(core == 0, 1, deep - 1)
    wanted = z ^ ((z + step_z) % deep)
    crossing = beside
    for k in across:
        if k & (k + 1) == 0:
            take = (wanted == k) & (y == jnp.where(core == 0, near_y - 1, 0))
            crossing = jnp.where(take, across[k], crossing)
    far = swap(crossing, 1)
    side = jnp.where(core == 0, 1, -1).astype(jnp.int32).reshape(1)
    short = short_range(
        side, payload, pair, far, own_cols, radial_weight.reshape(basis_count * width, width),
        cells, slots, basis_count,
    )

    early = [payload, beside] + [along[k] for k in along]
    late = [across[k] for k in across]
    groups = [early[i : i + 4] for i in range(0, len(early), 4)]
    groups += [late[i : i + 4] for i in range(0, len(late), 4)]
    running = None
    for index, group in enumerate(groups):
        running = add_structure(
            group, main_waves, tail_waves, running, atoms, scale, index == len(groups) - 1
        )
    mine, send = running
    factors = filter_half(mine, swap(send, 1), charge_weight, gain)
    other_factors = swap(factors, 1)

    base = atom_features.reshape(atoms, width).astype(F32) + short * (1.0 / math.sqrt(slots))
    recip_scale = 1.0 / math.sqrt(atoms * size * wave_count)
    vmem = pl.BlockSpec(memory_space=pltpu.VMEM)
    base = pl.pallas_call(
        functools.partial(inverse_kernel, recip_scale),
        grid=(1,),
        in_specs=[
            pl.BlockSpec((atoms, wave_count), lambda i: (0, 0)),
            pl.BlockSpec((wave_count, width), lambda i: (0, 0)),
            pl.BlockSpec((atoms, width), lambda i: (0, 0)),
        ],
        out_specs=pl.BlockSpec((atoms, width), lambda i: (0, 0)),
        out_shape=jax.ShapeDtypeStruct((atoms, width), F32),
        compiler_params=PARAMS,
        name="inverse",
    )(table, factors, base)
    return pl.pallas_call(
        functools.partial(finish_kernel, recip_scale, slots),
        grid=(1,),
        in_specs=[
            pl.BlockSpec(memory_space=pltpu.SMEM),
            pl.BlockSpec((atoms, wave_count), lambda i: (0, 1)),
            pl.BlockSpec((wave_count, width), lambda i: (0, 0)),
            pl.BlockSpec((atoms, width), lambda i: (0, 0)),
        ],
        out_specs=pl.BlockSpec((cells, slots, width), lambda i: (0, 0, 0)),
        out_shape=jax.ShapeDtypeStruct((cells, slots, width), BF16),
        compiler_params=PARAMS,
        name="finish",
    )(counts, table, other_factors, base)


def solution(mesh):
    in_specs = (
        P(("groups", "space"), None, None),
        P(("groups", "space"), None, None),
        P(("groups", "space")),
        P(),
        P(),
        P(),
        P(),
    )
    out_specs = P(("groups", "space"), None, None)
    return jax.shard_map(local, mesh=mesh, in_specs=in_specs, out_specs=out_specs, check_vma=False)
```

time: 151 us -> 51.6 us (0.34)
  waiting for transfers between devices: 76.7 us -> 8.68 us
  matrix products: 38 us -> 0 us
  Pallas kernels: 0 us -> 24.3 us
  between operations: 13.7 us -> 0.36 us
  local copies, waits for them, and re-layouts: 5.82 us -> 2 us
  other arithmetic: 6.27 us -> 4.4 us
  starting transfers between devices: 9.98 us -> 11.5 us
    reduce_scatter x1 -> x0, waiting for transfers between devices: 53.8 us -> none  [local(): lax.psum_scatter(structure_terms(positions, charges, wave_rows, layers_to...]
    dot_general x14 -> x0, matrix products: 38 us -> none  [the longest x4 19.3 us: cell_short(): jnp.dot(pair_weights, values[basis_index], preferred_element_type=jnp.flo...]
    pallas_call x0 -> x8, Pallas kernels: none -> 24.3 us  [the longest x3 17.5 us: add_structure(): pl.pallas_call(functools.partial(structure_kernel, count, atoms, scale, r...]
    all_gather x1 -> x0, waiting for transfers between devices: 22.9 us -> none  [local(): lax.all_gather(filtered, 'space', axis=0, tiled=True)]
    ppermute x4 -> x11, waiting for transfers between devices: 0.01 us -> 8.68 us  [swap(): return lax.ppermute(value, 'space', [(i, i ^ mask) for i in range(size)])]
    convert_element_type x11 -> x2, other arithmetic: 5.54 us -> 1.45 us  [the longest x1 0.73 us: local(): one = (waves * steps).astype(BF16)]
    dynamic_update_slice x4 -> x0, local copies, waits for them, and re-layouts: 2.77 us -> none  [structure_terms(): lax.map(structure_one_block, pieces).reshape(row_count, 2 * feature_width)]
    squeeze x3 -> x0, local copies, waits for them, and re-layouts: 2.27 us -> none  [the longest x2 2.2 us: add_inverse(): outcome = lax.scan(add_one_block, running, (factor_blocks, wave_blocks))]
  transfers between devices with their start and end apart: 6 -> 11, of which waited for: 2 -> 3; matrix products, arithmetic and copies ran while one was open for 11% -> 6% of each run, Pallas kernels for 0% -> 44%
where the time goes in v1:
time: 51.6 us; the launch traced here: 51.2 us
  Pallas kernels  24.3 us (47%)
  starting transfers between devices  11.5 us (22%)
  waiting for transfers between devices  8.68 us (17%)
  other arithmetic  4.4 us (9%)
  local copies, waits for them, and re-layouts  2 us (4%)
    pallas_call x3, Pallas kernels, add_structure(): pl.pallas_call(functools.partial(structure_kernel, count, atoms, scale, r...  17.5 us
    ppermute x11, starting transfers between devices, swap(): return lax.ppermute(value, 'space', [(i, i ^ mask) for i in range(size)])  11.5 us
    ppermute x11, waiting for transfers between devices, swap(): return lax.ppermute(value, 'space', [(i, i ^ mask) for i in range(size)])  8.68 us
    pallas_call x1, Pallas kernels, short_range(): pl.pallas_call(functools.partial(short_kernel, cells, slots, basis_count)...  3.33 us
    pallas_call x1, Pallas kernels, local(): pl.pallas_call(functools.partial(finish_kernel, recip_scale, slots), grid...  1.52 us
    pallas_call x1, Pallas kernels, own_table(): pl.pallas_call(functools.partial(own_table_kernel, scale), out_shape=jax....  1.29 us
  transfers between devices with their start and end apart: 11, of which 3 were waited for; matrix products, arithmetic and copies ran while one was open for 6% of the time, Pallas kernels for 44%

profile of v1, /device:TPU:0, one launch (start us, length us, event | category | flops | bytes accessed | tf_op | source)
XLA Modules:
  0.0 51.2 jit_solution(10257902928894846395)
XLA Ops:
  0.3 0.7 %copy.32 = bf16[3,9,32]{2,1,0:T(8,128)(2,1)S(1)} copy(bf16[3,9,32]{2,0,1:T(4,128)(2,1)} %bitcast.28) | data formatting | bytes 3456 | tf_op jit(solution)/shard_map/transpose | solution.py:333
  1.3 0.7 %iota_compare_fusion = pred[9,32]{1,0:T(8,128)(4,1)S(1)} fusion(s32[9]{0:T(128)} %counts_ref.1), kind=kLoop, calls=%fused_computation.13 | loop fusion | flops 288 | bytes 324 | tf_op jit(solution)/shard_map/lt | solution.py:329
  2.0 1.0 %broadcast_select_fusion = bf16[9,32,256]{2,1,0:T(8,128)(2,1)S(1)} fusion(bf16[9,32,256]{2,1,0:T(8,128)(2,1)} %param.8, pred[9,32]{1,0:T(8,128)(4,1)S(1)} %iota_compare_fusion), kind=kLoop, calls=%fused_computation.4 | loop fusion | flops 73728 | bytes 295200 | tf_op jit(solution)/shard_map/jit(_where)/select_n | solution.py:330
  3.0 3.1 %collective-permute-start = (bf16[304,256]{1,0:T(8,128)(2,1)S(1)}, bf16[304,256]{1,0:T(8,128)(2,1)S(1)}, u32[]{:S(2)}, u32[]{:S(2)}) collective-permute-start(bf16[304,256]{1,0:T(8,128)(2,1)S(1)} %pad_maximum_fusion.refs_0_.own_ref), channel_id=1, source_target_pairs={{0,4},{1,5},{2,6},{3,7},{4,0},{5,1},{6,2},{7,3},{8,12},{9,13},{10,... | collective-permute-start | bytes 466952 | tf_op jit(solution)/shard_map/ppermute | solution.py:351
  6.1 2.5 %collective-permute-start.4 = (bf16[304,256]{1,0:T(8,128)(2,1)S(1)}, bf16[304,256]{1,0:T(8,128)(2,1)S(1)}, u32[]{:S(2)}, u32[]{:S(2)}) collective-permute-start(bf16[304,256]{1,0:T(8,128)(2,1)S(1)} %pad_maximum_fusion.refs_0_.own_ref), channel_id=1, source_target_pairs={{0,12},{1,13},{2,14},{3,15},{4,8},{5,9},{6,10},{7,11},{8,4},{9,5},... | collective-permute-start | bytes 466952 | tf_op jit(solution)/shard_map/ppermute | solution.py:351
  8.6 1.5 %collective-permute-start.6 = (bf16[304,256]{1,0:T(8,128)(2,1)S(1)}, bf16[304,256]{1,0:T(8,128)(2,1)S(1)}, u32[]{:S(2)}, u32[]{:S(2)}) collective-permute-start(bf16[304,256]{1,0:T(8,128)(2,1)S(1)} %pad_maximum_fusion.refs_0_.own_ref), channel_id=1, source_target_pairs={{0,2},{1,3},{2,0},{3,1},{4,6},{5,7},{6,4},{7,5},{8,10},{9,11},{10,... | collective-permute-start | bytes 466952 | tf_op jit(solution)/shard_map/ppermute | solution.py:351
  10.2 0.7 %fusion.11 = (f32[3,512]{1,0:T(4,128)S(1)}, s32[3,512]{1,0:T(4,128)S(1)}, s32[3,512]{1,0:T(4,128)S(1)}) fusion(s32[3,1024]{1,0:T(4,128)} %param.14, s32[]{:T(128)S(6)} %select_n.89, s32[]{:T(128)S(6)} %select_n.90), kind=kLoop, calls=%fused_computation.33 | loop fusion | flops 1536 | bytes 30728 | tf_op jit(solution)/shard_map/convert_element_type | solution.py:372
  11.0 0.7 %fusion = bf16[3,1024]{1,0:T(4,128)(2,1)S(1)} fusion(s32[3,512]{1,0:T(4,128)S(1)} %get-tuple-element.15, s32[3,512]{1,0:T(4,128)S(1)} %get-tuple-element.12, s32[3]{0:T(128)} %constant.120), kind=kLoop, calls=%fused_computation.8 | loop fusion | flops 9216 | bytes 18444 | tf_op jit(solution)/shard_map/convert_element_type | solution.py:363
  12.2 0.6 %collective-permute-start.1 = (bf16[304,256]{1,0:T(8,128)(2,1)S(1)}, bf16[304,256]{1,0:T(8,128)(2,1)S(1)}, u32[]{:S(2)}, u32[]{:S(2)}) collective-permute-start(bf16[304,256]{1,0:T(8,128)(2,1)S(1)} %collective-permute-done.refs_0_), channel_id=1, source_target_pairs={{0,2},{1,3},{2,0},{3,1},{4,6},{5,7},{6,4},{7,5},{8,10},{9,11},{10,... | collective-permute-start | bytes 466952 | tf_op jit(solution)/shard_map/ppermute | solution.py:351
  12.8 4.1 %collective-permute-done.4.refs_2_ = bf16[304,256]{1,0:T(8,128)(2,1)S(1)} collective-permute-done((bf16[304,256]{1,0:T(8,128)(2,1)S(1)}, bf16[304,256]{1,0:T(8,128)(2,1)S(1)}, u32[]{:S(2)}, u32[]{:S(2)}) %collective-permute-start.4) | collective-permute-done | bytes 155680 | tf_op jit(solution)/shard_map/ppermute | solution.py:351
  16.9 1.5 %collective-permute-start.5 = (bf16[304,256]{1,0:T(8,128)(2,1)S(1)}, bf16[304,256]{1,0:T(8,128)(2,1)S(1)}, u32[]{:S(2)}, u32[]{:S(2)}) collective-permute-start(bf16[304,256]{1,0:T(8,128)(2,1)S(1)} %collective-permute-done.4.refs_2_), channel_id=1, source_target_pairs={{0,2},{1,3},{2,0},{3,1},{4,6},{5,7},{6,4},{7,5},{8,10},{9,11},{10,... | collective-permute-start | bytes 466952 | tf_op jit(solution)/shard_map/ppermute | solution.py:351
  18.4 4.0 %collective-permute-done.2.refs_3_ = bf16[304,256]{1,0:T(8,128)(2,1)S(1)} collective-permute-done((bf16[304,256]{1,0:T(8,128)(2,1)S(1)}, bf16[304,256]{1,0:T(8,128)(2,1)S(1)}, u32[]{:S(2)}, u32[]{:S(2)}) %collective-permute-start.2) | collective-permute-done | bytes 155680 | tf_op jit(solution)/shard_map/ppermute | solution.py:351
  22.4 1.6 %collective-permute-start.3 = (bf16[304,256]{1,0:T(8,128)(2,1)S(1)}, bf16[304,256]{1,0:T(8,128)(2,1)S(1)}, u32[]{:S(2)}, u32[]{:S(2)}) collective-permute-start(bf16[304,256]{1,0:T(8,128)(2,1)S(1)} %collective-permute-done.2.refs_3_), channel_id=1, source_target_pairs={{0,2},{1,3},{2,0},{3,1},{4,6},{5,7},{6,4},{7,5},{8,10},{9,11},{10,... | collective-permute-start | bytes 466952 | tf_op jit(solution)/shard_map/ppermute | solution.py:351
  24.0 7.7 %structure.3.refs_3_ = f32[2048,256]{1,0:T(8,128)S(1)} custom-call(bf16[304,256]{1,0:T(8,128)(2,1)S(1)} %pad_maximum_fusion.refs_0_.own_ref, bf16[304,256]{1,0:T(8,128)(2,1)S(1)} %collective-permute-done.6.refs_1_, bf16[304,256]{1,0:T(8,128)(2,1)S(1)} %collective-permute-done.4.refs_2_, bf16[304,256]{1,0:T(8,128)(2,1)S(1)} %collective-permute-done.2.refs_3_, ...), custom_call_target="tpu_custom_call" | custom-call | flops 3623878656 | bytes 2097152 | tf_op jit(solution)/shard_map/structure/pallas_call | solution.py:126
  31.7 2.9 %structure.4.refs_5_ = f32[2048,256]{1,0:T(8,128)S(1)} custom-call(bf16[304,256]{1,0:T(8,128)(2,1)S(1)} %collective-permute-done.refs_0_, bf16[1024,16]{1,0:T(8,128)(2,1)S(1)} %bitcast.19, bf16[1024,16]{1,0:T(8,128)(2,1)S(1)} %bitcast.22, f32[2048,256]{1,0:T(8,128)S(1)} %structure.3.refs_3_), custom_call_target="tpu_custom_call" | custom-call | flops 1207959552 | bytes 2097152 | tf_op jit(solution)/shard_map/structure/pallas_call | solution.py:126
  34.7 6.9 %structure.5 = (f32[1024,256]{1,0:T(8,128)S(1)}, bf16[1024,256]{1,0:T(8,128)(2,1)}) custom-call(bf16[304,256]{1,0:T(8,128)(2,1)S(1)} %collective-permute-done.1.refs_0_, bf16[304,256]{1,0:T(8,128)(2,1)S(1)} %collective-permute-done.3.refs_1_, bf16[304,256]{1,0:T(8,128)(2,1)S(1)} %collective-permute-done.5.refs_2_, bf16[1024,16]{1,0:T(8,128)(2,1)S(1)} %bitcast.20, ...), custom_call_target="tpu_custom_call" | custom-call | flops 2818572288 | bytes 2097152 | tf_op jit(solution)/shard_map/structure/pallas_call | solution.py:126
  41.7 0.7 %select_select_fusion = bf16[304,256]{1,0:T(8,128)(2,1)} fusion(bf16[304,256]{1,0:T(8,128)(2,1)S(1)} %collective-permute-done.5.refs_2_, bf16[304,256]{1,0:T(8,128)(2,1)S(1)} %collective-permute-done.1.refs_0_, bf16[304,256]{1,0:T(8,128)(2,1)S(1)} %collective-permute-done.6.refs_1_, pred[]{:T(512)S(6)} %and.63, pred[]{:T(512)S(6)} %and.62), kind=kLoop, calls=%fused_computation.3 | loop fusion | flops 155648 | bytes 622594 | tf_op jit(solution)/shard_map/jit(_where)/select_n | solution.py:392
  42.4 0.4 collective-permute-start.10
  42.8 0.3 multiply_add_fusion.gain_ref
  43.1 0.6 %collective-permute-done.7.other_ref = bf16[1024,256]{1,0:T(8,128)(2,1)S(1)} collective-permute-done((bf16[1024,256]{1,0:T(8,128)(2,1)}, bf16[1024,256]{1,0:T(8,128)(2,1)S(1)}, u32[]{:S(2)}, u32[]{:S(2)}) %collective-permute-start.7) | collective-permute-done | bytes 524320 | tf_op jit(solution)/shard_map/ppermute | solution.py:351
  44.4 1.3 %own_table.1.table_ref = bf16[288,2048]{1,0:T(8,128)(2,1)S(1)} custom-call(bf16[288,16]{1,0:T(8,128)(2,1)S(1)} %bitcast.24, bf16[16,1024]{1,0:T(8,128)(2,1)S(1)} %get-tuple-element.14.waves_ref), custom_call_target="tpu_custom_call" | custom-call | flops 353894400 | bytes 1179648 | tf_op jit(solution)/shard_map/own_table/pallas_call | solution.py:167
  45.7 3.3 %short_range.1 = f32[288,256]{1,0:T(8,128)S(1)} custom-call(s32[1]{0:T(128)} %bitcast.14.side_ref, bf16[304,256]{1,0:T(8,128)(2,1)S(1)} %pad_maximum_fusion.refs_0_.own_ref, bf16[304,256]{1,0:T(8,128)(2,1)} %collective-permute-done.9.side_chunk_ref, bf16[304,256]{1,0:T(8,128)(2,1)S(1)} %collective-permute-done.10.far_ref, bf16[288,16]{1,0:T(8,128)(2,1)S(1)} %bitcast.25, ...), custom_call_target="tpu_custom_call" | custom-call | flops 2642411520 | bytes 917504 | tf_op jit(solution)/shard_map/short_range/pallas_call | solution.py:262
  49.1 0.3 inverse.1.base_ref
  49.7 1.5 %finish.1 = bf16[9,32,256]{2,1,0:T(8,128)(2,1)} custom-call(s32[9]{0:T(128)S(1)} %copy-done.1, bf16[288,2048]{1,0:T(8,128)(2,1)S(1)} %own_table.1.table_ref, bf16[1024,256]{1,0:T(8,128)(2,1)S(1)} %collective-permute-done.8.factor_ref, f32[288,256]{1,0:T(8,128)S(1)} %inverse.1.base_ref), custom_call_target="tpu_custom_call" | custom-call | tf_op jit(solution)/shard_map/finish/pallas_call | solution.py:429
  (51 shorter events, 2.1 us)
Async XLA Ops:
  3.0 9.1 %collective-permute-start = (bf16[304,256]{1,0:T(8,128)(2,1)S(1)}, bf16[304,256]{1,0:T(8,128)(2,1)S(1)}, u32[]{:S(2)}, u32[]{:S(2)}) collective-permute-start(bf16[304,256]{1,0:T(8,128)(2,1)S(1)} %pad_maximum_fusion.refs_0_.own_ref), channel_id=1, source_target_pairs={{0,4},{1,5},{2,6},{3,7},{4,0},{5,1},{6,2},{7,3},{8,12},{9,13},{10,... | collective-permute-start | bytes 466952 | tf_op jit(solution)/shard_map/ppermute | solution.py:351
  6.1 10.8 %collective-permute-start.4 = (bf16[304,256]{1,0:T(8,128)(2,1)S(1)}, bf16[304,256]{1,0:T(8,128)(2,1)S(1)}, u32[]{:S(2)}, u32[]{:S(2)}) collective-permute-start(bf16[304,256]{1,0:T(8,128)(2,1)S(1)} %pad_maximum_fusion.refs_0_.own_ref), channel_id=1, source_target_pairs={{0,12},{1,13},{2,14},{3,15},{4,8},{5,9},{6,10},{7,11},{8,4},{9,5},... | collective-permute-start | bytes 466952 | tf_op jit(solution)/shard_map/ppermute | solution.py:351
  8.6 15.4 %collective-permute-start.6 = (bf16[304,256]{1,0:T(8,128)(2,1)S(1)}, bf16[304,256]{1,0:T(8,128)(2,1)S(1)}, u32[]{:S(2)}, u32[]{:S(2)}) collective-permute-start(bf16[304,256]{1,0:T(8,128)(2,1)S(1)} %pad_maximum_fusion.refs_0_.own_ref), channel_id=1, source_target_pairs={{0,2},{1,3},{2,0},{3,1},{4,6},{5,7},{6,4},{7,5},{8,10},{9,11},{10,... | collective-permute-start | bytes 466952 | tf_op jit(solution)/shard_map/ppermute | solution.py:351
  10.1 35.6 %collective-permute-start.9 = (bf16[304,256]{1,0:T(8,128)(2,1)S(1)}, bf16[304,256]{1,0:T(8,128)(2,1)}, u32[]{:S(2)}, u32[]{:S(2)}) collective-permute-start(bf16[304,256]{1,0:T(8,128)(2,1)S(1)} %pad_maximum_fusion.refs_0_.own_ref), channel_id=1, source_target_pairs={{0,1},{1,0},{2,3},{3,2},{4,5},{5,4},{6,7},{7,6},{8,9},{9,8},{10,11... | collective-permute-start | bytes 466952 | tf_op jit(solution)/shard_map/ppermute | solution.py:351
  10.1 12.3 %collective-permute-start.2 = (bf16[304,256]{1,0:T(8,128)(2,1)S(1)}, bf16[304,256]{1,0:T(8,128)(2,1)S(1)}, u32[]{:S(2)}, u32[]{:S(2)}) collective-permute-start(bf16[304,256]{1,0:T(8,128)(2,1)S(1)} %pad_maximum_fusion.refs_0_.own_ref), channel_id=1, source_target_pairs={{0,8},{1,9},{2,10},{3,11},{4,12},{5,13},{6,14},{7,15},{8,0},{9,1},... | collective-permute-start | bytes 466952 | tf_op jit(solution)/shard_map/ppermute | solution.py:351
  12.2 22.5 %collective-permute-start.1 = (bf16[304,256]{1,0:T(8,128)(2,1)S(1)}, bf16[304,256]{1,0:T(8,128)(2,1)S(1)}, u32[]{:S(2)}, u32[]{:S(2)}) collective-permute-start(bf16[304,256]{1,0:T(8,128)(2,1)S(1)} %collective-permute-done.refs_0_), channel_id=1, source_target_pairs={{0,2},{1,3},{2,0},{3,1},{4,6},{5,7},{6,4},{7,5},{8,10},{9,11},{10,... | collective-permute-start | bytes 466952 | tf_op jit(solution)/shard_map/ppermute | solution.py:351
  16.9 17.7 %collective-permute-start.5 = (bf16[304,256]{1,0:T(8,128)(2,1)S(1)}, bf16[304,256]{1,0:T(8,128)(2,1)S(1)}, u32[]{:S(2)}, u32[]{:S(2)}) collective-permute-start(bf16[304,256]{1,0:T(8,128)(2,1)S(1)} %collective-permute-done.4.refs_2_), channel_id=1, source_target_pairs={{0,2},{1,3},{2,0},{3,1},{4,6},{5,7},{6,4},{7,5},{8,10},{9,11},{10,... | collective-permute-start | bytes 466952 | tf_op jit(solution)/shard_map/ppermute | solution.py:351
  22.4 12.3 %collective-permute-start.3 = (bf16[304,256]{1,0:T(8,128)(2,1)S(1)}, bf16[304,256]{1,0:T(8,128)(2,1)S(1)}, u32[]{:S(2)}, u32[]{:S(2)}) collective-permute-start(bf16[304,256]{1,0:T(8,128)(2,1)S(1)} %collective-permute-done.2.refs_3_), channel_id=1, source_target_pairs={{0,2},{1,3},{2,0},{3,1},{4,6},{5,7},{6,4},{7,5},{8,10},{9,11},{10,... | collective-permute-start | bytes 466952 | tf_op jit(solution)/shard_map/ppermute | solution.py:351
  34.6 7.0 %copy-start.4 = (f32[4,256]{1,0:T(4,128)S(1)}, f32[4,256]{1,0:T(4,128)}, u32[]{:S(2)}) copy-start(f32[4,256]{1,0:T(4,128)} %param.13) | copy-start | bytes 12292
  34.6 9.1 %copy-start = (bf16[256,256]{1,0:T(8,128)(2,1)S(1)}, bf16[256,256]{1,0:T(8,128)(2,1)}, u32[]{:S(2)}) copy-start(bf16[256,256]{1,0:T(8,128)(2,1)} %charge_ref.1) | copy-start | bytes 393220
  41.6 2.1 %collective-permute-start.7 = (bf16[1024,256]{1,0:T(8,128)(2,1)}, bf16[1024,256]{1,0:T(8,128)(2,1)S(1)}, u32[]{:S(2)}, u32[]{:S(2)}) collective-permute-start(bf16[1024,256]{1,0:T(8,128)(2,1)} %get-tuple-element.8), channel_id=1, source_target_pairs={{0,1},{1,0},{2,3},{3,2},{4,5},{5,4},{6,7},{7,6},{8,9},{9,8},{10,11... | collective-permute-start | bytes 1572872 | tf_op jit(solution)/shard_map/ppermute | solution.py:351
  42.4 3.3 %collective-permute-start.10 = (bf16[304,256]{1,0:T(8,128)(2,1)}, bf16[304,256]{1,0:T(8,128)(2,1)S(1)}, u32[]{:S(2)}, u32[]{:S(2)}) collective-permute-start(bf16[304,256]{1,0:T(8,128)(2,1)} %select_select_fusion), channel_id=1, source_target_pairs={{0,1},{1,0},{2,3},{3,2},{4,5},{5,4},{6,7},{7,6},{8,9},{9,8},{10,11... | collective-permute-start | bytes 466952 | tf_op jit(solution)/shard_map/ppermute | solution.py:351
  43.1 2.6 %copy-start.2 = (bf16[4,256,256]{2,1,0:T(8,128)(2,1)S(1)}, bf16[4,256,256]{2,1,0:T(8,128)(2,1)}, u32[]{:S(2)}) copy-start(bf16[4,256,256]{2,1,0:T(8,128)(2,1)} %param.11) | copy-start | bytes 1572868
  44.0 5.5 %collective-permute-start.8 = (bf16[1024,256]{1,0:T(8,128)(2,1)S(1)}, bf16[1024,256]{1,0:T(8,128)(2,1)S(1)}, u32[]{:S(2)}, u32[]{:S(2)}) collective-permute-start(bf16[1024,256]{1,0:T(8,128)(2,1)S(1)} %filter.1.factor_ref), channel_id=1, source_target_pairs={{0,1},{1,0},{2,3},{3,2},{4,5},{5,4},{6,7},{7,6},{8,9},{9,8},{10,11... | collective-permute-start | bytes 1572872 | tf_op jit(solution)/shard_map/ppermute | solution.py:351
  45.7 3.3 %copy-start.3 = (bf16[9,32,256]{2,1,0:T(8,128)(2,1)S(1)}, bf16[9,32,256]{2,1,0:T(8,128)(2,1)}, u32[]{:S(2)}) copy-start(bf16[9,32,256]{2,1,0:T(8,128)(2,1)} %param.8) | copy-start | bytes 442372
  49.1 0.7 %copy-start.1 = (s32[9]{0:T(128)S(1)}, s32[9]{0:T(128)}, u32[]{:S(2)}) copy-start(s32[9]{0:T(128)} %counts_ref.1) | copy-start | bytes 112

commit v2 on v1

v2 whole, which is shorter than its diff:
```python
import functools
import math

import jax
import jax.numpy as jnp
from jax import lax
from jax.experimental import pallas as pl
from jax.experimental.pallas import tpu as pltpu
from jax.sharding import PartitionSpec as P

GRID = 3
CUTOFF = 1.0
BF16 = jnp.bfloat16
F32 = jnp.float32
COORD_ROWS = 16
LANES = 128
SINE = (4.44287959, -7.30781805, 3.59778873, -0.791238217)
COSINE = (1.4142135, -6.97885099, 5.73946117, -1.88356299, 0.310698193)
HALF_COSINE = (0.999999953, -1.23369821, 0.253650745, -0.0208106275, 0.000858190619)
PARAMS = pltpu.CompilerParams(vmem_limit_bytes=32 * 1024 * 1024)
WIDE = pltpu.CompilerParams(vmem_limit_bytes=62 * 1024 * 1024)


def horner(coefficients, value):
    total = coefficients[-1]
    for coefficient in coefficients[-2::-1]:
        total = total * value + coefficient
    return total


def turn_cos_sin(scaled, scale):
    turns = scaled * scale
    rest = turns - jnp.round(turns)
    square = rest * rest
    half_sine = horner(SINE, square) * rest
    half_cosine = horner(COSINE, square)
    return (1.0 - half_sine * half_sine, half_sine * half_cosine)


def cost(flops):
    return pl.CostEstimate(flops=flops, bytes_accessed=flops // 1000, transcendentals=0)


def in_hbm(value):
    return pltpu.with_memory_space_constraint(value, pltpu.HBM)


def pad_up(value, unit):
    return -(-value // unit) * unit


def tails_side_by_side(rows_of, width, tail):
    lane = lax.broadcasted_iota(jnp.int32, (COORD_ROWS, width), 1)
    total = jnp.zeros((COORD_ROWS, width), F32)
    for l, rows in enumerate(rows_of):
        total = jnp.where((lane >= l * tail) & (lane < (l + 1) * tail), rows[:, :width], total)
    return total


def prepare_kernel(
    layer_ref, counts_any, features_any, offsets_any, payload_ref, cols_ref,
    counts_ref, features_ref, offsets_ref, rows_ref, sems,
):
    copies = [
        pltpu.make_async_copy(source, target, sems.at[i])
        for i, (source, target) in enumerate(
            ((features_any, features_ref), (offsets_any, offsets_ref), (counts_any, counts_ref))
        )
    ]
    for copy in copies:
        copy.start()
    cells, slots, width = features_ref.shape
    atoms = cells * slots
    tail = atoms - width
    slot = lax.broadcasted_iota(jnp.int32, (slots, width), 0)
    lane = lax.broadcasted_iota(jnp.int32, (1, width), 1)
    main_cells = width // slots
    for copy in copies[1:]:
        copy.wait()
    within = [offsets_ref[cell].astype(F32) for cell in range(cells)]
    for first, parts in (
        (0, list(range(main_cells))),
        (8, list(range(main_cells, cells)) * (width // tail)),
    ):
        along_x = jnp.zeros((1, width), F32)
        along_y = jnp.zeros((1, width), F32)
        lives = jnp.zeros((1, width), jnp.int32)
        for place, cell in enumerate(parts):
            here = (lane >= place * slots) & (lane < (place + 1) * slots)
            along_x = jnp.where(here, float(cell // GRID), along_x)
            along_y = jnp.where(here, float(cell % GRID), along_y)
            lives = jnp.where(here, counts_ref[cell] + place * slots, lives)
        rows_ref[first : first + 1, :] = along_x
        rows_ref[first + 1 : first + 2, :] = along_y
        rows_ref[first + 2 : first + 3, :] = jnp.full((1, width), layer_ref[0].astype(F32))
        rows_ref[first + 3 : first + 6, :] = jnp.concatenate([within[c] for c in parts], axis=1)
        rows_ref[first + 6 : first + 7, :] = jnp.where(lane < lives, 1.0, 0.0)
        rows_ref[first + 7 : first + 8, :] = jnp.zeros((1, width), F32)
    rows = rows_ref[...]
    payload_ref[atoms : atoms + COORD_ROWS, :] = rows.astype(BF16)
    cols_ref[0:width, :] = rows.T
    cols_ref[width:atoms, 0:8] = rows[8:16, 0:LANES].T[0:tail]
    cols_ref[width:atoms, 8:16] = jnp.zeros((tail, 8), F32)
    copies[0].wait()
    for cell in range(cells):
        rows = features_ref[cell].astype(F32)
        payload_ref[cell * slots : (cell + 1) * slots, :] = jnp.where(
            slot < counts_ref[cell], rows, 0.0
        ).astype(BF16)


def prepare(layer, counts, atom_features, offsets):
    cells, slots, width = atom_features.shape
    atoms = cells * slots
    smem = pl.BlockSpec(memory_space=pltpu.SMEM)
    vmem = pl.BlockSpec(memory_space=pltpu.VMEM)
    anywhere = pl.BlockSpec(memory_space=pltpu.HBM)
    return pl.pallas_call(
        prepare_kernel,
        out_shape=(
            jax.ShapeDtypeStruct((atoms + COORD_ROWS, width), BF16),
            jax.ShapeDtypeStruct((atoms, COORD_ROWS), F32),
        ),
        in_specs=[smem, anywhere, anywhere, anywhere],
        out_specs=(vmem, vmem),
        scratch_shapes=[
            pltpu.SMEM(counts.shape, jnp.int32),
            pltpu.VMEM(atom_features.shape, BF16),
            pltpu.VMEM(offsets.shape, BF16),
            pltpu.VMEM((COORD_ROWS, width), F32),
            pltpu.SemaphoreType.DMA((3,)),
        ],
        compiler_params=PARAMS,
        name="prepare",
    )(layer, *map(in_hbm, (counts, atom_features, offsets)))


def wave_kernel(
    size, core_ref, waves_any, filter_any, payload_ref, rows_ref, main_ref, tail_ref, gain_ref, passed_ref,
    waves_ref, filter_ref, all_ref, sems,
):
    copies = (
        pltpu.make_async_copy(waves_any, waves_ref, sems.at[0]),
        pltpu.make_async_copy(filter_any, filter_ref, sems.at[1]),
    )
    for copy in copies:
        copy.start()
    passed_ref[...] = payload_ref[...]
    for copy in copies:
        copy.wait()
    wave_count = waves_ref.shape[1]
    half = wave_count // 2
    basis_count, width = filter_ref.shape
    core = core_ref[0]
    all_ref[...] = jnp.zeros(all_ref.shape, F32)
    for place in range(2):
        start = pl.multiple_of((core if place == 0 else 1 - core) * half, LANES)
        taken = waves_ref[:, pl.ds(start, half)].astype(F32)
        at = slice(place * half, (place + 1) * half)
        for first in (0, 3):
            all_ref[first : first + 2, at] = taken[0:2] * float(size)
            all_ref[first + 2 : first + 3, at] = taken[2:3] * float(GRID)
    rows = all_ref[...]
    rows_ref[...] = rows.astype(BF16)
    columns = rows.T
    main_ref[...] = columns.astype(BF16)
    tail_ref[...] = jnp.concatenate([rows[8:16], rows[0:8]], axis=0).T.astype(BF16)
    own = columns[0:half]
    per_step = 2.0 * math.pi / (GRID * size)
    along_x, along_y, along_z = own[:, 0:1] * per_step, own[:, 1:2] * per_step, own[:, 2:3] * per_step
    magnitude = jnp.sqrt(along_x * along_x + along_y * along_y + along_z * along_z)
    gain = jnp.zeros((half, width), F32)
    for b in range(basis_count):
        offset_k = (magnitude - 3.0 * b) * (1.0 / 3.0)
        gain = gain + jnp.exp(-(offset_k * offset_k)) * filter_ref[b : b + 1, :]
    gain_ref[...] = gain


def wave_tables(core, wavevectors, wave_filter, size, payload):
    wave_count, width = wavevectors.shape[1], wave_filter.shape[1]
    vmem = pl.BlockSpec(memory_space=pltpu.VMEM)
    return pl.pallas_call(
        functools.partial(wave_kernel, size),
        out_shape=(
            jax.ShapeDtypeStruct((COORD_ROWS, wave_count), BF16),
            jax.ShapeDtypeStruct((wave_count, COORD_ROWS), BF16),
            jax.ShapeDtypeStruct((wave_count, COORD_ROWS), BF16),
            jax.ShapeDtypeStruct((wave_count // 2, width), F32),
            jax.ShapeDtypeStruct(payload.shape, payload.dtype),
        ),
        in_specs=[pl.BlockSpec(memory_space=pltpu.SMEM)] + [pl.BlockSpec(memory_space=pltpu.HBM)] * 2
        + [vmem],
        out_specs=(vmem,) * 5,
        scratch_shapes=[
            pltpu.VMEM(wavevectors.shape, jnp.int32),
            pltpu.VMEM(wave_filter.shape, F32),
            pltpu.VMEM((COORD_ROWS, wave_count), F32),
            pltpu.SemaphoreType.DMA((2,)),
        ],
        compiler_params=PARAMS,
        name="waves",
    )(core, in_hbm(wavevectors), in_hbm(wave_filter), payload)


def structure_kernel(chunk_count, atoms, scale, parts, *refs):
    chunks, refs = refs[:chunk_count], refs[chunk_count:]
    main_ref, tail_ref, _, refs = refs[0], refs[1], refs[2], refs[3:]
    count = len(parts)
    sums, outs, refs = refs[:count], refs[count : 2 * count], refs[2 * count :]
    phases, tables, stack_ref = refs[:count], refs[count : 2 * count], refs[2 * count]
    half = main_ref.shape[0] // 2
    width = chunks[0].shape[1]
    tail = atoms - width
    depth = stack_ref.shape[0]
    split = chunk_count * width
    step = 32
    for l, chunk in enumerate(chunks):
        stack_ref[l * width : (l + 1) * width, :] = chunk[0:width, :]
        at = split + l * tail
        stack_ref[at : at + tail, :] = chunk[width:atoms, :]
    used = chunk_count * atoms
    if used < depth:
        stack_ref[used:depth, :] = jnp.zeros((depth - used, width), BF16)
    rows = tails_side_by_side(
        [chunk[atoms : atoms + COORD_ROWS, :].astype(F32) for chunk in chunks], depth - split, tail
    )
    for part, sum_ref, out_ref, phase_ref, table_ref in zip(parts, sums, outs, phases, tables):
        waves = slice(part * half, (part + 1) * half)
        for l, chunk in enumerate(chunks):
            phase_ref[:, l * width : (l + 1) * width] = jnp.dot(
                main_ref[waves], chunk[atoms : atoms + COORD_ROWS, :], preferred_element_type=F32
            )
        phase_ref[:, split:depth] = jnp.dot(
            tail_ref[waves], rows.astype(BF16), preferred_element_type=F32
        )
        for first_lane in range(0, depth, width):
            here = slice(first_lane, min(first_lane + width, depth))
            for row in range(0, half, step):
                cosine, sine = turn_cos_sin(phase_ref[row : row + step, here], scale)
                table_ref[row : row + step, here] = cosine.astype(BF16)
                table_ref[half + row : half + row + step, here] = sine.astype(BF16)
        total = jnp.dot(table_ref[...], stack_ref[...], preferred_element_type=F32)
        out_ref[...] = (total + sum_ref[...]).astype(out_ref.dtype)


def add_structure(chunks, parts, main_waves, tail_waves, token, sums, atoms, scale, kept_as=F32):
    count = len(chunks)
    width = chunks[0].shape[1]
    half = main_waves.shape[0] // 2
    depth = count * width + pad_up(count * (atoms - width), LANES)
    vmem = pl.BlockSpec(memory_space=pltpu.VMEM)
    return pl.pallas_call(
        functools.partial(structure_kernel, count, atoms, scale, parts),
        in_specs=[vmem] * (count + 2) + [pl.BlockSpec(memory_space=pl.ANY)] + [vmem] * len(parts),
        out_specs=[vmem] * len(parts),
        out_shape=[jax.ShapeDtypeStruct((2 * half, width), kept_as)] * len(parts),
        scratch_shapes=[pltpu.VMEM((half, depth), F32)] * len(parts)
        + [pltpu.VMEM((2 * half, depth), BF16)] * len(parts)
        + [pltpu.VMEM((depth, width), BF16)],
        compiler_params=PARAMS,
        cost_estimate=cost(12 * half * len(parts) * depth * width),
        name="structure",
    )(*chunks, main_waves, tail_waves, token, *sums)


def own_kernel(scale, cols_ref, waves_ref, payload_ref, table_ref, mine_ref, other_ref, phase_ref):
    waves = waves_ref.shape[1]
    half = waves // 2
    atoms = cols_ref.shape[0]
    phase_ref[...] = jnp.dot(
        cols_ref[...].astype(BF16), waves_ref[...], preferred_element_type=F32
    )
    step = 16
    for part, out_ref in enumerate((mine_ref, other_ref)):
        at = part * waves
        for row in range(0, atoms, step):
            cosine, sine = turn_cos_sin(
                phase_ref[row : row + step, part * half : (part + 1) * half], scale
            )
            table_ref[row : row + step, at : at + half] = cosine.astype(BF16)
            table_ref[row : row + step, at + half : at + waves] = sine.astype(BF16)
        out_ref[...] = lax.dot_general(
            table_ref[:, at : at + waves],
            payload_ref[0:atoms, :],
            (((0,), (0,)), ((), ())),
            preferred_element_type=F32,
        )


def own_layer(own_cols, wave_rows, payload, scale):
    atoms, waves = own_cols.shape[0], wave_rows.shape[1]
    width = payload.shape[1]
    return pl.pallas_call(
        functools.partial(own_kernel, scale),
        out_shape=(
            jax.ShapeDtypeStruct((atoms, 2 * waves), BF16),
            jax.ShapeDtypeStruct((waves, width), F32),
            jax.ShapeDtypeStruct((waves, width), F32),
        ),
        scratch_shapes=[pltpu.VMEM((atoms, waves), F32)],
        compiler_params=PARAMS,
        cost_estimate=cost(4 * atoms * waves * width),
        name="own_layer",
    )(own_cols, wave_rows, payload)


def short_kernel(cells, slots, basis_count, signs, holds_own, last, scale, *refs):
    count = len(signs)
    side_ref, refs = refs[0], refs[1:]
    chunks, refs = refs[:count], refs[count:]
    cols_ref, radial_ref, refs = refs[0], refs[1], refs[2:]
    if last:
        before_ref, features_ref, refs = refs[0], refs[1], refs[2:]
    out_ref, near_ref, weight_ref, mixed_ref = refs
    atoms = cells * slots
    width = chunks[0].shape[1]
    tail = atoms - width
    near = near_ref.shape[0]
    tail_width = near - count * width
    side = side_ref[0].astype(F32)
    shifts = [sign * side for sign in signs]
    mains, tails = [], []
    tail_lane = lax.broadcasted_iota(jnp.int32, (1, tail_width), 1)
    shift_row = jnp.zeros((1, tail_width), F32)
    for l, chunk in enumerate(chunks):
        near_ref[l * width : (l + 1) * width, :] = chunk[0:width, :]
        at = count * width + l * tail
        near_ref[at : at + tail, :] = chunk[width:atoms, :]
        rows = chunk[atoms : atoms + COORD_ROWS, :].astype(F32)
        mains.append((rows[0:1], rows[1:2], rows[3:4], rows[4:5], rows[5:6] + shifts[l]))
        tails.append(rows)
        here = (tail_lane >= l * tail) & (tail_lane < (l + 1) * tail)
        shift_row = jnp.where(here, shifts[l], shift_row)
    used = count * (width + tail)
    if used < near:
        near_ref[used:near, :] = jnp.zeros((near - used, width), BF16)
    joined = tails_side_by_side(tails, tail_width, tail)
    mains.append(
        (joined[8:9], joined[9:10], joined[11:12], joined[12:13], joined[13:14] + shift_row)
    )
    cell_x, cell_y, off_x, off_y, off_z = (
        jnp.concatenate([part[k] for part in mains], axis=1) for k in range(5)
    )
    lane = lax.broadcasted_iota(jnp.int32, (1, near), 1)
    own_index = jnp.where(
        lane < width,
        lane,
        jnp.where(
            (lane >= count * width) & (lane < count * width + tail),
            lane - (count - 1) * width,
            near,
        ),
    )

    def wrapped(delta):
        return jnp.where(
            delta >= GRID - 1.0, delta - GRID, jnp.where(delta < -1.0, delta + GRID, delta)
        )

    step = 16
    sharp = basis_count / CUTOFF
    for cell in range(cells):
        row_x = wrapped(cell_x - float(cell // GRID)) + off_x
        row_y = wrapped(cell_y - float(cell % GRID)) + off_y
        for row in range(cell * slots, (cell + 1) * slots, step):
            own = cols_ref[row : row + step, :]
            delta_x = row_x - own[:, 3:4]
            delta_y = row_y - own[:, 4:5]
            delta_z = off_z - own[:, 5:6]
            square = delta_x * delta_x + delta_y * delta_y + delta_z * delta_z
            root = horner(HALF_COSINE, square * (1.0 / (CUTOFF * CUTOFF)))
            counted = square < CUTOFF * CUTOFF
            if holds_own:
                own_row = row + lax.broadcasted_iota(jnp.int32, (step, 1), 0)
                counted = counted & (own_index != own_row)
            smooth = jnp.where(counted, root * root, 0.0)
            scaled = jnp.sqrt(square) * sharp - 0.5
            weight = jnp.exp(-(scaled * scaled)) * smooth
            growth = jnp.exp(2.0 * scaled)
            for basis in range(basis_count):
                if basis:
                    weight = weight * (growth * math.exp(1.0 - 2.0 * basis))
                weight_ref[basis * atoms + row : basis * atoms + row + step, :] = weight.astype(BF16)
    for basis in range(basis_count):
        mixed_ref[:, basis * width : (basis + 1) * width] = jnp.dot(
            weight_ref[basis * atoms : (basis + 1) * atoms, :],
            near_ref[...],
            preferred_element_type=F32,
        ).astype(BF16)
    total = jnp.dot(mixed_ref[...], radial_ref[...], preferred_element_type=F32)
    if last:
        total = (total + before_ref[...]) * scale + features_ref[0:atoms, :].astype(F32)
    out_ref[...] = total


def short_range(side, chunks, signs, own_cols, radial_flat, slots, basis_count, before=None):
    atoms = own_cols.shape[0]
    count = len(chunks)
    width = chunks[0].shape[1]
    near = count * width + pad_up(count * (atoms - width), LANES)
    last = before is not None
    more = before if last else ()
    vmem = pl.BlockSpec(memory_space=pltpu.VMEM)
    scale = 1.0 / math.sqrt(slots)
    return pl.pallas_call(
        functools.partial(
            short_kernel, atoms // slots, slots, basis_count, signs, not last, last, scale
        ),
        out_shape=jax.ShapeDtypeStruct((atoms, width), F32),
        in_specs=[pl.BlockSpec(memory_space=pltpu.SMEM)] + [vmem] * (count + 2 + len(more)),
        out_specs=vmem,
        scratch_shapes=[
            pltpu.VMEM((near, width), BF16),
            pltpu.VMEM((basis_count * atoms, near), BF16),
            pltpu.VMEM((atoms, basis_count * width), BF16),
        ],
        compiler_params=PARAMS,
        cost_estimate=cost(10 * basis_count * atoms * near * width),
        name="short_range",
    )(side, *chunks, own_cols, radial_flat, *more)


def filter_kernel(mine_ref, other_ref, charge_ref, gain_ref, out_ref):
    half = gain_ref.shape[0]
    total = mine_ref[...] + other_ref[...].astype(F32)
    structure = jnp.dot(total.astype(BF16), charge_ref[...], preferred_element_type=F32)
    gain = gain_ref[...]
    out_ref[0:half] = (structure[0:half] * gain).astype(BF16)
    out_ref[half:] = (structure[half:] * gain).astype(BF16)


def filter_half(mine, other, charge_weight, gain):
    return pl.pallas_call(
        filter_kernel,
        out_shape=jax.ShapeDtypeStruct(mine.shape, BF16),
        compiler_params=PARAMS,
        name="filter",
    )(mine, other, charge_weight, gain)


def inverse_kernel(scale, table_ref, factor_ref, base_ref, out_ref):
    out_ref[...] = base_ref[...] + scale * jnp.dot(
        table_ref[...], factor_ref[...], preferred_element_type=F32
    )


def finish_kernel(scale, slots, cols_ref, table_ref, factor_ref, base_ref, out_ref):
    total = base_ref[...] + scale * jnp.dot(
        table_ref[...], factor_ref[...], preferred_element_type=F32
    )
    total = jnp.where(cols_ref[:, 6:7] > 0.5, total, 0.0)
    for cell in range(total.shape[0] // slots):
        out_ref[cell] = total[cell * slots : (cell + 1) * slots].astype(BF16)


def local(atom_features, offsets, counts, radial_weight, charge_weight, wave_filter, wavevectors):
    cells, slots, width = atom_features.shape
    atoms = cells * slots
    basis_count = radial_weight.shape[0]
    wave_count = wavevectors.shape[1]
    size = lax.axis_size("space")
    layer = lax.axis_index("space")
    cores = 2 if size % 2 == 0 else 1
    near_y = 2 if (size // cores) % 2 == 0 else 1
    deep = size // (cores * near_y)
    core = layer % cores
    layer_scalar = layer.astype(jnp.int32).reshape(1)
    core_scalar = core.astype(jnp.int32).reshape(1)
    payload, own_cols = prepare(layer_scalar, counts, atom_features, offsets)

    def swap(value, mask):
        return lax.ppermute(value, "space", [(i, i ^ mask) for i in range(size)])

    rows_main, main_waves, tail_waves, gain, second = wave_tables(
        core_scalar, wavevectors, wave_filter, size, payload
    )
    scale = 1.0 / (GRID * size)
    table, *sums = own_layer(own_cols, rows_main, second, scale)
    side = 1 - 2 * core_scalar
    radial_flat = radial_weight.reshape(basis_count * width, width)

    stride = cores * near_y
    near_keys = [k for k in range(1, deep) if k == 1]
    far_keys = [k for k in range(deep - 1, 2, -1)]
    last_keys = [k for k in range(1, deep) if k == 2]
    along = {k: swap(payload, k * stride) for k in far_keys + last_keys}
    along.update({k: swap(payload, k * stride) for k in near_keys})
    beside = swap(payload, cores)
    pair = swap(payload, 1)

    def structure(chunks, parts, token, sums, kept_as=F32):
        groups = [chunks[i : i + 4] for i in range(0, len(chunks), 4)]
        for index, group in enumerate(groups):
            kind = kept_as if index == len(groups) - 1 else F32
            sums = add_structure(
                group, parts, main_waves, tail_waves, token, sums, atoms, scale, kind
            )
        return sums

    def after(value, token):
        return lax.optimization_barrier((value, token))[0]

    both = (0, 1)
    across = {k: swap(after(along[k], table), cores) for k in near_keys}
    sums = structure([beside] + [along[k] for k in near_keys], both, side, sums)
    first = dict(across)
    for k in far_keys:
        across[k] = swap(after(along[k], (sums[1], first)), cores)
    short = short_range(side, (second, pair), (0.0, 1.0), own_cols, radial_flat, slots, basis_count)
    for k in last_keys:
        across[k] = swap(after(along[k], short), cores)

    z = layer // stride
    y = (layer // cores) % near_y
    step_z = jnp.where(core == 0, 1, deep - 1)
    wanted = z ^ ((z + step_z) % deep)
    crossing = beside
    for k in across:
        if k & (k + 1) == 0:
            take = (wanted == k) & (y == jnp.where(core == 0, near_y - 1, 0))
            crossing = jnp.where(take, across[k], crossing)
    far = swap(crossing, 1)
    sums = structure(
        [along[k] for k in far_keys] + [across[k] for k in near_keys] + [along[k] for k in last_keys]
        + [across[k] for k in far_keys],
        both, short, sums,
    )
    base = short_range(
        side, (far,), (-1.0,), own_cols, radial_flat, slots, basis_count, (short, second)
    )
    final = [across[k] for k in last_keys]
    (send,) = structure(final, (1,), base, sums[1:], BF16)
    (mine,) = structure(final, (0,), send, sums[:1])
    factors = filter_half(mine, swap(send, 1), charge_weight, gain)
    other_factors = swap(factors, 1)

    recip_scale = 1.0 / math.sqrt(atoms * size * wave_count)
    vmem = pl.BlockSpec(memory_space=pltpu.VMEM)
    base = pl.pallas_call(
        functools.partial(inverse_kernel, recip_scale),
        grid=(1,),
        in_specs=[
            pl.BlockSpec((atoms, wave_count), lambda i: (0, 0)),
            pl.BlockSpec((wave_count, width), lambda i: (0, 0)),
            pl.BlockSpec((atoms, width), lambda i: (0, 0)),
        ],
        out_specs=pl.BlockSpec((atoms, width), lambda i: (0, 0)),
        out_shape=jax.ShapeDtypeStruct((atoms, width), F32),
        compiler_params=PARAMS,
        name="inverse",
    )(table, factors, base)
    return pl.pallas_call(
        functools.partial(finish_kernel, recip_scale, slots),
        grid=(1,),
        in_specs=[
            pl.BlockSpec((atoms, COORD_ROWS), lambda i: (0, 0)),
            pl.BlockSpec((atoms, wave_count), lambda i: (0, 1)),
            pl.BlockSpec((wave_count, width), lambda i: (0, 0)),
            pl.BlockSpec((atoms, width), lambda i: (0, 0)),
        ],
        out_specs=pl.BlockSpec((cells, slots, width), lambda i: (0, 0, 0)),
        out_shape=jax.ShapeDtypeStruct((cells, slots, width), BF16),
        compiler_params=PARAMS,
        name="finish",
    )(own_cols, table, other_factors, base)


def solution(mesh):
    in_specs = (
        P(("groups", "space"), None, None),
        P(("groups", "space"), None, None),
        P(("groups", "space")),
        P(),
        P(),
        P(),
        P(),
    )
    out_specs = P(("groups", "space"), None, None)
    return jax.shard_map(local, mesh=mesh, in_specs=in_specs, out_specs=out_specs, check_vma=False)
```

time: 51.6 us -> 37.5 us (0.73)
  the two profiles are of different devices: /device:TPU:0 before, /device:TPU:11 now
where the time goes in v2:
time: 37.5 us; the launch traced here: 37.2 us
  Pallas kernels  18.6 us (50%)
  starting transfers between devices  13 us (35%)
  waiting for transfers between devices  5.44 us (15%)
    ppermute x11, starting transfers between devices, swap(): return lax.ppermute(value, 'space', [(i, i ^ mask) for i in range(size)])  13 us
    pallas_call x4, Pallas kernels, add_structure(): pl.pallas_call(functools.partial(structure_kernel, count, atoms, scale, p...  9.58 us
    ppermute x11, waiting for transfers between devices, swap(): return lax.ppermute(value, 'space', [(i, i ^ mask) for i in range(size)])  5.44 us
    pallas_call x2, Pallas kernels, short_range(): pl.pallas_call(functools.partial(short_kernel, atoms // slots, slots, bas...  3.06 us
    pallas_call x1, Pallas kernels, own_layer(): pl.pallas_call(functools.partial(own_kernel, scale), out_shape=(jax.Shape...  1.71 us
    pallas_call x1, Pallas kernels, wave_tables(): pl.pallas_call(functools.partial(wave_kernel, size), out_shape=(jax.Shape...  1.61 us
    pallas_call x1, Pallas kernels, prepare(): pl.pallas_call(prepare_kernel, out_shape=(jax.ShapeDtypeStruct((atoms + C...  1.04 us
    pallas_call x1, Pallas kernels, local(): pl.pallas_call(functools.partial(finish_kernel, recip_scale, slots), grid...  0.99 us
  transfers between devices with their start and end apart: 11, of which 5 were waited for; matrix products, arithmetic and copies ran while one was open for 0% of the time, Pallas kernels for 41%

profile of v2, /device:TPU:11, one launch (start us, length us, event | category | flops | bytes accessed | tf_op | source)
XLA Modules:
  0.0 37.2 jit_solution(3234067305325642931)
XLA Ops:
  0.0 1.0 %prepare.1 = (bf16[304,256]{1,0:T(8,128)(2,1)S(1)}, f32[288,16]{1,0:T(8,128)S(1)}) custom-call(s32[1]{0:T(128)} %bitcast.layer_ref, s32[9]{0:T(128)} %counts_any.1, bf16[9,32,256]{2,1,0:T(8,128)(2,1)} %features_any.1, bf16[9,3,32]{2,1,0:T(4,128)(2,1)} %offsets_any.1), custom_call_target="tpu_custom_call" | custom-call | tf_op jit(solution)/shard_map/prepare/pallas_call | solution.py:118
  1.3 1.2 %collective-permute-start.4 = (bf16[304,256]{1,0:T(8,128)(2,1)S(1)}, bf16[304,256]{1,0:T(8,128)(2,1)S(1)}, u32[]{:S(2)}, u32[]{:S(2)}) collective-permute-start(bf16[304,256]{1,0:T(8,128)(2,1)S(1)} %get-tuple-element.23.payload_ref), channel_id=1, source_target_pairs={{0,2},{1,3},{2,0},{3,1},{4,6},{5,7},{6,4},{7,5},{8,10},{9,11},{10,... | collective-permute-start | bytes 466952 | tf_op jit(solution)/shard_map/ppermute | solution.py:472
  2.5 2.4 %collective-permute-start.3 = (bf16[304,256]{1,0:T(8,128)(2,1)S(1)}, bf16[304,256]{1,0:T(8,128)(2,1)S(1)}, u32[]{:S(2)}, u32[]{:S(2)}) collective-permute-start(bf16[304,256]{1,0:T(8,128)(2,1)S(1)} %get-tuple-element.23.payload_ref), channel_id=1, source_target_pairs={{0,12},{1,13},{2,14},{3,15},{4,8},{5,9},{6,10},{7,11},{8,4},{9,5},... | collective-permute-start | bytes 466952 | tf_op jit(solution)/shard_map/ppermute | solution.py:472
  5.0 1.5 %collective-permute-start.1 = (bf16[304,256]{1,0:T(8,128)(2,1)S(1)}, bf16[304,256]{1,0:T(8,128)(2,1)S(1)}, u32[]{:S(2)}, u32[]{:S(2)}) collective-permute-start(bf16[304,256]{1,0:T(8,128)(2,1)S(1)} %get-tuple-element.23.payload_ref), channel_id=1, source_target_pairs={{0,1},{1,0},{2,3},{3,2},{4,5},{5,4},{6,7},{7,6},{8,9},{9,8},{10,11... | collective-permute-start | bytes 466952 | tf_op jit(solution)/shard_map/ppermute | solution.py:472
  6.5 1.0 %collective-permute-start = (bf16[304,256]{1,0:T(8,128)(2,1)S(1)}, bf16[304,256]{1,0:T(8,128)(2,1)S(1)}, u32[]{:S(2)}, u32[]{:S(2)}) collective-permute-start(bf16[304,256]{1,0:T(8,128)(2,1)S(1)} %get-tuple-element.23.payload_ref), channel_id=1, source_target_pairs={{0,8},{1,9},{2,10},{3,11},{4,12},{5,13},{6,14},{7,15},{8,0},{9,1},... | collective-permute-start | bytes 466952 | tf_op jit(solution)/shard_map/ppermute | solution.py:472
  7.4 1.6 %waves.1 = (bf16[16,1024]{1,0:T(8,128)(2,1)S(1)}, bf16[1024,16]{1,0:T(8,128)(2,1)S(1)}, bf16[1024,16]{1,0:T(8,128)(2,1)S(1)}, f32[512,256]{1,0:T(8,128)S(1)}, bf16[304,256]{1,0:T(8,128)(2,1)S(1)}) custom-call(s32[1]{0:T(128)} %bitcast.1.core_ref, s32[3,1024]{1,0:T(4,128)} %waves_any.1, f32[4,256]{1,0:T(4,128)} %filter_any.1, ...), custom_call_target="tpu_custom_call" | custom-call | tf_op jit(solution)/shard_map/waves/pallas_call | solution.py:182
  9.0 1.7 %own_layer.1 = (bf16[288,2048]{1,0:T(8,128)(2,1)S(1)}, f32[1024,256]{1,0:T(8,128)S(1)}, f32[1024,256]{1,0:T(8,128)S(1)}) custom-call(f32[288,16]{1,0:T(8,128)S(1)} %get-tuple-element.22.cols_ref.refs_3_.refs_2_, bf16[16,1024]{1,0:T(8,128)(2,1)S(1)} %get-tuple-element.24.waves_ref, bf16[304,256]{1,0:T(8,128)(2,1)S(1)} %get-tuple-element.25.payload_ref.refs_1_.refs_5_), custom_call_target="tpu_custom_call" | custom-call | flops 301989888 | bytes 301989 | tf_op jit(solution)/shard_map/own_layer/pallas_call | solution.py:293
  10.8 0.3 collective-permute-start.6
  11.1 2.6 %structure.4 = (f32[1024,256]{1,0:T(8,128)S(1)}, f32[1024,256]{1,0:T(8,128)S(1)}) custom-call(bf16[304,256]{1,0:T(8,128)(2,1)S(1)} %collective-permute-done.4.refs_0_, bf16[304,256]{1,0:T(8,128)(2,1)S(1)} %collective-permute-done.5.refs_1_, bf16[1024,16]{1,0:T(8,128)(2,1)S(1)} %get-tuple-element.28.refs_2_.refs_4_.refs_1_, ...), custom_call_target="tpu_custom_call" | custom-call | flops 2013265920 | bytes 2013265 | tf_op jit(solution)/shard_map/structure/pallas_call | solution.py:252
  13.7 1.3 %collective-permute-done.3.refs_0_ = bf16[304,256]{1,0:T(8,128)(2,1)S(1)} collective-permute-done((bf16[304,256]{1,0:T(8,128)(2,1)S(1)}, bf16[304,256]{1,0:T(8,128)(2,1)S(1)}, u32[]{:S(2)}, u32[]{:S(2)}) %collective-permute-start.3) | collective-permute-done | bytes 155680 | tf_op jit(solution)/shard_map/ppermute | solution.py:472
  14.9 1.2 %collective-permute-done.6.refs_1_ = bf16[304,256]{1,0:T(8,128)(2,1)S(1)} collective-permute-done((bf16[304,256]{1,0:T(8,128)(2,1)S(1)}, bf16[304,256]{1,0:T(8,128)(2,1)S(1)}, u32[]{:S(2)}, u32[]{:S(2)}) %collective-permute-start.6) | collective-permute-done | bytes 155680 | tf_op jit(solution)/shard_map/ppermute | solution.py:472
  16.4 1.8 %short_range.2.refs_4_.refs_6_ = f32[288,256]{1,0:T(8,128)S(1)} custom-call(s32[1]{0:T(128)S(6)} %sub.10.refs_0_.refs_4_, bf16[304,256]{1,0:T(8,128)(2,1)S(1)} %get-tuple-element.25.payload_ref.refs_1_.refs_5_, bf16[304,256]{1,0:T(8,128)(2,1)S(1)} %collective-permute-done.1.refs_2_, f32[288,16]{1,0:T(8,128)S(1)} %get-tuple-element.22.cols_ref.refs_3_.refs_2_, ...), custom_call_target="tpu_custom_call" | custom-call | flops 1887436800 | bytes 1887436 | tf_op jit(solution)/shard_map/short_range/pallas_call | solution.py:405
  18.3 1.3 %collective-permute-start.2 = (bf16[304,256]{1,0:T(8,128)(2,1)S(1)}, bf16[304,256]{1,0:T(8,128)(2,1)S(1)}, u32[]{:S(2)}, u32[]{:S(2)}) collective-permute-start(bf16[304,256]{1,0:T(8,128)(2,1)S(1)} %collective-permute-done.refs_2_), channel_id=1, source_target_pairs={{0,2},{1,3},{2,0},{3,1},{4,6},{5,7},{6,4},{7,5},{8,10},{9,11},{10,... | collective-permute-start | bytes 466952 | tf_op jit(solution)/shard_map/ppermute | solution.py:472
  19.6 0.7 %collective-permute-done.7.refs_3_ = bf16[304,256]{1,0:T(8,128)(2,1)S(1)} collective-permute-done((bf16[304,256]{1,0:T(8,128)(2,1)S(1)}, bf16[304,256]{1,0:T(8,128)(2,1)S(1)}, u32[]{:S(2)}, u32[]{:S(2)}) %collective-permute-start.7) | collective-permute-done | bytes 155680 | tf_op jit(solution)/shard_map/ppermute | solution.py:472
  20.3 4.5 %collective-permute-start.8 = (bf16[304,256]{1,0:T(8,128)(2,1)S(1)}, bf16[304,256]{1,0:T(8,128)(2,1)S(1)}, u32[]{:S(2)}, u32[]{:S(2)}) collective-permute-start(bf16[304,256]{1,0:T(8,128)(2,1)S(1)} %select_select_fusion), channel_id=1, source_target_pairs={{0,1},{1,0},{2,3},{3,2},{4,5},{5,4},{6,7},{7,6},{8,9},{9,8},{10,11... | collective-permute-start | bytes 466952 | tf_op jit(solution)/shard_map/ppermute | solution.py:472
  24.8 4.8 %structure.5 = (f32[1024,256]{1,0:T(8,128)S(1)}, f32[1024,256]{1,0:T(8,128)S(1)}) custom-call(bf16[304,256]{1,0:T(8,128)(2,1)S(1)} %collective-permute-done.3.refs_0_, bf16[304,256]{1,0:T(8,128)(2,1)S(1)} %collective-permute-done.6.refs_1_, bf16[304,256]{1,0:T(8,128)(2,1)S(1)} %collective-permute-done.refs_2_, ...), custom_call_target="tpu_custom_call" | custom-call | flops 3623878656 | bytes 3623878 | tf_op jit(solution)/shard_map/structure/pallas_call | solution.py:252
  29.6 1.2 %short_range.3.refs_3_.base_ref = f32[288,256]{1,0:T(8,128)S(1)} custom-call(s32[1]{0:T(128)S(6)} %sub.10.refs_0_.refs_4_, bf16[304,256]{1,0:T(8,128)(2,1)S(1)} %collective-permute-done.8.refs_1_, f32[288,16]{1,0:T(8,128)S(1)} %get-tuple-element.22.cols_ref.refs_3_.refs_2_, bf16[1024,256]{1,0:T(8,128)(2,1)S(1)} %bitcast.4, ...), custom_call_target="tpu_custom_call" | custom-call | flops 1132462080 | bytes 1132462 | tf_op jit(solution)/shard_map/short_range/pallas_call | solution.py:405
  30.9 1.1 %structure.6.refs_3_ = bf16[1024,256]{1,0:T(8,128)(2,1)S(1)} custom-call(bf16[304,256]{1,0:T(8,128)(2,1)S(1)} %collective-permute-done.2.refs_0_, bf16[1024,16]{1,0:T(8,128)(2,1)S(1)} %get-tuple-element.28.refs_2_.refs_4_.refs_1_, bf16[1024,16]{1,0:T(8,128)(2,1)S(1)} %get-tuple-element.29.refs_3_.refs_5_.refs_2_, ...), custom_call_target="tpu_custom_call" | custom-call | flops 603979776 | bytes 603979 | tf_op jit(solution)/shard_map/structure/pallas_call | solution.py:252
  32.1 1.1 %structure.7.mine_ref = f32[1024,256]{1,0:T(8,128)S(1)} custom-call(bf16[304,256]{1,0:T(8,128)(2,1)S(1)} %collective-permute-done.2.refs_0_, bf16[1024,16]{1,0:T(8,128)(2,1)S(1)} %get-tuple-element.28.refs_2_.refs_4_.refs_1_, bf16[1024,16]{1,0:T(8,128)(2,1)S(1)} %get-tuple-element.29.refs_3_.refs_5_.refs_2_, bf16[1024,256]{1,0:T(8,128)(2,1)S(1)} %structure.6.refs_3_, ...), custom_call_target="tpu_custom_call" | custom-call | flops 603979776 | bytes 603979 | tf_op jit(solution)/shard_map/structure/pallas_call | solution.py:252
  33.2 0.8 %collective-permute-done.9.other_ref = bf16[1024,256]{1,0:T(8,128)(2,1)S(1)} collective-permute-done((bf16[1024,256]{1,0:T(8,128)(2,1)S(1)}, bf16[1024,256]{1,0:T(8,128)(2,1)S(1)}, u32[]{:S(2)}, u32[]{:S(2)}) %collective-permute-start.9) | collective-permute-done | bytes 524320 | tf_op jit(solution)/shard_map/ppermute | solution.py:472
  33.9 0.3 filter.1.factor_ref
  34.4 0.3 inverse.1.base_ref
  34.8 1.5 %collective-permute-done.10.factor_ref = bf16[1024,256]{1,0:T(8,128)(2,1)S(1)} collective-permute-done((bf16[1024,256]{1,0:T(8,128)(2,1)S(1)}, bf16[1024,256]{1,0:T(8,128)(2,1)S(1)}, u32[]{:S(2)}, u32[]{:S(2)}) %collective-permute-start.10) | collective-permute-done | bytes 524320 | tf_op jit(solution)/shard_map/ppermute | solution.py:472
  36.2 1.0 %finish.1 = bf16[9,32,256]{2,1,0:T(8,128)(2,1)} custom-call(f32[288,16]{1,0:T(8,128)S(1)} %get-tuple-element.22.cols_ref.refs_3_.refs_2_, bf16[288,2048]{1,0:T(8,128)(2,1)S(1)} %get-tuple-element.26.table_ref, bf16[1024,256]{1,0:T(8,128)(2,1)S(1)} %collective-permute-done.10.factor_ref, f32[288,256]{1,0:T(8,128)S(1)} %inverse.1.base_ref), custom_call_target="tpu_custom_call" | custom-call | tf_op jit(solution)/shard_map/finish/pallas_call | solution.py:552
  (15 shorter events, 0.8 us)
Async XLA Ops:
  1.1 9.7 %collective-permute-start.5 = (bf16[304,256]{1,0:T(8,128)(2,1)S(1)}, bf16[304,256]{1,0:T(8,128)(2,1)S(1)}, u32[]{:S(2)}, u32[]{:S(2)}) collective-permute-start(bf16[304,256]{1,0:T(8,128)(2,1)S(1)} %get-tuple-element.23.payload_ref), channel_id=1, source_target_pairs={{0,4},{1,5},{2,6},{3,7},{4,0},{5,1},{6,2},{7,3},{8,12},{9,13},{10,... | collective-permute-start | bytes 466952 | tf_op jit(solution)/shard_map/ppermute | solution.py:472
  1.3 9.8 %collective-permute-start.4 = (bf16[304,256]{1,0:T(8,128)(2,1)S(1)}, bf16[304,256]{1,0:T(8,128)(2,1)S(1)}, u32[]{:S(2)}, u32[]{:S(2)}) collective-permute-start(bf16[304,256]{1,0:T(8,128)(2,1)S(1)} %get-tuple-element.23.payload_ref), channel_id=1, source_target_pairs={{0,2},{1,3},{2,0},{3,1},{4,6},{5,7},{6,4},{7,5},{8,10},{9,11},{10,... | collective-permute-start | bytes 466952 | tf_op jit(solution)/shard_map/ppermute | solution.py:472
  2.5 12.4 %collective-permute-start.3 = (bf16[304,256]{1,0:T(8,128)(2,1)S(1)}, bf16[304,256]{1,0:T(8,128)(2,1)S(1)}, u32[]{:S(2)}, u32[]{:S(2)}) collective-permute-start(bf16[304,256]{1,0:T(8,128)(2,1)S(1)} %get-tuple-element.23.payload_ref), channel_id=1, source_target_pairs={{0,12},{1,13},{2,14},{3,15},{4,8},{5,9},{6,10},{7,11},{8,4},{9,5},... | collective-permute-start | bytes 466952 | tf_op jit(solution)/shard_map/ppermute | solution.py:472
  5.0 11.5 %collective-permute-start.1 = (bf16[304,256]{1,0:T(8,128)(2,1)S(1)}, bf16[304,256]{1,0:T(8,128)(2,1)S(1)}, u32[]{:S(2)}, u32[]{:S(2)}) collective-permute-start(bf16[304,256]{1,0:T(8,128)(2,1)S(1)} %get-tuple-element.23.payload_ref), channel_id=1, source_target_pairs={{0,1},{1,0},{2,3},{3,2},{4,5},{5,4},{6,7},{7,6},{8,9},{9,8},{10,11... | collective-permute-start | bytes 466952 | tf_op jit(solution)/shard_map/ppermute | solution.py:472
  6.5 11.8 %collective-permute-start = (bf16[304,256]{1,0:T(8,128)(2,1)S(1)}, bf16[304,256]{1,0:T(8,128)(2,1)S(1)}, u32[]{:S(2)}, u32[]{:S(2)}) collective-permute-start(bf16[304,256]{1,0:T(8,128)(2,1)S(1)} %get-tuple-element.23.payload_ref), channel_id=1, source_target_pairs={{0,8},{1,9},{2,10},{3,11},{4,12},{5,13},{6,14},{7,15},{8,0},{9,1},... | collective-permute-start | bytes 466952 | tf_op jit(solution)/shard_map/ppermute | solution.py:472
  10.8 5.4 %collective-permute-start.6 = (bf16[304,256]{1,0:T(8,128)(2,1)S(1)}, bf16[304,256]{1,0:T(8,128)(2,1)S(1)}, u32[]{:S(2)}, u32[]{:S(2)}) collective-permute-start(bf16[304,256]{1,0:T(8,128)(2,1)S(1)} %collective-permute-done.5.refs_1_), channel_id=1, source_target_pairs={{0,2},{1,3},{2,0},{3,1},{4,6},{5,7},{6,4},{7,5},{8,10},{9,11},{10,... | collective-permute-start | bytes 466952 | tf_op jit(solution)/shard_map/ppermute | solution.py:472
  11.1 5.3 %copy-start.1 = (bf16[4,256,256]{2,1,0:T(8,128)(2,1)S(1)}, bf16[4,256,256]{2,1,0:T(8,128)(2,1)}, u32[]{:S(2)}) copy-start(bf16[4,256,256]{2,1,0:T(8,128)(2,1)} %param.10) | copy-start | bytes 1572868
  16.2 4.1 %collective-permute-start.7 = (bf16[304,256]{1,0:T(8,128)(2,1)S(1)}, bf16[304,256]{1,0:T(8,128)(2,1)S(1)}, u32[]{:S(2)}, u32[]{:S(2)}) collective-permute-start(bf16[304,256]{1,0:T(8,128)(2,1)S(1)} %collective-permute-done.3.refs_0_), channel_id=1, source_target_pairs={{0,2},{1,3},{2,0},{3,1},{4,6},{5,7},{6,4},{7,5},{8,10},{9,11},{10,... | collective-permute-start | bytes 466952 | tf_op jit(solution)/shard_map/ppermute | solution.py:472
  18.3 12.6 %collective-permute-start.2 = (bf16[304,256]{1,0:T(8,128)(2,1)S(1)}, bf16[304,256]{1,0:T(8,128)(2,1)S(1)}, u32[]{:S(2)}, u32[]{:S(2)}) collective-permute-start(bf16[304,256]{1,0:T(8,128)(2,1)S(1)} %collective-permute-done.refs_2_), channel_id=1, source_target_pairs={{0,2},{1,3},{2,0},{3,1},{4,6},{5,7},{6,4},{7,5},{8,10},{9,11},{10,... | collective-permute-start | bytes 466952 | tf_op jit(solution)/shard_map/ppermute | solution.py:472
  20.3 9.3 %collective-permute-start.8 = (bf16[304,256]{1,0:T(8,128)(2,1)S(1)}, bf16[304,256]{1,0:T(8,128)(2,1)S(1)}, u32[]{:S(2)}, u32[]{:S(2)}) collective-permute-start(bf16[304,256]{1,0:T(8,128)(2,1)S(1)} %select_select_fusion), channel_id=1, source_target_pairs={{0,1},{1,0},{2,3},{3,2},{4,5},{5,4},{6,7},{7,6},{8,9},{9,8},{10,11... | collective-permute-start | bytes 466952 | tf_op jit(solution)/shard_map/ppermute | solution.py:472
  32.0 2.0 %collective-permute-start.9 = (bf16[1024,256]{1,0:T(8,128)(2,1)S(1)}, bf16[1024,256]{1,0:T(8,128)(2,1)S(1)}, u32[]{:S(2)}, u32[]{:S(2)}) collective-permute-start(bf16[1024,256]{1,0:T(8,128)(2,1)S(1)} %structure.6.refs_3_), channel_id=1, source_target_pairs={{0,1},{1,0},{2,3},{3,2},{4,5},{5,4},{6,7},{7,6},{8,9},{9,8},{10,11... | collective-permute-start | bytes 1572872 | tf_op jit(solution)/shard_map/ppermute | solution.py:472
  32.1 1.9 %copy-start = (bf16[256,256]{1,0:T(8,128)(2,1)S(1)}, bf16[256,256]{1,0:T(8,128)(2,1)}, u32[]{:S(2)}) copy-start(bf16[256,256]{1,0:T(8,128)(2,1)} %charge_ref.1) | copy-start | bytes 393220
  34.3 2.0 %collective-permute-start.10 = (bf16[1024,256]{1,0:T(8,128)(2,1)S(1)}, bf16[1024,256]{1,0:T(8,128)(2,1)S(1)}, u32[]{:S(2)}, u32[]{:S(2)}) collective-permute-start(bf16[1024,256]{1,0:T(8,128)(2,1)S(1)} %filter.1.factor_ref), channel_id=1, source_target_pairs={{0,1},{1,0},{2,3},{3,2},{4,5},{5,4},{6,7},{7,6},{8,9},{9,8},{10,11... | collective-permute-start | bytes 1572872 | tf_op jit(solution)/shard_map/ppermute | solution.py:472

commit v3 on v2

--- a/solution.py
+++ b/solution.py
@@ -14,8 +14,9 @@
 F32 = jnp.float32
 COORD_ROWS = 16
 LANES = 128
+TERMS = 3
 SINE = (4.44287959, -7.30781805, 3.59778873, -0.791238217)
-COSINE = (1.4142135, -6.97885099, 5.73946117, -1.88356299, 0.310698193)
+COSINE = (1.41420408, -6.97764206, 5.7152384, -1.72834866)
 HALF_COSINE = (0.999999953, -1.23369821, 0.253650745, -0.0208106275, 0.000858190619)
 PARAMS = pltpu.CompilerParams(vmem_limit_bytes=32 * 1024 * 1024)
 WIDE = pltpu.CompilerParams(vmem_limit_bytes=62 * 1024 * 1024)
@@ -28,8 +29,7 @@
     return total
 
 
-def turn_cos_sin(scaled, scale):
-    turns = scaled * scale
+def turn_cos_sin(turns):
     rest = turns - jnp.round(turns)
     square = rest * rest
     half_sine = horner(SINE, square) * rest
@@ -58,13 +58,20 @@
 
 
 def prepare_kernel(
-    layer_ref, counts_any, features_any, offsets_any, payload_ref, cols_ref,
+    layer_ref, counts_any, features_any, offsets_any, waves_any, filter_any,
+    payload_ref, cols_ref, waves_ref, filter_ref,
     counts_ref, features_ref, offsets_ref, rows_ref, sems,
 ):
     copies = [
         pltpu.make_async_copy(source, target, sems.at[i])
         for i, (source, target) in enumerate(
-            ((features_any, features_ref), (offsets_any, offsets_ref), (counts_any, counts_ref))
+            (
+                (features_any, features_ref),
+                (offsets_any, offsets_ref),
+                (counts_any, counts_ref),
+                (waves_any, waves_ref),
+                (filter_any, filter_ref),
+            )
         )
     ]
     for copy in copies:
@@ -75,7 +82,7 @@
     slot = lax.broadcasted_iota(jnp.int32, (slots, width), 0)
     lane = lax.broadcasted_iota(jnp.int32, (1, width), 1)
     main_cells = width // slots
-    for copy in copies[1:]:
+    for copy in copies[1:3]:
         copy.wait()
     within = [offsets_ref[cell].astype(F32) for cell in range(cells)]
     for first, parts in (
@@ -107,9 +114,11 @@
         payload_ref[cell * slots : (cell + 1) * slots, :] = jnp.where(
             slot < counts_ref[cell], rows, 0.0
         ).astype(BF16)
-
-
-def prepare(layer, counts, atom_features, offsets):
+    for copy in copies[3:]:
+        copy.wait()
+
+
+def prepare(layer, counts, atom_features, offsets, wavevectors, wave_filter):
     cells, slots, width = atom_features.shape
     atoms = cells * slots
     smem = pl.BlockSpec(memory_space=pltpu.SMEM)
@@ -120,93 +129,85 @@
         out_shape=(
             jax.ShapeDtypeStruct((atoms + COORD_ROWS, width), BF16),
             jax.ShapeDtypeStruct((atoms, COORD_ROWS), F32),
+            jax.ShapeDtypeStruct(wavevectors.shape, wavevectors.dtype),
+            jax.ShapeDtypeStruct(wave_filter.shape, wave_filter.dtype),
         ),
-        in_specs=[smem, anywhere, anywhere, anywhere],
-        out_specs=(vmem, vmem),
+        in_specs=[smem] + [anywhere] * 5,
+        out_specs=(vmem,) * 4,
         scratch_shapes=[
             pltpu.SMEM(counts.shape, jnp.int32),
             pltpu.VMEM(atom_features.shape, BF16),
             pltpu.VMEM(offsets.shape, BF16),
             pltpu.VMEM((COORD_ROWS, width), F32),
-            pltpu.SemaphoreType.DMA((3,)),
+            pltpu.SemaphoreType.DMA((5,)),
         ],
         compiler_params=PARAMS,
         name="prepare",
-    )(layer, *map(in_hbm, (counts, atom_features, offsets)))
+    )(layer, *map(in_hbm, (counts, atom_features, offsets, wavevectors, wave_filter)))
 
 
 def wave_kernel(
-    size, core_ref, waves_any, filter_any, payload_ref, rows_ref, main_ref, tail_ref, gain_ref, passed_ref,
-    waves_ref, filter_ref, all_ref, sems,
+    size, waves_ref, filter_ref, rows_ref, main_ref, tail_ref, gain_ref, all_ref
 ):
-    copies = (
-        pltpu.make_async_copy(waves_any, waves_ref, sems.at[0]),
-        pltpu.make_async_copy(filter_any, filter_ref, sems.at[1]),
-    )
-    for copy in copies:
-        copy.start()
-    passed_ref[...] = payload_ref[...]
-    for copy in copies:
-        copy.wait()
     wave_count = waves_ref.shape[1]
-    half = wave_count // 2
     basis_count, width = filter_ref.shape
-    core = core_ref[0]
     all_ref[...] = jnp.zeros(all_ref.shape, F32)
-    for place in range(2):
-        start = pl.multiple_of((core if place == 0 else 1 - core) * half, LANES)
-        taken = waves_ref[:, pl.ds(start, half)].astype(F32)
-        at = slice(place * half, (place + 1) * half)
-        for first in (0, 3):
-            all_ref[first : first + 2, at] = taken[0:2] * float(size)
-            all_ref[first + 2 : first + 3, at] = taken[2:3] * float(GRID)
-    rows = all_ref[...]
-    rows_ref[...] = rows.astype(BF16)
-    columns = rows.T
-    main_ref[...] = columns.astype(BF16)
-    tail_ref[...] = jnp.concatenate([rows[8:16], rows[0:8]], axis=0).T.astype(BF16)
-    own = columns[0:half]
-    per_step = 2.0 * math.pi / (GRID * size)
-    along_x, along_y, along_z = own[:, 0:1] * per_step, own[:, 1:2] * per_step, own[:, 2:3] * per_step
+    taken = waves_ref[...].astype(F32)
+    for first in (0, 3):
+        all_ref[first : first + 2, :] = taken[0:2] * (1.0 / GRID)
+        all_ref[first + 2 : first + 3, :] = taken[2:3] * (1.0 / size)
+    rest = all_ref[...]
+    own = rest[0:3] * (2.0 * math.pi)
+    terms = []
+    for term in range(TERMS):
+        rounded = rest.astype(BF16).astype(F32)
+        rows_ref[term * COORD_ROWS : (term + 1) * COORD_ROWS, :] = rounded.astype(BF16)
+        terms.append(rounded)
+        rest = rest - rounded
+    main_ref[...] = jnp.concatenate(terms, axis=0).T.astype(BF16)
+    tail_ref[...] = jnp.concatenate(
+        [rows for term in terms for rows in (term[8:16], term[0:8])], axis=0
+    ).T.astype(BF16)
+    along_x, along_y, along_z = own[0:1], own[1:2], own[2:3]
     magnitude = jnp.sqrt(along_x * along_x + along_y * along_y + along_z * along_z)
-    gain = jnp.zeros((half, width), F32)
-    for b in range(basis_count):
+    basis = []
+    for b in range(pad_up(basis_count, 8)):
         offset_k = (magnitude - 3.0 * b) * (1.0 / 3.0)
-        gain = gain + jnp.exp(-(offset_k * offset_k)) * filter_ref[b : b + 1, :]
+        basis.append(jnp.exp(-(offset_k * offset_k)))
+    columns = jnp.concatenate(basis, axis=0).T
+    gain = columns[:, 0:1] * filter_ref[0:1, :]
+    for b in range(1, basis_count):
+        gain = gain + columns[:, b : b + 1] * filter_ref[b : b + 1, :]
     gain_ref[...] = gain
 
 
-def wave_tables(core, wavevectors, wave_filter, size, payload):
+def wave_tables(wavevectors, wave_filter, size):
     wave_count, width = wavevectors.shape[1], wave_filter.shape[1]
     vmem = pl.BlockSpec(memory_space=pltpu.VMEM)
     return pl.pallas_call(
         functools.partial(wave_kernel, size),
         out_shape=(
-            jax.ShapeDtypeStruct((COORD_ROWS, wave_count), BF16),
-            jax.ShapeDtypeStruct((wave_count, COORD_ROWS), BF16),
-            jax.ShapeDtypeStruct((wave_count, COORD_ROWS), BF16),
-            jax.ShapeDtypeStruct((wave_count // 2, width), F32),
-            jax.ShapeDtypeStruct(payload.shape, payload.dtype),
+            jax.ShapeDtypeStruct((TERMS * COORD_ROWS, wave_count), BF16),
+            jax.ShapeDtypeStruct((wave_count, TERMS * COORD_ROWS), BF16),
+            jax.ShapeDtypeStruct((wave_count, TERMS * COORD_ROWS), BF16),
+            jax.ShapeDtypeStruct((wave_count, width), F32),
         ),
-        in_specs=[pl.BlockSpec(memory_space=pltpu.SMEM)] + [pl.BlockSpec(memory_space=pltpu.HBM)] * 2
-        + [vmem],
-        out_specs=(vmem,) * 5,
-        scratch_shapes=[
-            pltpu.VMEM(wavevectors.shape, jnp.int32),
-            pltpu.VMEM(wave_filter.shape, F32),
-            pltpu.VMEM((COORD_ROWS, wave_count), F32),
-            pltpu.SemaphoreType.DMA((2,)),
-        ],
+        in_specs=[vmem, vmem],
+        out_specs=(vmem,) * 4,
+        scratch_shapes=[pltpu.VMEM((COORD_ROWS, wave_count), F32)],
         compiler_params=PARAMS,
         name="waves",
-    )(core, in_hbm(wavevectors), in_hbm(wave_filter), payload)
-
-
-def structure_kernel(chunk_count, atoms, scale, parts, *refs):
+    )(wavevectors, wave_filter)
+
+
+def structure_kernel(chunk_count, atoms, parts, sent, *refs):
     chunks, refs = refs[:chunk_count], refs[chunk_count:]
     main_ref, tail_ref, _, refs = refs[0], refs[1], refs[2], refs[3:]
     count = len(parts)
     sums, outs, refs = refs[:count], refs[count : 2 * count], refs[2 * count :]
+    sent_ref = None
+    if sent:
+        sent_ref, refs = refs[0], refs[1:]
     phases, tables, stack_ref = refs[:count], refs[count : 2 * count], refs[2 * count]
     half = main_ref.shape[0] // 2
     width = chunks[0].shape[1]
@@ -227,33 +228,39 @@
     for part, sum_ref, out_ref, phase_ref, table_ref in zip(parts, sums, outs, phases, tables):
         waves = slice(part * half, (part + 1) * half)
         for l, chunk in enumerate(chunks):
+            places = jnp.concatenate([chunk[atoms : atoms + COORD_ROWS, :]] * TERMS, axis=0)
             phase_ref[:, l * width : (l + 1) * width] = jnp.dot(
-                main_ref[waves], chunk[atoms : atoms + COORD_ROWS, :], preferred_element_type=F32
+                main_ref[waves], places, preferred_element_type=F32
             )
         phase_ref[:, split:depth] = jnp.dot(
-            tail_ref[waves], rows.astype(BF16), preferred_element_type=F32
+            tail_ref[waves],
+            jnp.concatenate([rows.astype(BF16)] * TERMS, axis=0),
+            preferred_element_type=F32,
         )
         for first_lane in range(0, depth, width):
             here = slice(first_lane, min(first_lane + width, depth))
             for row in range(0, half, step):
-                cosine, sine = turn_cos_sin(phase_ref[row : row + step, here], scale)
+                cosine, sine = turn_cos_sin(phase_ref[row : row + step, here])
                 table_ref[row : row + step, here] = cosine.astype(BF16)
                 table_ref[half + row : half + row + step, here] = sine.astype(BF16)
-        total = jnp.dot(table_ref[...], stack_ref[...], preferred_element_type=F32)
-        out_ref[...] = (total + sum_ref[...]).astype(out_ref.dtype)
-
-
-def add_structure(chunks, parts, main_waves, tail_waves, token, sums, atoms, scale, kept_as=F32):
+        total = jnp.dot(table_ref[...], stack_ref[...], preferred_element_type=F32) + sum_ref[...]
+        out_ref[...] = total
+        if sent_ref is not None:
+            sent_ref[...] = total.astype(BF16)
+
+
+def add_structure(chunks, parts, main_waves, tail_waves, token, sums, atoms, sent=False):
     count = len(chunks)
     width = chunks[0].shape[1]
     half = main_waves.shape[0] // 2
     depth = count * width + pad_up(count * (atoms - width), LANES)
     vmem = pl.BlockSpec(memory_space=pltpu.VMEM)
     return pl.pallas_call(
-        functools.partial(structure_kernel, count, atoms, scale, parts),
+        functools.partial(structure_kernel, count, atoms, parts, sent),
         in_specs=[vmem] * (count + 2) + [pl.BlockSpec(memory_space=pl.ANY)] + [vmem] * len(parts),
-        out_specs=[vmem] * len(parts),
-        out_shape=[jax.ShapeDtypeStruct((2 * half, width), kept_as)] * len(parts),
+        out_specs=[vmem] * (len(parts) + sent),
+        out_shape=[jax.ShapeDtypeStruct((2 * half, width), F32)] * len(parts)
+        + [jax.ShapeDtypeStruct((2 * half, width), BF16)] * sent,
         scratch_shapes=[pltpu.VMEM((half, depth), F32)] * len(parts)
         + [pltpu.VMEM((2 * half, depth), BF16)] * len(parts)
         + [pltpu.VMEM((depth, width), BF16)],
@@ -263,19 +270,20 @@
     )(*chunks, main_waves, tail_waves, token, *sums)
 
 
-def own_kernel(scale, cols_ref, waves_ref, payload_ref, table_ref, mine_ref, other_ref, phase_ref):
+def own_kernel(cols_ref, waves_ref, payload_ref, table_ref, mine_ref, other_ref, phase_ref):
     waves = waves_ref.shape[1]
     half = waves // 2
     atoms = cols_ref.shape[0]
+    places = cols_ref[...].astype(BF16)
     phase_ref[...] = jnp.dot(
-        cols_ref[...].astype(BF16), waves_ref[...], preferred_element_type=F32
+        jnp.concatenate([places] * TERMS, axis=1), waves_ref[...], preferred_element_type=F32
     )
     step = 16
     for part, out_ref in enumerate((mine_ref, other_ref)):
         at = part * waves
         for row in range(0, atoms, step):
             cosine, sine = turn_cos_sin(
-                phase_ref[row : row + step, part * half : (part + 1) * half], scale
+                phase_ref[row : row + step, part * half : (part + 1) * half]
             )
             table_ref[row : row + step, at : at + half] = cosine.astype(BF16)
             table_ref[row : row + step, at + half : at + waves] = sine.astype(BF16)
@@ -287,11 +295,11 @@
         )
 
 
-def own_layer(own_cols, wave_rows, payload, scale):
+def own_layer(own_cols, wave_rows, payload):
     atoms, waves = own_cols.shape[0], wave_rows.shape[1]
     width = payload.shape[1]
     return pl.pallas_call(
-        functools.partial(own_kernel, scale),
+        own_kernel,
         out_shape=(
             jax.ShapeDtypeStruct((atoms, 2 * waves), BF16),
             jax.ShapeDtypeStruct((waves, width), F32),
@@ -420,37 +428,43 @@
     )(side, *chunks, own_cols, radial_flat, *more)
 
 
-def filter_kernel(mine_ref, other_ref, charge_ref, gain_ref, out_ref):
-    half = gain_ref.shape[0]
+def inverse_kernel(
+    part, scale, last, table_ref, mine_ref, other_ref, charge_ref, gain_ref, base_ref, cols_ref,
+    out_ref, factor_ref,
+):
+    waves = mine_ref.shape[0]
+    half = waves // 2
     total = mine_ref[...] + other_ref[...].astype(F32)
     structure = jnp.dot(total.astype(BF16), charge_ref[...], preferred_element_type=F32)
-    gain = gain_ref[...]
-    out_ref[0:half] = (structure[0:half] * gain).astype(BF16)
-    out_ref[half:] = (structure[half:] * gain).astype(BF16)
-
-
-def filter_half(mine, other, charge_weight, gain):
+    gain = gain_ref[part * half : (part + 1) * half, :]
+    factor_ref[0:half] = (structure[0:half] * gain).astype(BF16)
+    factor_ref[half:] = (structure[half:] * gain).astype(BF16)
+    total = base_ref[...] + scale * jnp.dot(
+        table_ref[:, part * waves : (part + 1) * waves],
+        factor_ref[...],
+        preferred_element_type=F32,
+    )
+    if not last:
+        out_ref[...] = total
+        return
+    total = jnp.where(cols_ref[:, 6:7] > 0.5, total, 0.0)
+    cells, slots, _ = out_ref.shape
+    for cell in range(cells):
+        out_ref[cell] = total[cell * slots : (cell + 1) * slots].astype(BF16)
+
+
+def add_inverse(
+    part, scale, table, mine, other, charge_weight, gain, base, own_cols, out_shape=None
+):
+    last = out_shape is not None
     return pl.pallas_call(
-        filter_kernel,
-        out_shape=jax.ShapeDtypeStruct(mine.shape, BF16),
+        functools.partial(inverse_kernel, part, scale, last),
+        out_shape=out_shape if last else jax.ShapeDtypeStruct(base.shape, F32),
+        scratch_shapes=[pltpu.VMEM(mine.shape, BF16)],
         compiler_params=PARAMS,
-        name="filter",
-    )(mine, other, charge_weight, gain)
-
-
-def inverse_kernel(scale, table_ref, factor_ref, base_ref, out_ref):
-    out_ref[...] = base_ref[...] + scale * jnp.dot(
-        table_ref[...], factor_ref[...], preferred_element_type=F32
-    )
-
-
-def finish_kernel(scale, slots, cols_ref, table_ref, factor_ref, base_ref, out_ref):
-    total = base_ref[...] + scale * jnp.dot(
-        table_ref[...], factor_ref[...], preferred_element_type=F32
-    )
-    total = jnp.where(cols_ref[:, 6:7] > 0.5, total, 0.0)
-    for cell in range(total.shape[0] // slots):
-        out_ref[cell] = total[cell * slots : (cell + 1) * slots].astype(BF16)
+        cost_estimate=cost(mine.shape[0] * mine.shape[1] * base.shape[0] * 4),
+        name="inverse",
+    )(table, mine, other, charge_weight, gain, base, own_cols)
 
 
 def local(atom_features, offsets, counts, radial_weight, charge_weight, wave_filter, wavevectors):
@@ -466,16 +480,15 @@
     core = layer % cores
     layer_scalar = layer.astype(jnp.int32).reshape(1)
     core_scalar = core.astype(jnp.int32).reshape(1)
-    payload, own_cols = prepare(layer_scalar, counts, atom_features, offsets)
+    payload, own_cols, own_waves, own_filter = prepare(
+        layer_scalar, counts, atom_features, offsets, wavevectors, wave_filter
+    )
 
     def swap(value, mask):
         return lax.ppermute(value, "space", [(i, i ^ mask) for i in range(size)])
 
-    rows_main, main_waves, tail_waves, gain, second = wave_tables(
-        core_scalar, wavevectors, wave_filter, size, payload
-    )
-    scale = 1.0 / (GRID * size)
-    table, *sums = own_layer(own_cols, rows_main, second, scale)
+    rows_main, main_waves, tail_waves, gain = wave_tables(own_waves, own_filter, size)
+    table, *sums = own_layer(own_cols, rows_main, payload)
     side = 1 - 2 * core_scalar
     radial_flat = radial_weight.reshape(basis_count * width, width)
 
@@ -483,17 +496,17 @@
     near_keys = [k for k in range(1, deep) if k == 1]
     far_keys = [k for k in range(deep - 1, 2, -1)]
     last_keys = [k for k in range(1, deep) if k == 2]
-    along = {k: swap(payload, k * stride) for k in far_keys + last_keys}
+    along = {k: swap(payload, k * stride) for k in far_keys}
     along.update({k: swap(payload, k * stride) for k in near_keys})
     beside = swap(payload, cores)
     pair = swap(payload, 1)
 
-    def structure(chunks, parts, token, sums, kept_as=F32):
+    def structure(chunks, parts, token, sums, sent=False):
         groups = [chunks[i : i + 4] for i in range(0, len(chunks), 4)]
         for index, group in enumerate(groups):
-            kind = kept_as if index == len(groups) - 1 else F32
+            ends = sent and index == len(groups) - 1
             sums = add_structure(
-                group, parts, main_waves, tail_waves, token, sums, atoms, scale, kind
+                group, parts, main_waves, tail_waves, token, sums, atoms, ends
             )
         return sums
 
@@ -503,12 +516,16 @@
     both = (0, 1)
     across = {k: swap(after(along[k], table), cores) for k in near_keys}
     sums = structure([beside] + [along[k] for k in near_keys], both, side, sums)
-    first = dict(across)
+    short = short_range(side, (payload, pair), (0.0, 1.0), own_cols, radial_flat, slots, basis_count)
+    along.update({k: swap(after(payload, short), k * stride) for k in last_keys})
+    near = dict(across)
     for k in far_keys:
-        across[k] = swap(after(along[k], (sums[1], first)), cores)
-    short = short_range(side, (second, pair), (0.0, 1.0), own_cols, radial_flat, slots, basis_count)
+        across[k] = swap(after(along[k], (sums[1], short)), cores)
+    sums = structure(
+        [along[k] for k in far_keys] + [across[k] for k in near_keys], both, short, sums
+    )
     for k in last_keys:
-        across[k] = swap(after(along[k], short), cores)
+        across[k] = swap(after(along[k], sums[1]), cores)
 
     z = layer // stride
     y = (layer // cores) % near_y
@@ -520,49 +537,22 @@
             take = (wanted == k) & (y == jnp.where(core == 0, near_y - 1, 0))
             crossing = jnp.where(take, across[k], crossing)
     far = swap(crossing, 1)
-    sums = structure(
-        [along[k] for k in far_keys] + [across[k] for k in near_keys] + [along[k] for k in last_keys]
-        + [across[k] for k in far_keys],
-        both, short, sums,
-    )
+    sums = structure([along[k] for k in last_keys] + [across[k] for k in far_keys], both, side, sums)
     base = short_range(
-        side, (far,), (-1.0,), own_cols, radial_flat, slots, basis_count, (short, second)
+        side, (far,), (-1.0,), own_cols, radial_flat, slots, basis_count, (short, payload)
     )
     final = [across[k] for k in last_keys]
-    (send,) = structure(final, (1,), base, sums[1:], BF16)
-    (mine,) = structure(final, (0,), send, sums[:1])
-    factors = filter_half(mine, swap(send, 1), charge_weight, gain)
-    other_factors = swap(factors, 1)
+    mine_a, sent_a = structure(final, (0,), base, sums[:1], True)
+    mine_b, sent_b = structure(final, (1,), sent_a, sums[1:], True)
+    theirs_a = swap(sent_a, 1)
+    theirs_b = swap(sent_b, 1)
 
     recip_scale = 1.0 / math.sqrt(atoms * size * wave_count)
-    vmem = pl.BlockSpec(memory_space=pltpu.VMEM)
-    base = pl.pallas_call(
-        functools.partial(inverse_kernel, recip_scale),
-        grid=(1,),
-        in_specs=[
-            pl.BlockSpec((atoms, wave_count), lambda i: (0, 0)),
-            pl.BlockSpec((wave_count, width), lambda i: (0, 0)),
-            pl.BlockSpec((atoms, width), lambda i: (0, 0)),
-        ],
-        out_specs=pl.BlockSpec((atoms, width), lambda i: (0, 0)),
-        out_shape=jax.ShapeDtypeStruct((atoms, width), F32),
-        compiler_params=PARAMS,
-        name="inverse",
-    )(table, factors, base)
-    return pl.pallas_call(
-        functools.partial(finish_kernel, recip_scale, slots),
-        grid=(1,),
-        in_specs=[
-            pl.BlockSpec((atoms, COORD_ROWS), lambda i: (0, 0)),
-            pl.BlockSpec((atoms, wave_count), lambda i: (0, 1)),
-            pl.BlockSpec((wave_count, width), lambda i: (0, 0)),
-            pl.BlockSpec((atoms, width), lambda i: (0, 0)),
-        ],
-        out_specs=pl.BlockSpec((cells, slots, width), lambda i: (0, 0, 0)),
-        out_shape=jax.ShapeDtypeStruct((cells, slots, width), BF16),
-        compiler_params=PARAMS,
-        name="finish",
-    )(own_cols, table, other_factors, base)
+    base = add_inverse(0, recip_scale, table, mine_a, theirs_a, charge_weight, gain, base, own_cols)
+    out_shape = jax.ShapeDtypeStruct(atom_features.shape, BF16)
+    return add_inverse(
+        1, recip_scale, table, mine_b, theirs_b, charge_weight, gain, base, own_cols, out_shape
+    )
 
 
 def solution(mesh):

time: 37.5 us -> 34.3 us (0.915)
  the two profiles are of different devices: /device:TPU:11 before, /device:TPU:0 now
where the time goes in v3:
time: 34.3 us; the launch traced here: 34.1 us
  Pallas kernels  17.9 us (52%)
  starting transfers between devices  10.6 us (31%)
  waiting for transfers between devices  5.4 us (16%)
    ppermute x11, starting transfers between devices, swap(): return lax.ppermute(value, 'space', [(i, i ^ mask) for i in range(size)])  10.6 us
    pallas_call x5, Pallas kernels, add_structure(): pl.pallas_call(functools.partial(structure_kernel, count, atoms, parts, s...  8.91 us
    ppermute x11, waiting for transfers between devices, swap(): return lax.ppermute(value, 'space', [(i, i ^ mask) for i in range(size)])  5.4 us
    pallas_call x2, Pallas kernels, short_range(): pl.pallas_call(functools.partial(short_kernel, atoms // slots, slots, bas...  3.22 us
    pallas_call x2, Pallas kernels, add_inverse(): pl.pallas_call(functools.partial(inverse_kernel, part, scale, last), out_...  1.93 us
    pallas_call x1, Pallas kernels, own_layer(): pl.pallas_call(own_kernel, out_shape=(jax.ShapeDtypeStruct((atoms, 2 * wa...  1.74 us
    pallas_call x1, Pallas kernels, prepare(): pl.pallas_call(prepare_kernel, out_shape=(jax.ShapeDtypeStruct((atoms + C...  1.11 us
    pallas_call x1, Pallas kernels, wave_tables(): pl.pallas_call(functools.partial(wave_kernel, size), out_shape=(jax.Shape...  1.03 us
  transfers between devices with their start and end apart: 11, of which 5 were waited for; matrix products, arithmetic and copies ran while one was open for 0% of the time, Pallas kernels for 43%

profile of v3, /device:TPU:0, one launch (start us, length us, event | category | flops | bytes accessed | tf_op | source)
XLA Modules:
  0.0 34.1 jit_solution(17860504916617915787)
XLA Ops:
  0.0 1.1 %prepare.1 = (bf16[304,256]{1,0:T(8,128)(2,1)S(1)}, f32[288,16]{1,0:T(8,128)S(1)}, s32[3,1024]{1,0:T(4,128)S(1)}, f32[4,256]{1,0:T(4,128)S(1)}) custom-call(s32[1]{0:T(128)} %bitcast.layer_ref, s32[9]{0:T(128)} %counts_any.1, bf16[9,32,256]{2,1,0:T(8,128)(2,1)} %features_any.1, bf16[9,3,32]{2,1,0:T(4,128)(2,1)} %offsets_any.1, s32[3,1024]{1,0:T(4,128)} %waves_any.1, ...), custom_call_target="tpu_custom_call" | custom-call | tf_op jit(solution)/shard_map/prepare/pallas_call | solution.py:127
  1.1 0.5 %collective-permute-start = (bf16[304,256]{1,0:T(8,128)(2,1)S(1)}, bf16[304,256]{1,0:T(8,128)(2,1)S(1)}, u32[]{:S(2)}, u32[]{:S(2)}) collective-permute-start(bf16[304,256]{1,0:T(8,128)(2,1)S(1)} %get-tuple-element.36.payload_ref.refs_1_.refs_5_), channel_id=1, source_target_pairs={{0,1},{1,0},{2,3},{3,2},{4,5},{5,4},{6,7},{7,6},{8,9},{9,8},{10,11... | collective-permute-start | bytes 466952 | tf_op jit(solution)/shard_map/ppermute | solution.py:488
  1.6 2.6 %collective-permute-start.5 = (bf16[304,256]{1,0:T(8,128)(2,1)S(1)}, bf16[304,256]{1,0:T(8,128)(2,1)S(1)}, u32[]{:S(2)}, u32[]{:S(2)}) collective-permute-start(bf16[304,256]{1,0:T(8,128)(2,1)S(1)} %get-tuple-element.36.payload_ref.refs_1_.refs_5_), channel_id=1, source_target_pairs={{0,2},{1,3},{2,0},{3,1},{4,6},{5,7},{6,4},{7,5},{8,10},{9,11},{10,... | collective-permute-start | bytes 466952 | tf_op jit(solution)/shard_map/ppermute | solution.py:488
  4.2 1.6 %collective-permute-start.3 = (bf16[304,256]{1,0:T(8,128)(2,1)S(1)}, bf16[304,256]{1,0:T(8,128)(2,1)S(1)}, u32[]{:S(2)}, u32[]{:S(2)}) collective-permute-start(bf16[304,256]{1,0:T(8,128)(2,1)S(1)} %get-tuple-element.36.payload_ref.refs_1_.refs_5_), channel_id=1, source_target_pairs={{0,4},{1,5},{2,6},{3,7},{4,0},{5,1},{6,2},{7,3},{8,12},{9,13},{10,... | collective-permute-start | bytes 466952 | tf_op jit(solution)/shard_map/ppermute | solution.py:488
  5.8 2.5 %collective-permute-start.2 = (bf16[304,256]{1,0:T(8,128)(2,1)S(1)}, bf16[304,256]{1,0:T(8,128)(2,1)S(1)}, u32[]{:S(2)}, u32[]{:S(2)}) collective-permute-start(bf16[304,256]{1,0:T(8,128)(2,1)S(1)} %get-tuple-element.36.payload_ref.refs_1_.refs_5_), channel_id=1, source_target_pairs={{0,12},{1,13},{2,14},{3,15},{4,8},{5,9},{6,10},{7,11},{8,4},{9,5},... | collective-permute-start | bytes 466952 | tf_op jit(solution)/shard_map/ppermute | solution.py:488
  8.3 1.0 %waves.1 = (bf16[48,1024]{1,0:T(8,128)(2,1)S(1)}, bf16[1024,48]{1,0:T(8,128)(2,1)S(1)}, bf16[1024,48]{1,0:T(8,128)(2,1)S(1)}, f32[1024,256]{1,0:T(8,128)S(1)}) custom-call(s32[3,1024]{1,0:T(4,128)S(1)} %get-tuple-element.31.waves_ref, f32[4,256]{1,0:T(4,128)S(1)} %get-tuple-element.32.filter_ref), custom_call_target="tpu_custom_call" | custom-call | tf_op jit(solution)/shard_map/waves/pallas_call | solution.py:187
  9.3 1.7 %own_layer.1 = (bf16[288,2048]{1,0:T(8,128)(2,1)S(1)}, f32[1024,256]{1,0:T(8,128)S(1)}, f32[1024,256]{1,0:T(8,128)S(1)}) custom-call(f32[288,16]{1,0:T(8,128)S(1)} %get-tuple-element.30.cols_ref.refs_3_.refs_2_, bf16[48,1024]{1,0:T(8,128)(2,1)S(1)} %get-tuple-element.33.waves_ref, bf16[304,256]{1,0:T(8,128)(2,1)S(1)} %get-tuple-element.36.payload_ref.refs_1_.refs_5_), custom_call_target="tpu_custom_call" | custom-call | flops 301989888 | bytes 301989 | tf_op jit(solution)/shard_map/own_layer/pallas_call | solution.py:301
  11.1 1.8 %short_range.2.refs_4_ = f32[288,256]{1,0:T(8,128)S(1)} custom-call(s32[1]{0:T(128)} %bitcast.1.refs_0_.refs_4_, bf16[304,256]{1,0:T(8,128)(2,1)S(1)} %get-tuple-element.36.payload_ref.refs_1_.refs_5_, bf16[304,256]{1,0:T(8,128)(2,1)S(1)} %collective-permute-done.refs_2_, f32[288,16]{1,0:T(8,128)S(1)} %get-tuple-element.30.cols_ref.refs_3_.refs_2_, ...), custom_call_target="tpu_custom_call" | custom-call | flops 1887436800 | bytes 1887436 | tf_op jit(solution)/shard_map/short_range/pallas_call | solution.py:413
  13.1 0.5 %collective-permute-start.4 = (bf16[304,256]{1,0:T(8,128)(2,1)S(1)}, bf16[304,256]{1,0:T(8,128)(2,1)S(1)}, u32[]{:S(2)}, u32[]{:S(2)}) collective-permute-start(bf16[304,256]{1,0:T(8,128)(2,1)S(1)} %collective-permute-done.3.refs_1_), channel_id=1, source_target_pairs={{0,2},{1,3},{2,0},{3,1},{4,6},{5,7},{6,4},{7,5},{8,10},{9,11},{10,... | collective-permute-start | bytes 466952 | tf_op jit(solution)/shard_map/ppermute | solution.py:488
  13.6 2.3 %structure.5 = (f32[1024,256]{1,0:T(8,128)S(1)}, f32[1024,256]{1,0:T(8,128)S(1)}) custom-call(bf16[304,256]{1,0:T(8,128)(2,1)S(1)} %collective-permute-done.5.refs_0_, bf16[304,256]{1,0:T(8,128)(2,1)S(1)} %collective-permute-done.3.refs_1_, bf16[1024,48]{1,0:T(8,128)(2,1)S(1)} %get-tuple-element.38.refs_2_.refs_1_, ...), custom_call_target="tpu_custom_call" | custom-call | flops 2013265920 | bytes 2013265 | tf_op jit(solution)/shard_map/structure/pallas_call | solution.py:258
  15.9 1.6 %collective-permute-start.7 = (bf16[304,256]{1,0:T(8,128)(2,1)S(1)}, bf16[304,256]{1,0:T(8,128)(2,1)S(1)}, u32[]{:S(2)}, u32[]{:S(2)}) collective-permute-start(bf16[304,256]{1,0:T(8,128)(2,1)S(1)} %collective-permute-done.2.refs_0_), channel_id=1, source_target_pairs={{0,2},{1,3},{2,0},{3,1},{4,6},{5,7},{6,4},{7,5},{8,10},{9,11},{10,... | collective-permute-start | bytes 466952 | tf_op jit(solution)/shard_map/ppermute | solution.py:488
  17.5 1.8 %collective-permute-done.4.refs_1_ = bf16[304,256]{1,0:T(8,128)(2,1)S(1)} collective-permute-done((bf16[304,256]{1,0:T(8,128)(2,1)S(1)}, bf16[304,256]{1,0:T(8,128)(2,1)S(1)}, u32[]{:S(2)}, u32[]{:S(2)}) %collective-permute-start.4) | collective-permute-done | bytes 155680 | tf_op jit(solution)/shard_map/ppermute | solution.py:488
  19.3 2.3 %structure.6 = (f32[1024,256]{1,0:T(8,128)S(1)}, f32[1024,256]{1,0:T(8,128)S(1)}) custom-call(bf16[304,256]{1,0:T(8,128)(2,1)S(1)} %collective-permute-done.2.refs_0_, bf16[304,256]{1,0:T(8,128)(2,1)S(1)} %collective-permute-done.4.refs_1_, bf16[1024,48]{1,0:T(8,128)(2,1)S(1)} %get-tuple-element.38.refs_2_.refs_1_, ...), custom_call_target="tpu_custom_call" | custom-call | flops 2013265920 | bytes 2013265 | tf_op jit(solution)/shard_map/structure/pallas_call | solution.py:258
  21.6 1.1 %collective-permute-done.1.refs_0_ = bf16[304,256]{1,0:T(8,128)(2,1)S(1)} collective-permute-done((bf16[304,256]{1,0:T(8,128)(2,1)S(1)}, bf16[304,256]{1,0:T(8,128)(2,1)S(1)}, u32[]{:S(2)}, u32[]{:S(2)}) %collective-permute-start.1) | collective-permute-done | bytes 155680 | tf_op jit(solution)/shard_map/ppermute | solution.py:488
  22.7 0.5 %collective-permute-start.6 = (bf16[304,256]{1,0:T(8,128)(2,1)S(1)}, bf16[304,256]{1,0:T(8,128)(2,1)S(1)}, u32[]{:S(2)}, u32[]{:S(2)}) collective-permute-start(bf16[304,256]{1,0:T(8,128)(2,1)S(1)} %collective-permute-done.1.refs_0_), channel_id=1, source_target_pairs={{0,2},{1,3},{2,0},{3,1},{4,6},{5,7},{6,4},{7,5},{8,10},{9,11},{10,... | collective-permute-start | bytes 466952 | tf_op jit(solution)/shard_map/ppermute | solution.py:488
  23.4 2.3 %structure.7 = (f32[1024,256]{1,0:T(8,128)S(1)}, f32[1024,256]{1,0:T(8,128)S(1)}) custom-call(bf16[304,256]{1,0:T(8,128)(2,1)S(1)} %collective-permute-done.1.refs_0_, bf16[304,256]{1,0:T(8,128)(2,1)S(1)} %collective-permute-done.7.refs_1_, bf16[1024,48]{1,0:T(8,128)(2,1)S(1)} %get-tuple-element.38.refs_2_.refs_1_, ...), custom_call_target="tpu_custom_call" | custom-call | flops 2013265920 | bytes 2013265 | tf_op jit(solution)/shard_map/structure/pallas_call | solution.py:258
  25.7 1.4 %short_range.3.refs_3_.base_ref = f32[288,256]{1,0:T(8,128)S(1)} custom-call(s32[1]{0:T(128)} %bitcast.1.refs_0_.refs_4_, bf16[304,256]{1,0:T(8,128)(2,1)S(1)} %collective-permute-done.8.refs_1_, f32[288,16]{1,0:T(8,128)S(1)} %get-tuple-element.30.cols_ref.refs_3_.refs_2_, bf16[1024,256]{1,0:T(8,128)(2,1)S(1)} %bitcast.4, ...), custom_call_target="tpu_custom_call" | custom-call | flops 1132462080 | bytes 1132462 | tf_op jit(solution)/shard_map/short_range/pallas_call | solution.py:413
  27.1 1.6 %collective-permute-done.6.refs_0_ = bf16[304,256]{1,0:T(8,128)(2,1)S(1)} collective-permute-done((bf16[304,256]{1,0:T(8,128)(2,1)S(1)}, bf16[304,256]{1,0:T(8,128)(2,1)S(1)}, u32[]{:S(2)}, u32[]{:S(2)}) %collective-permute-start.6) | collective-permute-done | bytes 155680 | tf_op jit(solution)/shard_map/ppermute | solution.py:488
  28.7 1.0 %structure.8 = (f32[1024,256]{1,0:T(8,128)S(1)}, bf16[1024,256]{1,0:T(8,128)(2,1)S(1)}) custom-call(bf16[304,256]{1,0:T(8,128)(2,1)S(1)} %collective-permute-done.6.refs_0_, bf16[1024,48]{1,0:T(8,128)(2,1)S(1)} %get-tuple-element.38.refs_2_.refs_1_, bf16[1024,48]{1,0:T(8,128)(2,1)S(1)} %get-tuple-element.39.refs_3_.refs_2_, ...), custom_call_target="tpu_custom_call" | custom-call | flops 603979776 | bytes 603979 | tf_op jit(solution)/shard_map/structure/pallas_call | solution.py:258
  29.7 1.0 %structure.9 = (f32[1024,256]{1,0:T(8,128)S(1)}, bf16[1024,256]{1,0:T(8,128)(2,1)S(1)}) custom-call(bf16[304,256]{1,0:T(8,128)(2,1)S(1)} %collective-permute-done.6.refs_0_, bf16[1024,48]{1,0:T(8,128)(2,1)S(1)} %get-tuple-element.38.refs_2_.refs_1_, bf16[1024,48]{1,0:T(8,128)(2,1)S(1)} %get-tuple-element.39.refs_3_.refs_2_, ...), custom_call_target="tpu_custom_call" | custom-call | flops 603979776 | bytes 603979 | tf_op jit(solution)/shard_map/structure/pallas_call | solution.py:258
  30.7 0.6 %collective-permute-start.9 = (bf16[1024,256]{1,0:T(8,128)(2,1)S(1)}, bf16[1024,256]{1,0:T(8,128)(2,1)S(1)}, u32[]{:S(2)}, u32[]{:S(2)}) collective-permute-start(bf16[1024,256]{1,0:T(8,128)(2,1)S(1)} %get-tuple-element.52), channel_id=1, source_target_pairs={{0,1},{1,0},{2,3},{3,2},{4,5},{5,4},{6,7},{7,6},{8,9},{9,8},{10,11... | collective-permute-start | bytes 1572872 | tf_op jit(solution)/shard_map/ppermute | solution.py:488
  31.6 0.6 %inverse.2.base_ref = f32[288,256]{1,0:T(8,128)S(1)} custom-call(bf16[288,2048]{1,0:T(8,128)(2,1)S(1)} %get-tuple-element.35.table_ref, f32[1024,256]{1,0:T(8,128)S(1)} %get-tuple-element.54.mine_ref, bf16[1024,256]{1,0:T(8,128)(2,1)S(1)} %collective-permute-done.10.other_ref, bf16[256,256]{1,0:T(8,128)(2,1)S(1)} %copy-done, ...), custom_call_target="tpu_custom_call" | custom-call | flops 301989888 | bytes 301989 | tf_op jit(solution)/shard_map/inverse/pallas_call | solution.py:460
  32.3 0.6 %collective-permute-done.9.other_ref = bf16[1024,256]{1,0:T(8,128)(2,1)S(1)} collective-permute-done((bf16[1024,256]{1,0:T(8,128)(2,1)S(1)}, bf16[1024,256]{1,0:T(8,128)(2,1)S(1)}, u32[]{:S(2)}, u32[]{:S(2)}) %collective-permute-start.9) | collective-permute-done | bytes 524320 | tf_op jit(solution)/shard_map/ppermute | solution.py:488
  32.8 1.3 %inverse.3 = bf16[9,32,256]{2,1,0:T(8,128)(2,1)} custom-call(bf16[288,2048]{1,0:T(8,128)(2,1)S(1)} %get-tuple-element.35.table_ref, f32[1024,256]{1,0:T(8,128)S(1)} %get-tuple-element.51.mine_ref, bf16[1024,256]{1,0:T(8,128)(2,1)S(1)} %collective-permute-done.9.other_ref, bf16[256,256]{1,0:T(8,128)(2,1)S(1)} %copy-done, ...), custom_call_target="tpu_custom_call" | custom-call | flops 301989888 | bytes 301989 | tf_op jit(solution)/shard_map/inverse/pallas_call | solution.py:460
  (15 shorter events, 0.7 us)
Async XLA Ops:
  0.0 11.1 %copy-start.1 = (bf16[4,256,256]{2,1,0:T(8,128)(2,1)S(1)}, bf16[4,256,256]{2,1,0:T(8,128)(2,1)}, u32[]{:S(2)}) copy-start(bf16[4,256,256]{2,1,0:T(8,128)(2,1)} %param.10) | copy-start | bytes 1572868
  1.1 9.9 %collective-permute-start = (bf16[304,256]{1,0:T(8,128)(2,1)S(1)}, bf16[304,256]{1,0:T(8,128)(2,1)S(1)}, u32[]{:S(2)}, u32[]{:S(2)}) collective-permute-start(bf16[304,256]{1,0:T(8,128)(2,1)S(1)} %get-tuple-element.36.payload_ref.refs_1_.refs_5_), channel_id=1, source_target_pairs={{0,1},{1,0},{2,3},{3,2},{4,5},{5,4},{6,7},{7,6},{8,9},{9,8},{10,11... | collective-permute-start | bytes 466952 | tf_op jit(solution)/shard_map/ppermute | solution.py:488
  1.6 12.0 %collective-permute-start.5 = (bf16[304,256]{1,0:T(8,128)(2,1)S(1)}, bf16[304,256]{1,0:T(8,128)(2,1)S(1)}, u32[]{:S(2)}, u32[]{:S(2)}) collective-permute-start(bf16[304,256]{1,0:T(8,128)(2,1)S(1)} %get-tuple-element.36.payload_ref.refs_1_.refs_5_), channel_id=1, source_target_pairs={{0,2},{1,3},{2,0},{3,1},{4,6},{5,7},{6,4},{7,5},{8,10},{9,11},{10,... | collective-permute-start | bytes 466952 | tf_op jit(solution)/shard_map/ppermute | solution.py:488
  4.2 8.9 %collective-permute-start.3 = (bf16[304,256]{1,0:T(8,128)(2,1)S(1)}, bf16[304,256]{1,0:T(8,128)(2,1)S(1)}, u32[]{:S(2)}, u32[]{:S(2)}) collective-permute-start(bf16[304,256]{1,0:T(8,128)(2,1)S(1)} %get-tuple-element.36.payload_ref.refs_1_.refs_5_), channel_id=1, source_target_pairs={{0,4},{1,5},{2,6},{3,7},{4,0},{5,1},{6,2},{7,3},{8,12},{9,13},{10,... | collective-permute-start | bytes 466952 | tf_op jit(solution)/shard_map/ppermute | solution.py:488
  5.8 10.1 %collective-permute-start.2 = (bf16[304,256]{1,0:T(8,128)(2,1)S(1)}, bf16[304,256]{1,0:T(8,128)(2,1)S(1)}, u32[]{:S(2)}, u32[]{:S(2)}) collective-permute-start(bf16[304,256]{1,0:T(8,128)(2,1)S(1)} %get-tuple-element.36.payload_ref.refs_1_.refs_5_), channel_id=1, source_target_pairs={{0,12},{1,13},{2,14},{3,15},{4,8},{5,9},{6,10},{7,11},{8,4},{9,5},... | collective-permute-start | bytes 466952 | tf_op jit(solution)/shard_map/ppermute | solution.py:488
  12.9 9.8 %collective-permute-start.1 = (bf16[304,256]{1,0:T(8,128)(2,1)S(1)}, bf16[304,256]{1,0:T(8,128)(2,1)S(1)}, u32[]{:S(2)}, u32[]{:S(2)}) collective-permute-start(bf16[304,256]{1,0:T(8,128)(2,1)S(1)} %get-tuple-element.36.payload_ref.refs_1_.refs_5_), channel_id=1, source_target_pairs={{0,8},{1,9},{2,10},{3,11},{4,12},{5,13},{6,14},{7,15},{8,0},{9,1},... | collective-permute-start | bytes 466952 | tf_op jit(solution)/shard_map/ppermute | solution.py:488
  13.1 6.2 %collective-permute-start.4 = (bf16[304,256]{1,0:T(8,128)(2,1)S(1)}, bf16[304,256]{1,0:T(8,128)(2,1)S(1)}, u32[]{:S(2)}, u32[]{:S(2)}) collective-permute-start(bf16[304,256]{1,0:T(8,128)(2,1)S(1)} %collective-permute-done.3.refs_1_), channel_id=1, source_target_pairs={{0,2},{1,3},{2,0},{3,1},{4,6},{5,7},{6,4},{7,5},{8,10},{9,11},{10,... | collective-permute-start | bytes 466952 | tf_op jit(solution)/shard_map/ppermute | solution.py:488
  15.9 7.3 %collective-permute-start.7 = (bf16[304,256]{1,0:T(8,128)(2,1)S(1)}, bf16[304,256]{1,0:T(8,128)(2,1)S(1)}, u32[]{:S(2)}, u32[]{:S(2)}) collective-permute-start(bf16[304,256]{1,0:T(8,128)(2,1)S(1)} %collective-permute-done.2.refs_0_), channel_id=1, source_target_pairs={{0,2},{1,3},{2,0},{3,1},{4,6},{5,7},{6,4},{7,5},{8,10},{9,11},{10,... | collective-permute-start | bytes 466952 | tf_op jit(solution)/shard_map/ppermute | solution.py:488
  22.7 5.9 %collective-permute-start.6 = (bf16[304,256]{1,0:T(8,128)(2,1)S(1)}, bf16[304,256]{1,0:T(8,128)(2,1)S(1)}, u32[]{:S(2)}, u32[]{:S(2)}) collective-permute-start(bf16[304,256]{1,0:T(8,128)(2,1)S(1)} %collective-permute-done.1.refs_0_), channel_id=1, source_target_pairs={{0,2},{1,3},{2,0},{3,1},{4,6},{5,7},{6,4},{7,5},{8,10},{9,11},{10,... | collective-permute-start | bytes 466952 | tf_op jit(solution)/shard_map/ppermute | solution.py:488
  23.3 2.4 %collective-permute-start.8 = (bf16[304,256]{1,0:T(8,128)(2,1)S(1)}, bf16[304,256]{1,0:T(8,128)(2,1)S(1)}, u32[]{:S(2)}, u32[]{:S(2)}) collective-permute-start(bf16[304,256]{1,0:T(8,128)(2,1)S(1)} %select_select_fusion), channel_id=1, source_target_pairs={{0,1},{1,0},{2,3},{3,2},{4,5},{5,4},{6,7},{7,6},{8,9},{9,8},{10,11... | collective-permute-start | bytes 466952 | tf_op jit(solution)/shard_map/ppermute | solution.py:488
  29.7 2.0 %copy-start = (bf16[256,256]{1,0:T(8,128)(2,1)S(1)}, bf16[256,256]{1,0:T(8,128)(2,1)}, u32[]{:S(2)}) copy-start(bf16[256,256]{1,0:T(8,128)(2,1)} %charge_ref.3) | copy-start | bytes 393220
  29.7 2.0 %collective-permute-start.10 = (bf16[1024,256]{1,0:T(8,128)(2,1)S(1)}, bf16[1024,256]{1,0:T(8,128)(2,1)S(1)}, u32[]{:S(2)}, u32[]{:S(2)}) collective-permute-start(bf16[1024,256]{1,0:T(8,128)(2,1)S(1)} %get-tuple-element.49.refs_3_), channel_id=1, source_target_pairs={{0,1},{1,0},{2,3},{3,2},{4,5},{5,4},{6,7},{7,6},{8,9},{9,8},{10,11... | collective-permute-start | bytes 1572872 | tf_op jit(solution)/shard_map/ppermute | solution.py:488
  30.7 2.1 %collective-permute-start.9 = (bf16[1024,256]{1,0:T(8,128)(2,1)S(1)}, bf16[1024,256]{1,0:T(8,128)(2,1)S(1)}, u32[]{:S(2)}, u32[]{:S(2)}) collective-permute-start(bf16[1024,256]{1,0:T(8,128)(2,1)S(1)} %get-tuple-element.52), channel_id=1, source_target_pairs={{0,1},{1,0},{2,3},{3,2},{4,5},{5,4},{6,7},{7,6},{8,9},{9,8},{10,11... | collective-permute-start | bytes 1572872 | tf_op jit(solution)/shard_map/ppermute | solution.py:488

commit v4 on v3

--- a/solution.py
+++ b/solution.py
@@ -270,7 +270,9 @@
     )(*chunks, main_waves, tail_waves, token, *sums)
 
 
-def own_kernel(cols_ref, waves_ref, payload_ref, table_ref, mine_ref, other_ref, phase_ref):
+def own_kernel(
+    cols_ref, waves_ref, payload_ref, _, table_ref, mine_ref, other_ref, phase_ref
+):
     waves = waves_ref.shape[1]
     half = waves // 2
     atoms = cols_ref.shape[0]
@@ -295,7 +297,7 @@
         )
 
 
-def own_layer(own_cols, wave_rows, payload):
+def own_layer(own_cols, wave_rows, payload, token):
     atoms, waves = own_cols.shape[0], wave_rows.shape[1]
     width = payload.shape[1]
     return pl.pallas_call(
@@ -305,11 +307,12 @@
             jax.ShapeDtypeStruct((waves, width), F32),
             jax.ShapeDtypeStruct((waves, width), F32),
         ),
+        in_specs=[pl.BlockSpec(memory_space=pltpu.VMEM)] * 3 + [pl.BlockSpec(memory_space=pl.ANY)],
         scratch_shapes=[pltpu.VMEM((atoms, waves), F32)],
         compiler_params=PARAMS,
         cost_estimate=cost(4 * atoms * waves * width),
         name="own_layer",
-    )(own_cols, wave_rows, payload)
+    )(own_cols, wave_rows, payload, token)
 
 
 def short_kernel(cells, slots, basis_count, signs, holds_own, last, scale, *refs):
@@ -488,9 +491,11 @@
         return lax.ppermute(value, "space", [(i, i ^ mask) for i in range(size)])
 
     rows_main, main_waves, tail_waves, gain = wave_tables(own_waves, own_filter, size)
-    table, *sums = own_layer(own_cols, rows_main, payload)
     side = 1 - 2 * core_scalar
     radial_flat = radial_weight.reshape(basis_count * width, width)
+
+    def after(value, token):
+        return lax.optimization_barrier((value, token))[0]
 
     stride = cores * near_y
     near_keys = [k for k in range(1, deep) if k == 1]
@@ -498,7 +503,7 @@
     last_keys = [k for k in range(1, deep) if k == 2]
     along = {k: swap(payload, k * stride) for k in far_keys}
     along.update({k: swap(payload, k * stride) for k in near_keys})
-    beside = swap(payload, cores)
+    beside = swap(after(payload, rows_main), cores)
     pair = swap(payload, 1)
 
     def structure(chunks, parts, token, sums, sent=False):
@@ -510,13 +515,11 @@
             )
         return sums
 
-    def after(value, token):
-        return lax.optimization_barrier((value, token))[0]
-
+    short = short_range(side, (payload, pair), (0.0, 1.0), own_cols, radial_flat, slots, basis_count)
+    table, *sums = own_layer(own_cols, rows_main, payload, short)
     both = (0, 1)
     across = {k: swap(after(along[k], table), cores) for k in near_keys}
     sums = structure([beside] + [along[k] for k in near_keys], both, side, sums)
-    short = short_range(side, (payload, pair), (0.0, 1.0), own_cols, radial_flat, slots, basis_count)
     along.update({k: swap(after(payload, short), k * stride) for k in last_keys})
     near = dict(across)
     for k in far_keys:

time: 34.3 us -> 33.7 us (0.983)
  waiting for transfers between devices: 5.4 us -> 4.05 us
  local copies, waits for them, and re-layouts: 0.01 us -> 1.05 us
    ppermute x11, waiting for transfers between devices: 5.4 us -> 4.05 us  [swap(): return lax.ppermute(value, 'space', [(i, i ^ mask) for i in range(size)])]
    unnamed x4 -> x6, local copies, waits for them, and re-layouts: 0.01 us -> 1.05 us
where the time goes in v4:
time: 33.7 us; the launch traced here: 33.5 us
  Pallas kernels  17.9 us (53%)
  starting transfers between devices  10.3 us (31%)
  waiting for transfers between devices  4.05 us (12%)
  local copies, waits for them, and re-layouts  1.05 us (3%)
    ppermute x11, starting transfers between devices, swap(): return lax.ppermute(value, 'space', [(i, i ^ mask) for i in range(size)])  10.3 us
    pallas_call x5, Pallas kernels, add_structure(): pl.pallas_call(functools.partial(structure_kernel, count, atoms, parts, s...  8.94 us
    ppermute x11, waiting for transfers between devices, swap(): return lax.ppermute(value, 'space', [(i, i ^ mask) for i in range(size)])  4.05 us
    pallas_call x2, Pallas kernels, short_range(): pl.pallas_call(functools.partial(short_kernel, atoms // slots, slots, bas...  3.2 us
    pallas_call x2, Pallas kernels, add_inverse(): pl.pallas_call(functools.partial(inverse_kernel, part, scale, last), out_...  1.93 us
    pallas_call x1, Pallas kernels, own_layer(): pl.pallas_call(own_kernel, out_shape=(jax.ShapeDtypeStruct((atoms, 2 * wa...  1.74 us
    pallas_call x1, Pallas kernels, prepare(): pl.pallas_call(prepare_kernel, out_shape=(jax.ShapeDtypeStruct((atoms + C...  1.07 us
    unnamed x6, local copies, waits for them, and re-layouts  1.05 us
  transfers between devices with their start and end apart: 11, of which 5 were waited for; matrix products, arithmetic and copies ran while one was open for 0% of the time, Pallas kernels for 43%

profile of v4, /device:TPU:0, one launch (start us, length us, event | category | flops | bytes accessed | tf_op | source)
XLA Modules:
  0.0 33.5 jit_solution(15157905058761666954)
XLA Ops:
  0.0 1.1 %prepare.1 = (bf16[304,256]{1,0:T(8,128)(2,1)S(1)}, f32[288,16]{1,0:T(8,128)S(1)}, s32[3,1024]{1,0:T(4,128)S(1)}, f32[4,256]{1,0:T(4,128)S(1)}) custom-call(s32[1]{0:T(128)} %bitcast.layer_ref, s32[9]{0:T(128)} %counts_any.1, bf16[9,32,256]{2,1,0:T(8,128)(2,1)} %features_any.1, bf16[9,3,32]{2,1,0:T(4,128)(2,1)} %offsets_any.1, s32[3,1024]{1,0:T(4,128)} %waves_any.1, ...), custom_call_target="tpu_custom_call" | custom-call | tf_op jit(solution)/shard_map/prepare/pallas_call | solution.py:127
  1.1 0.5 %collective-permute-start = (bf16[304,256]{1,0:T(8,128)(2,1)S(1)}, bf16[304,256]{1,0:T(8,128)(2,1)S(1)}, u32[]{:S(2)}, u32[]{:S(2)}) collective-permute-start(bf16[304,256]{1,0:T(8,128)(2,1)S(1)} %get-tuple-element.41.refs_1_.payload_ref.refs_5_), channel_id=1, source_target_pairs={{0,1},{1,0},{2,3},{3,2},{4,5},{5,4},{6,7},{7,6},{8,9},{9,8},{10,11... | collective-permute-start | bytes 466952 | tf_op jit(solution)/shard_map/ppermute | solution.py:491
  1.6 2.6 %collective-permute-start.3 = (bf16[304,256]{1,0:T(8,128)(2,1)S(1)}, bf16[304,256]{1,0:T(8,128)(2,1)S(1)}, u32[]{:S(2)}, u32[]{:S(2)}) collective-permute-start(bf16[304,256]{1,0:T(8,128)(2,1)S(1)} %get-tuple-element.41.refs_1_.payload_ref.refs_5_), channel_id=1, source_target_pairs={{0,4},{1,5},{2,6},{3,7},{4,0},{5,1},{6,2},{7,3},{8,12},{9,13},{10,... | collective-permute-start | bytes 466952 | tf_op jit(solution)/shard_map/ppermute | solution.py:491
  4.2 2.5 %collective-permute-start.2 = (bf16[304,256]{1,0:T(8,128)(2,1)S(1)}, bf16[304,256]{1,0:T(8,128)(2,1)S(1)}, u32[]{:S(2)}, u32[]{:S(2)}) collective-permute-start(bf16[304,256]{1,0:T(8,128)(2,1)S(1)} %get-tuple-element.41.refs_1_.payload_ref.refs_5_), channel_id=1, source_target_pairs={{0,12},{1,13},{2,14},{3,15},{4,8},{5,9},{6,10},{7,11},{8,4},{9,5},... | collective-permute-start | bytes 466952 | tf_op jit(solution)/shard_map/ppermute | solution.py:491
  6.7 1.0 %waves.1 = (bf16[48,1024]{1,0:T(8,128)(2,1)S(1)}, bf16[1024,48]{1,0:T(8,128)(2,1)S(1)}, bf16[1024,48]{1,0:T(8,128)(2,1)S(1)}, f32[1024,256]{1,0:T(8,128)S(1)}) custom-call(s32[3,1024]{1,0:T(4,128)S(1)} %get-tuple-element.32.waves_ref, f32[4,256]{1,0:T(4,128)S(1)} %get-tuple-element.33.filter_ref), custom_call_target="tpu_custom_call" | custom-call | tf_op jit(solution)/shard_map/waves/pallas_call | solution.py:187
  7.8 1.6 %collective-permute-start.5 = (bf16[304,256]{1,0:T(8,128)(2,1)S(1)}, bf16[304,256]{1,0:T(8,128)(2,1)S(1)}, u32[]{:S(2)}, u32[]{:S(2)}) collective-permute-start(bf16[304,256]{1,0:T(8,128)(2,1)S(1)} %get-tuple-element.41.refs_1_.payload_ref.refs_5_), channel_id=1, source_target_pairs={{0,2},{1,3},{2,0},{3,1},{4,6},{5,7},{6,4},{7,5},{8,10},{9,11},{10,... | collective-permute-start | bytes 466952 | tf_op jit(solution)/shard_map/ppermute | solution.py:491
  9.3 1.0 %copy-done.1 = bf16[4,256,256]{2,1,0:T(8,128)(2,1)S(1)} copy-done((bf16[4,256,256]{2,1,0:T(8,128)(2,1)S(1)}, bf16[4,256,256]{2,1,0:T(8,128)(2,1)}, u32[]{:S(2)}) %copy-start.1) | copy-done | bytes 524312
  10.4 1.8 %short_range.2._.refs_4_ = f32[288,256]{1,0:T(8,128)S(1)} custom-call(s32[1]{0:T(128)} %bitcast.1.refs_0_.refs_4_, bf16[304,256]{1,0:T(8,128)(2,1)S(1)} %get-tuple-element.41.refs_1_.payload_ref.refs_5_, bf16[304,256]{1,0:T(8,128)(2,1)S(1)} %collective-permute-done.refs_2_, f32[288,16]{1,0:T(8,128)S(1)} %get-tuple-element.31.refs_3_.cols_ref.refs_2_, ...), custom_call_target="tpu_custom_call" | custom-call | flops 1887436800 | bytes 1887436 | tf_op jit(solution)/shard_map/short_range/pallas_call | solution.py:416
  12.4 1.7 %own_layer.1 = (bf16[288,2048]{1,0:T(8,128)(2,1)S(1)}, f32[1024,256]{1,0:T(8,128)S(1)}, f32[1024,256]{1,0:T(8,128)S(1)}) custom-call(f32[288,16]{1,0:T(8,128)S(1)} %get-tuple-element.31.refs_3_.cols_ref.refs_2_, bf16[48,1024]{1,0:T(8,128)(2,1)S(1)} %get-tuple-element.34.waves_ref, bf16[304,256]{1,0:T(8,128)(2,1)S(1)} %get-tuple-element.41.refs_1_.payload_ref.refs_5_, ...), custom_call_target="tpu_custom_call" | custom-call | flops 301989888 | bytes 301989 | tf_op jit(solution)/shard_map/own_layer/pallas_call | solution.py:303
  14.1 0.6 %collective-permute-start.4 = (bf16[304,256]{1,0:T(8,128)(2,1)S(1)}, bf16[304,256]{1,0:T(8,128)(2,1)S(1)}, u32[]{:S(2)}, u32[]{:S(2)}) collective-permute-start(bf16[304,256]{1,0:T(8,128)(2,1)S(1)} %collective-permute-done.3.refs_1_), channel_id=1, source_target_pairs={{0,2},{1,3},{2,0},{3,1},{4,6},{5,7},{6,4},{7,5},{8,10},{9,11},{10,... | collective-permute-start | bytes 466952 | tf_op jit(solution)/shard_map/ppermute | solution.py:491
  14.7 2.3 %structure.5 = (f32[1024,256]{1,0:T(8,128)S(1)}, f32[1024,256]{1,0:T(8,128)S(1)}) custom-call(bf16[304,256]{1,0:T(8,128)(2,1)S(1)} %collective-permute-done.5.refs_0_, bf16[304,256]{1,0:T(8,128)(2,1)S(1)} %collective-permute-done.3.refs_1_, bf16[1024,48]{1,0:T(8,128)(2,1)S(1)} %get-tuple-element.39.refs_2_.refs_1_, ...), custom_call_target="tpu_custom_call" | custom-call | flops 2013265920 | bytes 2013265 | tf_op jit(solution)/shard_map/structure/pallas_call | solution.py:258
  17.1 1.6 %collective-permute-start.7 = (bf16[304,256]{1,0:T(8,128)(2,1)S(1)}, bf16[304,256]{1,0:T(8,128)(2,1)S(1)}, u32[]{:S(2)}, u32[]{:S(2)}) collective-permute-start(bf16[304,256]{1,0:T(8,128)(2,1)S(1)} %collective-permute-done.2.refs_0_), channel_id=1, source_target_pairs={{0,2},{1,3},{2,0},{3,1},{4,6},{5,7},{6,4},{7,5},{8,10},{9,11},{10,... | collective-permute-start | bytes 466952 | tf_op jit(solution)/shard_map/ppermute | solution.py:491
  18.6 1.8 %collective-permute-done.4.refs_1_ = bf16[304,256]{1,0:T(8,128)(2,1)S(1)} collective-permute-done((bf16[304,256]{1,0:T(8,128)(2,1)S(1)}, bf16[304,256]{1,0:T(8,128)(2,1)S(1)}, u32[]{:S(2)}, u32[]{:S(2)}) %collective-permute-start.4) | collective-permute-done | bytes 155680 | tf_op jit(solution)/shard_map/ppermute | solution.py:491
  20.4 2.3 %structure.6 = (f32[1024,256]{1,0:T(8,128)S(1)}, f32[1024,256]{1,0:T(8,128)S(1)}) custom-call(bf16[304,256]{1,0:T(8,128)(2,1)S(1)} %collective-permute-done.2.refs_0_, bf16[304,256]{1,0:T(8,128)(2,1)S(1)} %collective-permute-done.4.refs_1_, bf16[1024,48]{1,0:T(8,128)(2,1)S(1)} %get-tuple-element.39.refs_2_.refs_1_, ...), custom_call_target="tpu_custom_call" | custom-call | flops 2013265920 | bytes 2013265 | tf_op jit(solution)/shard_map/structure/pallas_call | solution.py:258
  23.2 2.3 %structure.7 = (f32[1024,256]{1,0:T(8,128)S(1)}, f32[1024,256]{1,0:T(8,128)S(1)}) custom-call(bf16[304,256]{1,0:T(8,128)(2,1)S(1)} %collective-permute-done.1.refs_0_, bf16[304,256]{1,0:T(8,128)(2,1)S(1)} %collective-permute-done.7.refs_1_, bf16[1024,48]{1,0:T(8,128)(2,1)S(1)} %get-tuple-element.39.refs_2_.refs_1_, ...), custom_call_target="tpu_custom_call" | custom-call | flops 2013265920 | bytes 2013265 | tf_op jit(solution)/shard_map/structure/pallas_call | solution.py:258
  25.6 1.4 %short_range.3.refs_3_.base_ref = f32[288,256]{1,0:T(8,128)S(1)} custom-call(s32[1]{0:T(128)} %bitcast.1.refs_0_.refs_4_, bf16[304,256]{1,0:T(8,128)(2,1)S(1)} %collective-permute-done.8.refs_1_, f32[288,16]{1,0:T(8,128)S(1)} %get-tuple-element.31.refs_3_.cols_ref.refs_2_, bf16[1024,256]{1,0:T(8,128)(2,1)S(1)} %bitcast.4, ...), custom_call_target="tpu_custom_call" | custom-call | flops 1132462080 | bytes 1132462 | tf_op jit(solution)/shard_map/short_range/pallas_call | solution.py:416
  26.9 1.1 %collective-permute-done.6.refs_0_ = bf16[304,256]{1,0:T(8,128)(2,1)S(1)} collective-permute-done((bf16[304,256]{1,0:T(8,128)(2,1)S(1)}, bf16[304,256]{1,0:T(8,128)(2,1)S(1)}, u32[]{:S(2)}, u32[]{:S(2)}) %collective-permute-start.6) | collective-permute-done | bytes 155680 | tf_op jit(solution)/shard_map/ppermute | solution.py:491
  28.0 1.0 %structure.8 = (f32[1024,256]{1,0:T(8,128)S(1)}, bf16[1024,256]{1,0:T(8,128)(2,1)S(1)}) custom-call(bf16[304,256]{1,0:T(8,128)(2,1)S(1)} %collective-permute-done.6.refs_0_, bf16[1024,48]{1,0:T(8,128)(2,1)S(1)} %get-tuple-element.39.refs_2_.refs_1_, bf16[1024,48]{1,0:T(8,128)(2,1)S(1)} %get-tuple-element.40.refs_3_.refs_2_, ...), custom_call_target="tpu_custom_call" | custom-call | flops 603979776 | bytes 603979 | tf_op jit(solution)/shard_map/structure/pallas_call | solution.py:258
  29.1 1.0 %structure.9 = (f32[1024,256]{1,0:T(8,128)S(1)}, bf16[1024,256]{1,0:T(8,128)(2,1)S(1)}) custom-call(bf16[304,256]{1,0:T(8,128)(2,1)S(1)} %collective-permute-done.6.refs_0_, bf16[1024,48]{1,0:T(8,128)(2,1)S(1)} %get-tuple-element.39.refs_2_.refs_1_, bf16[1024,48]{1,0:T(8,128)(2,1)S(1)} %get-tuple-element.40.refs_3_.refs_2_, ...), custom_call_target="tpu_custom_call" | custom-call | flops 603979776 | bytes 603979 | tf_op jit(solution)/shard_map/structure/pallas_call | solution.py:258
  30.1 0.6 %collective-permute-start.9 = (bf16[1024,256]{1,0:T(8,128)(2,1)S(1)}, bf16[1024,256]{1,0:T(8,128)(2,1)S(1)}, u32[]{:S(2)}, u32[]{:S(2)}) collective-permute-start(bf16[1024,256]{1,0:T(8,128)(2,1)S(1)} %get-tuple-element.54), channel_id=1, source_target_pairs={{0,1},{1,0},{2,3},{3,2},{4,5},{5,4},{6,7},{7,6},{8,9},{9,8},{10,11... | collective-permute-start | bytes 1572872 | tf_op jit(solution)/shard_map/ppermute | solution.py:491
  30.7 0.3 collective-permute-done.10.other_ref
  31.0 0.6 %inverse.2.base_ref = f32[288,256]{1,0:T(8,128)S(1)} custom-call(bf16[288,2048]{1,0:T(8,128)(2,1)S(1)} %get-tuple-element.36.table_ref, f32[1024,256]{1,0:T(8,128)S(1)} %get-tuple-element.56.mine_ref, bf16[1024,256]{1,0:T(8,128)(2,1)S(1)} %collective-permute-done.10.other_ref, bf16[256,256]{1,0:T(8,128)(2,1)S(1)} %copy-done, ...), custom_call_target="tpu_custom_call" | custom-call | flops 301989888 | bytes 301989 | tf_op jit(solution)/shard_map/inverse/pallas_call | solution.py:463
  31.7 0.6 %collective-permute-done.9.other_ref = bf16[1024,256]{1,0:T(8,128)(2,1)S(1)} collective-permute-done((bf16[1024,256]{1,0:T(8,128)(2,1)S(1)}, bf16[1024,256]{1,0:T(8,128)(2,1)S(1)}, u32[]{:S(2)}, u32[]{:S(2)}) %collective-permute-start.9) | collective-permute-done | bytes 524320 | tf_op jit(solution)/shard_map/ppermute | solution.py:491
  32.2 1.3 %inverse.3 = bf16[9,32,256]{2,1,0:T(8,128)(2,1)} custom-call(bf16[288,2048]{1,0:T(8,128)(2,1)S(1)} %get-tuple-element.36.table_ref, f32[1024,256]{1,0:T(8,128)S(1)} %get-tuple-element.53.mine_ref, bf16[1024,256]{1,0:T(8,128)(2,1)S(1)} %collective-permute-done.9.other_ref, bf16[256,256]{1,0:T(8,128)(2,1)S(1)} %copy-done, ...), custom_call_target="tpu_custom_call" | custom-call | flops 301989888 | bytes 301989 | tf_op jit(solution)/shard_map/inverse/pallas_call | solution.py:463
  (17 shorter events, 0.7 us)
Async XLA Ops:
  1.1 8.3 %collective-permute-start = (bf16[304,256]{1,0:T(8,128)(2,1)S(1)}, bf16[304,256]{1,0:T(8,128)(2,1)S(1)}, u32[]{:S(2)}, u32[]{:S(2)}) collective-permute-start(bf16[304,256]{1,0:T(8,128)(2,1)S(1)} %get-tuple-element.41.refs_1_.payload_ref.refs_5_), channel_id=1, source_target_pairs={{0,1},{1,0},{2,3},{3,2},{4,5},{5,4},{6,7},{7,6},{8,9},{9,8},{10,11... | collective-permute-start | bytes 466952 | tf_op jit(solution)/shard_map/ppermute | solution.py:491
  1.6 12.5 %collective-permute-start.3 = (bf16[304,256]{1,0:T(8,128)(2,1)S(1)}, bf16[304,256]{1,0:T(8,128)(2,1)S(1)}, u32[]{:S(2)}, u32[]{:S(2)}) collective-permute-start(bf16[304,256]{1,0:T(8,128)(2,1)S(1)} %get-tuple-element.41.refs_1_.payload_ref.refs_5_), channel_id=1, source_target_pairs={{0,4},{1,5},{2,6},{3,7},{4,0},{5,1},{6,2},{7,3},{8,12},{9,13},{10,... | collective-permute-start | bytes 466952 | tf_op jit(solution)/shard_map/ppermute | solution.py:491
  4.2 12.8 %collective-permute-start.2 = (bf16[304,256]{1,0:T(8,128)(2,1)S(1)}, bf16[304,256]{1,0:T(8,128)(2,1)S(1)}, u32[]{:S(2)}, u32[]{:S(2)}) collective-permute-start(bf16[304,256]{1,0:T(8,128)(2,1)S(1)} %get-tuple-element.41.refs_1_.payload_ref.refs_5_), channel_id=1, source_target_pairs={{0,12},{1,13},{2,14},{3,15},{4,8},{5,9},{6,10},{7,11},{8,4},{9,5},... | collective-permute-start | bytes 466952 | tf_op jit(solution)/shard_map/ppermute | solution.py:491
  7.8 7.0 %collective-permute-start.5 = (bf16[304,256]{1,0:T(8,128)(2,1)S(1)}, bf16[304,256]{1,0:T(8,128)(2,1)S(1)}, u32[]{:S(2)}, u32[]{:S(2)}) collective-permute-start(bf16[304,256]{1,0:T(8,128)(2,1)S(1)} %get-tuple-element.41.refs_1_.payload_ref.refs_5_), channel_id=1, source_target_pairs={{0,2},{1,3},{2,0},{3,1},{4,6},{5,7},{6,4},{7,5},{8,10},{9,11},{10,... | collective-permute-start | bytes 466952 | tf_op jit(solution)/shard_map/ppermute | solution.py:491
  9.3 1.0 %copy-start.1 = (bf16[4,256,256]{2,1,0:T(8,128)(2,1)S(1)}, bf16[4,256,256]{2,1,0:T(8,128)(2,1)}, u32[]{:S(2)}) copy-start(bf16[4,256,256]{2,1,0:T(8,128)(2,1)} %param.10) | copy-start | bytes 1572868
  12.2 10.5 %collective-permute-start.1 = (bf16[304,256]{1,0:T(8,128)(2,1)S(1)}, bf16[304,256]{1,0:T(8,128)(2,1)S(1)}, u32[]{:S(2)}, u32[]{:S(2)}) collective-permute-start(bf16[304,256]{1,0:T(8,128)(2,1)S(1)} %get-tuple-element.41.refs_1_.payload_ref.refs_5_), channel_id=1, source_target_pairs={{0,8},{1,9},{2,10},{3,11},{4,12},{5,13},{6,14},{7,15},{8,0},{9,1},... | collective-permute-start | bytes 466952 | tf_op jit(solution)/shard_map/ppermute | solution.py:491
  14.1 6.3 %collective-permute-start.4 = (bf16[304,256]{1,0:T(8,128)(2,1)S(1)}, bf16[304,256]{1,0:T(8,128)(2,1)S(1)}, u32[]{:S(2)}, u32[]{:S(2)}) collective-permute-start(bf16[304,256]{1,0:T(8,128)(2,1)S(1)} %collective-permute-done.3.refs_1_), channel_id=1, source_target_pairs={{0,2},{1,3},{2,0},{3,1},{4,6},{5,7},{6,4},{7,5},{8,10},{9,11},{10,... | collective-permute-start | bytes 466952 | tf_op jit(solution)/shard_map/ppermute | solution.py:491
  17.1 6.0 %collective-permute-start.7 = (bf16[304,256]{1,0:T(8,128)(2,1)S(1)}, bf16[304,256]{1,0:T(8,128)(2,1)S(1)}, u32[]{:S(2)}, u32[]{:S(2)}) collective-permute-start(bf16[304,256]{1,0:T(8,128)(2,1)S(1)} %collective-permute-done.2.refs_0_), channel_id=1, source_target_pairs={{0,2},{1,3},{2,0},{3,1},{4,6},{5,7},{6,4},{7,5},{8,10},{9,11},{10,... | collective-permute-start | bytes 466952 | tf_op jit(solution)/shard_map/ppermute | solution.py:491
  22.7 5.3 %collective-permute-start.6 = (bf16[304,256]{1,0:T(8,128)(2,1)S(1)}, bf16[304,256]{1,0:T(8,128)(2,1)S(1)}, u32[]{:S(2)}, u32[]{:S(2)}) collective-permute-start(bf16[304,256]{1,0:T(8,128)(2,1)S(1)} %collective-permute-done.1.refs_0_), channel_id=1, source_target_pairs={{0,2},{1,3},{2,0},{3,1},{4,6},{5,7},{6,4},{7,5},{8,10},{9,11},{10,... | collective-permute-start | bytes 466952 | tf_op jit(solution)/shard_map/ppermute | solution.py:491
  23.1 2.4 %collective-permute-start.8 = (bf16[304,256]{1,0:T(8,128)(2,1)S(1)}, bf16[304,256]{1,0:T(8,128)(2,1)S(1)}, u32[]{:S(2)}, u32[]{:S(2)}) collective-permute-start(bf16[304,256]{1,0:T(8,128)(2,1)S(1)} %select_select_fusion), channel_id=1, source_target_pairs={{0,1},{1,0},{2,3},{3,2},{4,5},{5,4},{6,7},{7,6},{8,9},{9,8},{10,11... | collective-permute-start | bytes 466952 | tf_op jit(solution)/shard_map/ppermute | solution.py:491
  23.2 2.4 %copy-start.2 = (bf16[4,256,256]{2,1,0:T(8,128)(2,1)S(1)}, bf16[4,256,256]{2,1,0:T(8,128)(2,1)}, u32[]{:S(2)}) copy-start(bf16[4,256,256]{2,1,0:T(8,128)(2,1)} %param.10) | copy-start | bytes 1572868
  29.0 2.0 %copy-start = (bf16[256,256]{1,0:T(8,128)(2,1)S(1)}, bf16[256,256]{1,0:T(8,128)(2,1)}, u32[]{:S(2)}) copy-start(bf16[256,256]{1,0:T(8,128)(2,1)} %charge_ref.3) | copy-start | bytes 393220
  29.1 2.0 %collective-permute-start.10 = (bf16[1024,256]{1,0:T(8,128)(2,1)S(1)}, bf16[1024,256]{1,0:T(8,128)(2,1)S(1)}, u32[]{:S(2)}, u32[]{:S(2)}) collective-permute-start(bf16[1024,256]{1,0:T(8,128)(2,1)S(1)} %get-tuple-element.51.refs_3_), channel_id=1, source_target_pairs={{0,1},{1,0},{2,3},{3,2},{4,5},{5,4},{6,7},{7,6},{8,9},{9,8},{10,11... | collective-permute-start | bytes 1572872 | tf_op jit(solution)/shard_map/ppermute | solution.py:491
  30.1 2.1 %collective-permute-start.9 = (bf16[1024,256]{1,0:T(8,128)(2,1)S(1)}, bf16[1024,256]{1,0:T(8,128)(2,1)S(1)}, u32[]{:S(2)}, u32[]{:S(2)}) collective-permute-start(bf16[1024,256]{1,0:T(8,128)(2,1)S(1)} %get-tuple-element.54), channel_id=1, source_target_pairs={{0,1},{1,0},{2,3},{3,2},{4,5},{5,4},{6,7},{7,6},{8,9},{9,8},{10,11... | collective-permute-start | bytes 1572872 | tf_op jit(solution)/shard_map/ppermute | solution.py:491
